TPU v7x, 256 devices: a whole 4x4x8 slice. The times are simulated.
256 devices in a mesh: group: 8 (over y, core), dev: 32 (over x, z).
Axes of the slice: x: 4, y: 4, z: 8, core: 2. Of those that a mesh axis runs over, the one named last changes fastest.
Arguments:
- fine_state: float32 [256, 19, 4096], P(('group', 'dev')), may hold values from 0.01 to 0.6, as said below
- coarse_state: float32 [256, 19, 4096], P(('group', 'dev')), may hold values from 0.01 to 0.6, as said below
- fine_depth: int32 [256, 4096], P(('group', 'dev')), may hold values from -30 to 119, as said below
- coarse_depth: int32 [256, 4096], P(('group', 'dev')), may hold values from -30 to 119, as said below
- fine_links: int32 [8, 32, 6], P('group'), may hold values from -1 to 31, as said below
- coarse_links: int32 [8, 32, 6], P('group'), may hold values from -2 to 31, as said below
- parents: int32 [8, 32, 2], P('group'), may hold values from 0 to 31, as said below
Outputs:
- fine_out: float32 [256, 19, 4096], P(('group', 'dev'))
- coarse_out: float32 [256, 19, 4096], P(('group', 'dev'))
Inputs may be any that keep to these rules, and one draw needn't show every extreme that they name: `fine_state`: each population is its weight w_q times a factor between 0.4 and 1.6. `coarse_state`: each population is its weight w_q times a factor between 0.4 and 1.6. `fine_depth`: in units of 1 / 7 cell: the distance from the cell to the surface of a union of two balls placed in the block, negative inside, rounded down and clipped. `coarse_depth`: in units of 1 / 7 cell: the distance from the cell to the surface of a union of two balls placed in the block, negative inside, rounded down and clipped. `fine_links`: entry (group, device, face) is the device of the same group holding the fine block across that face, or -1 where the fine region ends; neighbours are mutual (a block is its neighbour's neighbour across the opposite face) and the six neighbours of a block are distinct or -1. `coarse_links`: entry (group, device, face) is the device of the same group holding the coarse block across that face, -2 on faces 2 and 3 where the block across lies on the same device of the neighbouring group, or -1 where the domain ends; neighbours are mutual and the six of a block are distinct or negative. Each region's coarse blocks sit on devices in the same arrangement in every group. `parents`: column 0 is a device of the same group, column 1 an octant 0..7; no two fine blocks of a group share a parent device and octant.
All inputs are finite; a program needn't handle non-finite values.
Results may differ from a plain program's by a relative error of at most 0.0003.
Values sent between devices are 32-bit elements; how exact they have to be, the bound alone decides.
No kernel may reach another device: no remote copies, remote signals or barrier semaphores. Data moves between devices by JAX's collectives and lax.ppermute only.
A program may use at most 128 MiB of HBM per device.

v0:
```python
import jax
import jax.numpy as jnp
from jax import lax
from jax.sharding import PartitionSpec as P

VELOCITIES = [
    (0, 0, 0),
    (1, 0, 0),
    (-1, 0, 0),
    (0, 1, 0),
    (0, -1, 0),
    (0, 0, 1),
    (0, 0, -1),
    (1, 1, 0),
    (-1, -1, 0),
    (1, -1, 0),
    (-1, 1, 0),
    (1, 0, 1),
    (-1, 0, -1),
    (1, 0, -1),
    (-1, 0, 1),
    (0, 1, 1),
    (0, -1, -1),
    (0, 1, -1),
    (0, -1, 1),
]
WEIGHTS = [1.0 / 3.0] + [1.0 / 18.0] * 6 + [1.0 / 36.0] * 12
OPPOSITE = [VELOCITIES.index((-v[0], -v[1], -v[2])) for v in VELOCITIES]
OUTGOING = [
    [q for q in range(19) if VELOCITIES[q][face // 2] == 2 * (face % 2) - 1] for face in range(6)
]
OMEGA_FINE = 1.25
OMEGA_COARSE = 1.0 / 0.65
INFLOW = 0.05


def with_halo(block, sides, width):
    for axis, dim in sides:
        count = lax.axis_size(axis)
        forward = [(i, i + 1) for i in range(count - 1)]
        backward = [(target, source) for source, target in forward]
        low = lax.ppermute(
            lax.slice_in_dim(block, block.shape[dim] - width, None, axis=dim), axis, forward
        )
        high = lax.ppermute(lax.slice_in_dim(block, 0, width, axis=dim), axis, backward)
        block = jnp.concatenate([low, block, high], axis=dim)
    return block


def project(field, axis):
    total = jnp.zeros_like(field[0])
    for index in range(19):
        if VELOCITIES[index][axis] != 0:
            total = total + VELOCITIES[index][axis] * field[index]
    return total


def moments(field):
    density = jnp.sum(field, axis=0)
    return (
        density,
        (project(field, 0) / density, project(field, 1) / density, project(field, 2) / density),
    )


def stacked_moments(field):
    density, velocity = moments(field)
    return jnp.stack([density, velocity[0], velocity[1], velocity[2]])


def equilibrium(density, velocity, chosen):
    square = velocity[0] * velocity[0] + velocity[1] * velocity[1] + velocity[2] * velocity[2]
    rows = []
    for index in chosen:
        along = 0.0
        for axis in range(3):
            if VELOCITIES[index][axis] != 0:
                along = along + VELOCITIES[index][axis] * velocity[axis]
        rows.append(
            WEIGHTS[index] * density * (1.0 + 3.0 * along + 4.5 * along * along - 1.5 * square)
        )
    return jnp.stack(rows)


def collide(field, omega):
    density, velocity = moments(field)
    return field + omega * (equilibrium(density, velocity, range(19)) - field)


def pack(post):
    width = post.shape[1]
    planes = []
    for face in range(6):
        chosen = jnp.stack([post[index] for index in OUTGOING[face]])
        layer = 0 if face % 2 == 0 else width - 1
        planes.append(
            lax.index_in_dim(chosen, layer, face // 2 + 1, keepdims=False).reshape(5, width * width)
        )
    return jnp.stack(planes)


def stream(post, start, depth, ghosts):
    width = post.shape[1]
    solid = depth <= 0
    depth_pad = jnp.pad(depth, 1, constant_values=1)
    coords = jnp.arange(width)
    rows = []
    for index in range(19):
        shift = VELOCITIES[index]
        padded = jnp.pad(post[index], 1)
        for face in range(6):
            axis = face // 2
            sign = 2 * (face % 2) - 1
            if shift[axis] == -sign:
                slot = OUTGOING[face ^ 1].index(index)
                plane = ghosts[face, slot].reshape(width, width)
                position = 0 if sign < 0 else width + 1
                if axis == 0:
                    padded = padded.at[position, 1 : width + 1, 1 : width + 1].set(plane)
                elif axis == 1:
                    padded = padded.at[1 : width + 1, position, 1 : width + 1].set(plane)
                else:
                    padded = padded.at[1 : width + 1, 1 : width + 1, position].set(plane)
        lows = [1 - shift[0], 1 - shift[1], 1 - shift[2]]
        source = padded[
            lows[0] : lows[0] + width, lows[1] : lows[1] + width, lows[2] : lows[2] + width
        ]
        source_depth = depth_pad[
            lows[0] : lows[0] + width, lows[1] : lows[1] + width, lows[2] : lows[2] + width
        ]
        outside = []
        for axis in range(3):
            line = ((coords - shift[axis] < 0) | (coords - shift[axis] >= width)).astype(jnp.int32)
            shape = [1, 1, 1]
            shape[axis] = width
            outside.append(line.reshape(shape))
        corner = outside[0] + outside[1] + outside[2] >= 2
        wall = jnp.logical_not(solid) & (source_depth <= 0)
        gap = jnp.where(wall, depth - source_depth, 1).astype(jnp.float32)
        fraction = jnp.where(wall, depth.astype(jnp.float32) / gap, 1.0)
        weight = jnp.where(fraction >= 0.5, 0.5 / fraction, 2.0 * fraction)
        reflected = weight * post[OPPOSITE[index]] + (1.0 - weight) * post[index]
        value = jnp.where(corner, post[OPPOSITE[index]], source)
        value = jnp.where(wall, reflected, value)
        rows.append(jnp.where(solid, start[index], value))
    return jnp.stack(rows)


def layer_planes(layers):
    edge = layers.shape[2]
    half = 1
    while half * half < edge:
        half = half + 1
    planes = []
    for face in range(6):
        layer = layers[:, face].reshape(4, half, half)
        layer = jnp.repeat(jnp.repeat(layer, 2, axis=1), 2, axis=2)
        planes.append(
            equilibrium(layer[0], (layer[1], layer[2], layer[3]), OUTGOING[face ^ 1]).reshape(
                5, 4 * half * half
            )
        )
    return jnp.stack(planes)


def interface_planes(moment):
    half = moment.shape[1]
    layers = []
    for face in range(6):
        layer = lax.index_in_dim(
            moment, 0 if face % 2 == 0 else half - 1, face // 2 + 1, keepdims=False
        )
        layers.append(layer.reshape(4, half * half))
    return layer_planes(jnp.stack(layers, axis=1))


def boundary_planes(width):
    ones = jnp.ones((width, width), jnp.float32)
    flow = (INFLOW * ones, 0.0 * ones, 0.0 * ones)
    return jnp.stack(
        [equilibrium(ones, flow, OUTGOING[face ^ 1]).reshape(5, width * width) for face in range(6)]
    )


def octants(field):
    channels, width = (field.shape[0], field.shape[1])
    half = width // 2
    split = field.reshape(channels, 2, half, 2, half, 2, half).transpose(1, 3, 5, 0, 2, 4, 6)
    return split.reshape(8, channels, half * half * half)


def restrict(field):
    width = field.shape[1]
    half = width // 2
    whole = jnp.stack(
        [jnp.sum(field, axis=0), project(field, 0), project(field, 1), project(field, 2)]
    )
    return jnp.mean(whole.reshape(4, half, 2, half, 2, half, 2), axis=(2, 4, 6)).reshape(
        4, half * half * half
    )


def apply_restriction(coarse_new, gathered, present):
    width = coarse_new.shape[1]
    half = width // 2
    whole = (
        gathered.reshape(2, 2, 2, 4, half, half, half)
        .transpose(3, 0, 4, 1, 5, 2, 6)
        .reshape(4, width, width, width)
    )
    cover = (
        jnp.broadcast_to(present.reshape(2, 1, 2, 1, 2, 1), (2, half, 2, half, 2, half)).reshape(
            width, width, width
        )
        > 0.5
    )
    dense = jnp.where(cover, whole[0], 1.0)
    fine_eq = equilibrium(dense, (whole[1] / dense, whole[2] / dense, whole[3] / dense), range(19))
    density, velocity = moments(coarse_new)
    coarse_eq = equilibrium(density, velocity, range(19))
    return coarse_new + jnp.where(cover, fine_eq - coarse_eq, 0.0)


def coarse_neighbours(packets, codes):
    everyone = lax.all_gather(packets[None], "dev", axis=0, tiled=True)
    return [everyone[jnp.maximum(codes[face], 0), face ^ 1] for face in range(6)]


def fine_neighbours(packets, codes):
    everyone = lax.all_gather(packets[None], "dev", axis=0, tiled=True)
    return [everyone[jnp.maximum(codes[face], 0), face ^ 1] for face in range(6)]


def body(fine_state, coarse_state, fine_depth, coarse_depth, fine_links, coarse_links, parents):
    own_index = lax.axis_index("dev")
    count = lax.axis_size("dev")
    side = fine_state.shape[2]
    width = 1
    while width * width * width < side:
        width = width + 1
    half = width // 2
    coarse_in = coarse_state[0].reshape(19, width, width, width)
    coarse_codes = coarse_links[0][own_index]
    coarse_post = collide(coarse_in, OMEGA_COARSE)
    coarse_packets = pack(coarse_post)
    neighbours = coarse_neighbours(coarse_packets, coarse_codes)
    region_rims = with_halo(jnp.stack([coarse_packets[2], coarse_packets[3]]), (("group", 0),), 1)
    border = boundary_planes(width)
    ghosts = []
    for face in range(6):
        plane = border[face]
        if face == 2:
            plane = jnp.where(coarse_codes[face] == -2, region_rims[0], plane)
        if face == 3:
            plane = jnp.where(coarse_codes[face] == -2, region_rims[3], plane)
        ghosts.append(jnp.where(coarse_codes[face] >= 0, neighbours[face], plane))
    coarse_new = stream(
        coarse_post, coarse_in, coarse_depth[0].reshape(width, width, width), jnp.stack(ghosts)
    )
    old = stacked_moments(coarse_in)
    new = stacked_moments(coarse_new)
    mid = (old + new) * 0.5
    both = octants(jnp.concatenate([old, mid], axis=0))
    parent_rows = parents[0]
    select = (
        (parent_rows[:, 0] == own_index)[:, None]
        & (parent_rows[:, 1][:, None] == jnp.arange(8)[None, :])
    ).astype(jnp.float32)
    my_parent = parent_rows[own_index, 0]
    outgoing = jnp.einsum("po,ock->pck", select, both, precision=lax.Precision.HIGHEST)
    incoming = lax.all_to_all(outgoing, "dev", split_axis=0, concat_axis=0, tiled=True)
    mine = incoming[my_parent]
    below_turns = [
        interface_planes(mine[4 * turn : 4 * turn + 4].reshape(4, half, half, half))
        for turn in range(2)
    ]
    fine_codes = fine_links[0][own_index]
    depth = fine_depth[0].reshape(width, width, width)
    state = fine_state[0].reshape(19, width, width, width)
    for turn in range(2):
        post = collide(state, OMEGA_FINE)
        planes = fine_neighbours(pack(post), fine_codes)
        below = below_turns[turn]
        ghosts = jnp.stack(
            [jnp.where(fine_codes[face] >= 0, planes[face], below[face]) for face in range(6)]
        )
        state = stream(post, state, depth, ghosts)
    averaged = restrict(state)
    sending = (jnp.arange(count) == my_parent).astype(jnp.float32)[:, None, None] * averaged[None]
    received = lax.all_to_all(sending, "dev", split_axis=0, concat_axis=0, tiled=True)
    gathered = jnp.einsum("co,ckx->okx", select, received, precision=lax.Precision.HIGHEST)
    present = jnp.sum(select, axis=0)
    coarse_out = apply_restriction(coarse_new, gathered, present)
    return (state.reshape(1, 19, side), coarse_out.reshape(1, 19, side))


def solution(mesh):
    placed = (
        P(("group", "dev"), None, None),
        P(("group", "dev"), None, None),
        P(("group", "dev"), None),
        P(("group", "dev"), None),
        P("group", None, None),
        P("group", None, None),
        P("group", None, None),
    )
    return jax.shard_map(
        body,
        mesh=mesh,
        in_specs=placed,
        out_specs=(P(("group", "dev"), None, None), P(("group", "dev"), None, None)),
        check_vma=False,
    )
```

profile of v0, /device:TPU:16, one launch (start us, length us, event | category | flops | bytes accessed | tf_op | source)
XLA Modules:
  0.0 1143.8 jit_solution(7234506618147000642)
XLA Ops:
  8.9 3.5 fusion.511
  153.0 54.6 %all-gather.1 = f32[192,5,256]{2,1,0:T(8,128)S(1)} all-gather(f32[6,5,256]{2,1,0:T(8,128)S(1)} %copy.199), channel_id=3, replica_groups=mesh['group'=8,'dev'=32] {'dev'}, dimensions={0}, use_global_device_ids=true | all-gather | bytes 1013760 | tf_op jit(solution)/shard_map/all_gather | solution.py:225
  225.2 49.7 %all-gather = f32[192,5,256]{2,1,0:T(8,128)S(1)} all-gather(f32[6,5,256]{2,1,0:T(8,128)S(1)} %copy.197), channel_id=2, replica_groups=mesh['group'=8,'dev'=32] {'dev'}, dimensions={0}, use_global_device_ids=true | all-gather | bytes 1013760 | tf_op jit(solution)/shard_map/all_gather | solution.py:230
  357.6 4.0 scatter.309
  365.1 4.0 scatter.331
  369.1 4.0 scatter.329
  392.7 3.3 scatter.305
  402.4 3.3 scatter.321
  415.3 3.3 scatter.319
  418.6 3.3 scatter.315
  424.3 4.1 scatter.345
  428.4 3.4 scatter.341
  432.5 7.9 fusion.205
  487.0 6.3 all-to-all-start
  631.2 3.7 scatter.396
  680.5 4.0 scatter.395
  686.3 4.0 scatter.391
  690.4 4.0 scatter.381
  694.4 4.0 scatter.379
  698.4 3.4 scatter.359
  708.3 5.0 constant_dynamic-update-slice_fusion.139
  859.2 51.5 %all-gather.2 = f32[192,5,256]{2,1,0:T(8,128)S(1)} all-gather(f32[6,5,256]{2,1,0:T(8,128)S(1)} %copy.223), channel_id=4, replica_groups=mesh['group'=8,'dev'=32] {'dev'}, dimensions={0}, use_global_device_ids=true | all-gather | bytes 1013760 | tf_op jit(solution)/shard_map/all_gather | solution.py:230
  990.0 4.0 scatter.431
  994.0 4.0 scatter.429
  1001.5 5.1 multiply_add_fusion.4
  1039.2 4.0 scatter.445
  1045.0 4.0 scatter.441
  1050.8 4.0 multiply_add_fusion.3
  1062.7 4.0 scatter.409
  1104.1 8.3 add_add_fusion
  1119.0 7.9 all-to-all-start.1
  1127.3 10.4 all-to-all-done.1
  (1420 shorter events, 830.2 us)
Async XLA Ops:
  21.3 351.9 %collective-permute-start.1 = (f32[1,5,256]{2,0,1:T(1,128)}, f32[1,5,256]{2,0,1:T(1,128)}, u32[]{:S(2)}, u32[]{:S(2)}) collective-permute-start(f32[1,5,256]{2,0,1:T(1,128)} %stack_reshape_squeeze.62), channel_id=1, source_target_pairs={{32,0},{64,32},{96,64},{128,96},{160,128},{192,160},{224,192},{33,... | collective-permute-start | bytes 15368 | tf_op jit(solution)/shard_map/ppermute | solution.py:45
  24.5 40.4 %copy-start.6 = (f32[1,19,4096]{2,0,1:T(1,128)S(1)}, f32[1,19,4096]{2,0,1:T(1,128)}, u32[]{:S(2)}) copy-start(f32[1,19,4096]{2,0,1:T(1,128)} %param.187) | copy-start | bytes 933892
  25.9 45.3 %copy-start.4 = (f32[1,19,4096]{2,0,1:T(1,128)S(1)}, f32[1,19,4096]{2,0,1:T(1,128)}, u32[]{:S(2)}) copy-start(f32[1,19,4096]{2,0,1:T(1,128)} %param.188) | copy-start | bytes 933892
  30.0 344.5 %collective-permute-start = (f32[1,5,256]{2,0,1:T(1,128)}, f32[1,5,256]{2,0,1:T(1,128)}, u32[]{:S(2)}, u32[]{:S(2)}) collective-permute-start(f32[1,5,256]{2,0,1:T(1,128)} %stack_reshape_squeeze.63), channel_id=1, source_target_pairs={{0,32},{32,64},{64,96},{96,128},{128,160},{160,192},{192,224},{1,3... | collective-permute-start | bytes 15368 | tf_op jit(solution)/shard_map/ppermute | solution.py:42
  85.3 623.0 %copy-start.5 = (s32[16,16,16]{2,1,0:T(8,128)}, s32[16,16,16]{2,1,0:T(8,128)S(1)}, u32[]{:S(2)}) copy-start(s32[16,16,16]{2,1,0:T(8,128)S(1)} %reshape_squeeze.9) | copy-start | bytes 49156
  88.4 123.7 %copy-start.39 = (f32[1,16,16,16]{3,2,1,0:T(8,128)}, f32[1,16,16,16]{3,2,1,0:T(8,128)S(1)}, u32[]{:S(2)}) copy-start(f32[1,16,16,16]{3,2,1,0:T(8,128)S(1)} %convert_element_type.784) | copy-start | bytes 49156
  100.4 111.7 %copy-start.41 = (f32[1,16,16,16]{3,2,1,0:T(8,128)}, f32[1,16,16,16]{3,2,1,0:T(8,128)S(1)}, u32[]{:S(2)}) copy-start(f32[1,16,16,16]{3,2,1,0:T(8,128)S(1)} %squeeze.280) | copy-start | bytes 49156
  153.0 60.9 %copy-start.53 = (f32[2,16,16,16]{3,2,1,0:T(8,128)S(1)}, f32[2,16,16,16]{3,2,1,0:T(8,128)}, u32[]{:S(2)}) copy-start(f32[2,16,16,16]{3,2,1,0:T(8,128)} %get-tuple-element.1428) | copy-start | bytes 98308
  219.8 57.1 %copy-start.168 = (s32[16]{0:T(128)S(1)}, s32[16]{0:T(128)}, u32[]{:S(2)}) copy-start(s32[16]{0:T(128)} %get-tuple-element.1612) | copy-start | bytes 196
  219.8 57.1 %copy-start.169 = (s32[16]{0:T(128)S(1)}, s32[16]{0:T(128)}, u32[]{:S(2)}) copy-start(s32[16]{0:T(128)} %get-tuple-element.1613) | copy-start | bytes 196
  219.8 57.1 %copy-start.170 = (s32[16]{0:T(128)S(1)}, s32[16]{0:T(128)}, u32[]{:S(2)}) copy-start(s32[16]{0:T(128)} %compare_convert_fusion.1) | copy-start | bytes 196
  219.8 57.8 %copy-start.50 = (f32[1,2,8,2,8,2,8]{6,5,4,3,2,1,0:T(2,128)S(1)}, f32[1,2,8,2,8,2,8]{6,5,4,3,2,1,0:T(2,128)}, u32[]{:S(2)}) copy-start(f32[1,2,8,2,8,2,8]{6,5,4,3,2,1,0:T(2,128)} %reshape.21290) | copy-start | bytes 49156
  225.1 53.7 %copy-start.51 = (f32[1,2,8,2,8,2,8]{6,5,4,3,2,1,0:T(2,128)S(1)}, f32[1,2,8,2,8,2,8]{6,5,4,3,2,1,0:T(2,128)}, u32[]{:S(2)}) copy-start(f32[1,2,8,2,8,2,8]{6,5,4,3,2,1,0:T(2,128)} %reshape.21284) | copy-start | bytes 49156
  225.1 53.7 %copy-start.52 = (f32[1,2,8,2,8,2,8]{6,5,4,3,2,1,0:T(2,128)S(1)}, f32[1,2,8,2,8,2,8]{6,5,4,3,2,1,0:T(2,128)}, u32[]{:S(2)}) copy-start(f32[1,2,8,2,8,2,8]{6,5,4,3,2,1,0:T(2,128)} %reshape.21292) | copy-start | bytes 49156
  225.2 55.6 %copy-start.74 = (f32[16,16,16]{2,1,0:T(8,128)S(1)}, f32[16,16,16]{2,1,0:T(8,128)}, u32[]{:S(2)}) copy-start(f32[16,16,16]{2,1,0:T(8,128)} %get-tuple-element.1446) | copy-start | bytes 49156
  322.8 76.4 %copy-start.62 = (f32[18,18,18]{2,1,0:T(8,128)S(1)}, f32[18,18,18]{2,1,0:T(8,128)}, u32[]{:S(2)}) copy-start(f32[18,18,18]{2,1,0:T(8,128)} %pad.551) | copy-start | bytes 69988
  322.8 86.2 %copy-start.60 = (f32[18,18,18]{2,1,0:T(8,128)S(1)}, f32[18,18,18]{2,1,0:T(8,128)}, u32[]{:S(2)}) copy-start(f32[18,18,18]{2,1,0:T(8,128)} %pad.554) | copy-start | bytes 69988
  322.8 89.4 %copy-start.58 = (f32[18,18,18]{2,1,0:T(8,128)S(1)}, f32[18,18,18]{2,1,0:T(8,128)}, u32[]{:S(2)}) copy-start(f32[18,18,18]{2,1,0:T(8,128)} %pad.552) | copy-start | bytes 69988
  487.0 54.9 %all-to-all-start = ((f32[32,8,512]{2,1,0:T(8,128)}), f32[32,8,512]{2,1,0:T(8,128)}, u32[]{:S(2)}, u32[]{:S(2)}) async-start(f32[32,8,512]{2,1,0:T(8,128)} %copy.212), calls=%async_computation | async-start | bytes 1048576 | tf_op jit(solution)/shard_map/all_to_all | solution.py:271
  495.2 46.6 %copy-start.66 = (f32[16,16,16]{2,1,0:T(8,128)S(1)}, f32[16,16,16]{2,1,0:T(8,128)}, u32[]{:S(2)}) copy-start(f32[16,16,16]{2,1,0:T(8,128)} %get-tuple-element.1245) | copy-start | bytes 49156
  551.1 101.4 %copy-start.57 = (f32[18,18,18]{2,1,0:T(8,128)S(1)}, f32[18,18,18]{2,1,0:T(8,128)}, u32[]{:S(2)}) copy-start(f32[18,18,18]{2,1,0:T(8,128)} %pad.556) | copy-start | bytes 69988
  551.3 127.3 %copy-start.56 = (f32[18,18,18]{2,1,0:T(8,128)S(1)}, f32[18,18,18]{2,1,0:T(8,128)}, u32[]{:S(2)}) copy-start(f32[18,18,18]{2,1,0:T(8,128)} %pad.535) | copy-start | bytes 69988
  555.7 142.7 %copy-start.55 = (f32[18,18,18]{2,1,0:T(8,128)S(1)}, f32[18,18,18]{2,1,0:T(8,128)}, u32[]{:S(2)}) copy-start(f32[18,18,18]{2,1,0:T(8,128)} %pad.559) | copy-start | bytes 69988
  561.2 146.0 %copy-start.54 = (f32[18,18,18]{2,1,0:T(8,128)S(1)}, f32[18,18,18]{2,1,0:T(8,128)}, u32[]{:S(2)}) copy-start(f32[18,18,18]{2,1,0:T(8,128)} %pad.558) | copy-start | bytes 69988
  565.6 142.7 %copy-start.99 = (s32[16,16]{1,0:T(8,128)S(1)}, s32[16,16]{1,0:T(8,128)}, u32[]{:S(2)}) copy-start(s32[16,16]{1,0:T(8,128)} %get-tuple-element.1601) | copy-start | bytes 3076
  565.6 142.7 %copy-start.101 = (s32[16,16]{1,0:T(8,128)S(1)}, s32[16,16]{1,0:T(8,128)}, u32[]{:S(2)}) copy-start(s32[16,16]{1,0:T(8,128)} %get-tuple-element.1603) | copy-start | bytes 3076
  565.6 142.7 %copy-start.102 = (s32[16,16]{1,0:T(8,128)S(1)}, s32[16,16]{1,0:T(8,128)}, u32[]{:S(2)}) copy-start(s32[16,16]{1,0:T(8,128)} %get-tuple-element.1593) | copy-start | bytes 3076
  565.6 142.7 %copy-start.103 = (s32[16,16]{1,0:T(8,128)S(1)}, s32[16,16]{1,0:T(8,128)}, u32[]{:S(2)}) copy-start(s32[16,16]{1,0:T(8,128)} %get-tuple-element.1594) | copy-start | bytes 3076
  565.6 142.7 %copy-start.104 = (s32[16,16]{1,0:T(8,128)S(1)}, s32[16,16]{1,0:T(8,128)}, u32[]{:S(2)}) copy-start(s32[16,16]{1,0:T(8,128)} %get-tuple-element.1599) | copy-start | bytes 3076
  734.3 87.9 %copy-start.2 = (f32[19,16,16,16]{3,2,1,0:T(8,128)S(1)}, f32[19,16,16,16]{3,2,1,0:T(8,128)}, u32[]{:S(2)}) copy-start(f32[19,16,16,16]{3,2,1,0:T(8,128)} %copy-done.1) | copy-start | bytes 933892
  1001.5 49.2 %copy-start.100 = (s32[16,16]{1,0:T(8,128)S(1)}, s32[16,16]{1,0:T(8,128)}, u32[]{:S(2)}) copy-start(s32[16,16]{1,0:T(8,128)} %get-tuple-element.1601) | copy-start | bytes 3076
  1119.0 18.7 %all-to-all-start.1 = ((f32[32,4,512]{2,1,0:T(4,128)}), f32[32,4,512]{2,1,0:T(4,128)S(1)}, u32[]{:S(2)}, u32[]{:S(2)}) async-start(f32[32,4,512]{2,1,0:T(4,128)} %broadcast_multiply_fusion), calls=%async_computation.1 | async-start | bytes 524288 | tf_op jit(solution)/shard_map/all_to_all | solution.py:290
  (186 other events, 2121.0 us)
where the time goes:
time: 1170 us; the launch traced here: 1140 us
  local copies, waits for them, and re-layouts  802 us (69%)
  blocking collectives  156 us (13%)
  other arithmetic  132 us (11%)
  between operations  23.5 us (2%)
  starting transfers between devices  18.7 us (2%)
    another operation x90, local copies, waits for them, and re-layouts  123 us
    all_gather x2, blocking collectives, fine_neighbours(): everyone = lax.all_gather(packets[None], 'dev', axis=0, tiled=True)  101 us
    scatter x30, local copies, waits for them, and re-layouts, stream(): padded = padded.at[1:width + 1, position, 1:width + 1].set(plane)  98 us
    scatter x30, local copies, waits for them, and re-layouts, stream(): padded = padded.at[1:width + 1, 1:width + 1, position].set(plane)  84.2 us
    scatter x30, local copies, waits for them, and re-layouts, stream(): padded = padded.at[position, 1:width + 1, 1:width + 1].set(plane)  65.7 us
    pad x54, local copies, waits for them, and re-layouts, stream(): padded = jnp.pad(post[index], 1)  60.2 us
    broadcast_in_dim x186, local copies, waits for them, and re-layouts, layer_planes(): layer = jnp.repeat(jnp.repeat(layer, 2, axis=1), 2, axis=2)  55.1 us
    all_gather x1, blocking collectives, coarse_neighbours(): everyone = lax.all_gather(packets[None], 'dev', axis=0, tiled=True)  54.6 us
  transfers between devices with their start and end apart: 4, of which 1 were waited for; matrix products, arithmetic and copies ran while one was open for 24% of the time, Pallas kernels for 0%

commit v1 on v0

v1 whole, which is shorter than its diff:
```python
import jax
import jax.numpy as jnp
from jax import lax
from jax.experimental import pallas as pl
from jax.experimental.pallas import tpu as pltpu
from jax.sharding import PartitionSpec as P

VELOCITIES = [
    (0, 0, 0),
    (1, 0, 0),
    (-1, 0, 0),
    (0, 1, 0),
    (0, -1, 0),
    (0, 0, 1),
    (0, 0, -1),
    (1, 1, 0),
    (-1, -1, 0),
    (1, -1, 0),
    (-1, 1, 0),
    (1, 0, 1),
    (-1, 0, -1),
    (1, 0, -1),
    (-1, 0, 1),
    (0, 1, 1),
    (0, -1, -1),
    (0, 1, -1),
    (0, -1, 1),
]
WEIGHTS = [1.0 / 3.0] + [1.0 / 18.0] * 6 + [1.0 / 36.0] * 12
OPPOSITE = [VELOCITIES.index((-v[0], -v[1], -v[2])) for v in VELOCITIES]
OUTGOING = [
    [q for q in range(19) if VELOCITIES[q][face // 2] == 2 * (face % 2) - 1] for face in range(6)
]
OMEGA_FINE = 1.25
OMEGA_COARSE = 1.0 / 0.65
INFLOW = 0.05
F32 = jnp.float32
FIELD = (19, 16, 256)
SLOT1 = 40
SLOT2 = 32
SLOT3 = 16


def inflow_value(q):
    along = VELOCITIES[q][0] * INFLOW
    return WEIGHTS[q] * (1.0 + 3.0 * along + 4.5 * along * along - 1.5 * INFLOW * INFLOW)


def iota(shape, dim):
    return lax.broadcasted_iota(jnp.int32, shape, dim)


def tile(value, row, half):
    return value[8 * row : 8 * row + 8, 128 * half : 128 * half + 128]


def join(tiles):
    return jnp.concatenate([jnp.concatenate(line, axis=1) for line in tiles], axis=0)


def pick(value, index, axis):
    return jnp.take_along_axis(value, index, axis=axis, mode="promise_in_bounds")


def sums(f):
    density = f[0]
    for q in range(1, 19):
        density = density + f[q]
    momentum = []
    for axis in range(3):
        plus = [f[q] for q in range(19) if VELOCITIES[q][axis] == 1]
        minus = [f[q] for q in range(19) if VELOCITIES[q][axis] == -1]
        total = plus[0] - minus[0]
        for a, b in zip(plus[1:], minus[1:]):
            total = total + (a - b)
        momentum.append(total)
    return density, momentum


def moments(f):
    density, momentum = sums(f)
    inverse = 1.0 / density
    return density, [m * inverse for m in momentum]


def equilibrium(density, u, chosen):
    base = 1.0 - 1.5 * (u[0] * u[0] + u[1] * u[1] + u[2] * u[2])
    scaled = {}
    for q in chosen:
        if WEIGHTS[q] not in scaled:
            scaled[WEIGHTS[q]] = WEIGHTS[q] * density
    even, out = {}, {}
    for q in chosen:
        v = VELOCITIES[q]
        weight = scaled[WEIGHTS[q]]
        if q == 0:
            out[q] = weight * base
            continue
        lead = q if q % 2 == 1 else q - 1
        if lead not in even:
            along = None
            for axis in range(3):
                c = VELOCITIES[lead][axis]
                if c != 0:
                    if along is None:
                        along = u[axis]
                    else:
                        along = along + u[axis] if c > 0 else along - u[axis]
            even[lead] = (base + 4.5 * along * along, 3.0 * along)
        part, odd = even[lead]
        out[q] = weight * (part + odd) if q == lead else weight * (part - odd)
    return out


def collide(f, omega):
    density, u = moments(f)
    rest = equilibrium(density, u, range(19))
    return [(1.0 - omega) * f[q] + omega * rest[q] for q in range(19)]


def pack_face(post, face, offset):
    axis, side = face // 2, face % 2
    lane = iota((8, 128), 1)
    sub = iota((8, 128), 0)
    chosen = [post[q] for q in OUTGOING[face]]
    if axis == 0:
        at = 15 * side
        rows = [f[at : at + 1, :] for f in chosen]
        first = None
        for i in range(4):
            for half in range(2):
                line = jnp.broadcast_to(rows[i][:, 128 * half : 128 * half + 128], (8, 128))
                first = line if first is None else jnp.where(sub == 2 * i + half, line, first)
        second = None
        for half in range(2):
            line = jnp.broadcast_to(rows[4][:, 128 * half : 128 * half + 128], (8, 128))
            turned = pltpu.roll(line, 64, 1)
            low, high = (line, turned) if offset == 0 else (turned, line)
            for k, value in ((2 * half, low), (2 * half + 1, high)):
                second = value if second is None else jnp.where(sub == k, value, second)
        return first, second
    strips = []
    for f in chosen:
        for row in range(2):
            if axis == 1:
                strips.append(pick(tile(f, row, side), lane % 16 + 112 * side, 1))
            else:
                index = (lane % 8) * 16 + 15 * side
                a = pick(tile(f, row, 0), index, 1)
                b = pick(tile(f, row, 1), index, 1)
                strips.append(jnp.where(lane % 16 < 8, a, b))
    first = strips[0]
    for t in range(1, 8):
        first = jnp.where(lane // 16 == t, strips[t], first)
    second = jnp.where((lane // 16) % 2 == 0, strips[8], strips[9])
    return first, second


def unpack_face(first, second, offset, face):
    axis, side = face // 2, face % 2
    lane = iota((8, 128), 1)
    out = {}
    for i, q in enumerate(OUTGOING[face ^ 1]):
        if axis == 0:
            halves = []
            for half in range(2):
                if i < 4:
                    line = first[2 * i + half : 2 * i + half + 1, :]
                else:
                    turned = pltpu.roll(second, 64, 1)
                    low, high = (second, turned) if offset == 0 else (turned, second)
                    line = jnp.where(
                        lane[0:1] < 64,
                        low[2 * half : 2 * half + 1, :],
                        high[2 * half + 1 : 2 * half + 2, :],
                    )
                halves.append(jnp.broadcast_to(line, (16, 128)))
            out[q] = jnp.concatenate(halves, axis=1)
            continue
        rows = []
        for row in range(2):
            source, base = (first, 16 * (2 * i + row)) if i < 4 else (second, offset + 16 * row)
            if axis == 1:
                piece = pick(source, base + lane % 16, 1)
                rows.append([piece, piece])
            else:
                step = 1 if side == 0 else 15
                rows.append(
                    [
                        pick(source, base + (8 * half + lane // 16 + step) % 16, 1)
                        for half in range(2)
                    ]
                )
        out[q] = join(rows)
    return out


def shifted(value, v):
    if v[0] != 0:
        value = pltpu.roll(value, v[0] % 16, 0)
    lanes = (16 * v[1] + v[2]) % 256
    if lanes != 0:
        value = pltpu.roll(value, lanes, 1)
    return value


def positions():
    row = iota((16, 256), 0)
    lane = iota((16, 256), 1)
    return row, lane // 16, lane % 16


def wall_weights(depth):
    place = positions()
    solid = depth <= 0
    here = depth.astype(F32)
    out = [jnp.where(solid, 1.0, 0.0).astype(F32)]
    for q in range(1, 19):
        v = VELOCITIES[q]
        outside = []
        for axis in range(3):
            if v[axis] != 0:
                outside.append(place[axis] == (0 if v[axis] > 0 else 15))
        away = outside[0] if len(outside) == 1 else outside[0] | outside[1]
        there = shifted(here, v)
        wall = (there <= 0.0) & jnp.logical_not(away) & jnp.logical_not(solid)
        gap = jnp.where(wall, here - there, 1.0)
        own = jnp.where(wall, here, 1.0)
        far = own + own >= gap
        weight = jnp.where(far, 0.5 * gap, 2.0 * own) / jnp.where(far, own, gap)
        value = jnp.where(wall, weight, -1.0)
        if len(outside) == 2:
            value = jnp.where(outside[0] & outside[1], 1.0, value)
        out.append(value)
    return out


def stream(post, start, weights, ghosts):
    place = positions()
    solid = weights(0) > 0.5
    out = [jnp.where(solid, start(0), post(0))]
    for q in range(1, 19):
        v = VELOCITIES[q]
        own = post(q)
        value = own
        for axis in (1, 0, 2):
            if v[axis] != 0:
                edge = place[axis] == (15 if v[axis] > 0 else 0)
                value = jnp.where(edge, ghosts[axis][q], value)
        value = shifted(value, v)
        weight = weights(q)
        value = jnp.where(weight >= 0.0, own + weight * (post(OPPOSITE[q]) - own), value)
        out.append(jnp.where(solid, start(q), value))
    return out


def pack_octants(fields):
    low = iota((8, 128), 1) % 16 < 8
    out = {}
    for ox in range(2):
        for oy in range(2):
            a, b, c, d = [tile(f, ox, oy) for f in fields]
            out[4 * ox + 2 * oy] = (
                jnp.where(low, a, pltpu.roll(b, 8, 1)),
                jnp.where(low, c, pltpu.roll(d, 8, 1)),
            )
            out[4 * ox + 2 * oy + 1] = (
                jnp.where(low, pltpu.roll(a, 120, 1), b),
                jnp.where(low, pltpu.roll(c, 120, 1), d),
            )
    return out


def upsample(pair):
    lane = iota((8, 128), 1)
    sub = iota((8, 128), 0)
    fields = []
    for k in range(4):
        source = pair[k // 2]
        halves = []
        for half in range(2):
            index = (4 * half + lane // 32) * 16 + (lane % 16) // 2 + 8 * (k % 2)
            halves.append(pick(source, index, 1))
        fields.append(
            join([[pick(h, 4 * row + sub // 2, 0) for h in halves] for row in range(2)])
        )
    return fields


def below(fields):
    place = positions()
    out = []
    for axis in range(3):
        step = [0, 0, 0]
        step[axis] = 1
        back = [0, 0, 0]
        back[axis] = -1
        last = place[axis] == 15
        crossed = [jnp.where(last, shifted(f, back), shifted(f, step)) for f in fields]
        chosen = [q for q in range(19) if VELOCITIES[q][axis] != 0]
        out.append(equilibrium(crossed[0], crossed[1:], chosen))
    return out


def restrict(f):
    lane = iota((8, 128), 1)
    sub = iota((8, 128), 0)
    density, momentum = sums(f)
    packed = []
    for field in [density] + momentum:
        field = field + pltpu.roll(field, 255, 1)
        field = field + pltpu.roll(field, 240, 1)
        field = 0.125 * (field + pltpu.roll(field, 15, 0))
        index = ((lane // 16) % 4) * 32 + (lane % 8) * 2
        halves = []
        for half in range(2):
            upper = pick(tile(field, 0, half), (2 * sub) % 8, 0)
            lower = pick(tile(field, 1, half), (2 * sub) % 8, 0)
            halves.append(pick(jnp.where(sub < 4, upper, lower), index, 1))
        packed.append(jnp.where(lane < 64, halves[0], halves[1]))
    low = lane % 16 < 8
    return jnp.where(low, packed[0], packed[1]), jnp.where(low, packed[2], packed[3])


def load(ref):
    return [ref[q] for q in range(19)]


def send_kernel(coarse, fine, coarse_links, fine_links, parents, out, region, octs, work):
    me = lax.axis_index("dev")
    work[...] = coarse[0].reshape(FIELD)
    f = load(work)
    density, u = moments(f)
    for o, pair in pack_octants([density] + u).items():
        octs[o, 0:8, :] = pair[0]
        octs[o, 8:16, :] = pair[1]

    def give(d, carry):
        @pl.when(parents[0, d, 0] == me)
        def _():
            out[d, 24:40, :] = octs[parents[0, d, 1]]

        return carry

    lax.fori_loop(0, 32, give, 0)
    post = collide(f, OMEGA_COARSE)
    for face in range(6):
        first, second = pack_face(post, face, 0)
        if face in (2, 3):
            region[face - 2, 0:8, :] = first
            region[face - 2, 8:16, :] = second
        code = coarse_links[0, me, face]

        @pl.when(code >= 0)
        def _():
            out[code, 0:8, :] = first
            out[code, 16:24, 0:64] = second[:, 0:64]

    work[...] = fine[0].reshape(FIELD)
    post = collide(load(work), OMEGA_FINE)
    for face in range(6):
        first, second = pack_face(post, face, 64)
        code = fine_links[0, me, face]

        @pl.when(code >= 0)
        def _():
            out[code, 8:16, :] = first
            out[code, 16:24, 64:128] = second[:, 64:128]


def prepare_kernel(state, depth, post, start, weights, *, omega):
    start[...] = state[0].reshape(FIELD)
    for q, value in enumerate(collide(load(start), omega)):
        post[q] = value
    for q, value in enumerate(wall_weights(depth[...].reshape(16, 256))):
        weights[q] = value


def merge_ghosts(take):
    ghosts = [{}, {}, {}]
    for face in range(6):
        ghosts[face // 2].update(take(face))
    return ghosts


def middle_kernel(
    received, from_low, from_high, c_post, c_start, c_weights, f_post, f_start, f_weights,
    coarse_links, fine_links, parents, out, coarse_new, state, post, octs,
):
    me = lax.axis_index("dev")

    def coarse_ghost(face):
        code = coarse_links[0, me, face]
        slot = jnp.maximum(code, 0)
        first = received[slot, 0:8, :]
        second = received[slot, 16:24, :]
        if face in (2, 3):
            beside = from_low if face == 2 else from_high
            first = jnp.where(code == -2, beside[0, 0:8, :], first)
            second = jnp.where(code == -2, beside[0, 8:16, :], second)
        plane = unpack_face(first, second, 0, face)
        return {q: jnp.where(code == -1, inflow_value(q), plane[q]) for q in plane}

    new = stream(
        lambda q: c_post[q], lambda q: c_start[q], lambda q: c_weights[q], merge_ghosts(coarse_ghost)
    )
    for q in range(19):
        coarse_new[q] = new[q]
    old_density, old_u = moments([c_start[q] for q in range(19)])
    density, u = moments(new)
    mid = [0.5 * (old_density + density)] + [0.5 * (a + b) for a, b in zip(old_u, u)]
    for o, pair in pack_octants(mid).items():
        octs[o, 0:8, :] = pair[0]
        octs[o, 8:16, :] = pair[1]

    def give(d, carry):
        @pl.when(parents[0, d, 0] == me)
        def _():
            out[d, 16:32, :] = octs[parents[0, d, 1]]

        return carry

    lax.fori_loop(0, 32, give, 0)
    parent = parents[0, me, 0]
    under = below(upsample((received[parent, 24:32, :], received[parent, 32:40, :])))

    def fine_ghost(face):
        code = fine_links[0, me, face]
        slot = jnp.maximum(code, 0)
        plane = unpack_face(received[slot, 8:16, :], received[slot, 16:24, :], 64, face)
        return {q: jnp.where(code >= 0, plane[q], under[face // 2][q]) for q in plane}

    new = stream(
        lambda q: f_post[q], lambda q: f_start[q], lambda q: f_weights[q], merge_ghosts(fine_ghost)
    )
    for q in range(19):
        state[q] = new[q]
    after = collide(new, OMEGA_FINE)
    for q in range(19):
        post[q] = after[q]
    for face in range(6):
        first, second = pack_face(after, face, 0)
        code = fine_links[0, me, face]

        @pl.when(code >= 0)
        def _():
            out[code, 0:8, :] = first
            out[code, 8:16, :] = second


def last_kernel(received, f_post, f_start, f_weights, fine_links, parents, out, state):
    me = lax.axis_index("dev")
    parent = parents[0, me, 0]
    under = below(upsample((received[parent, 16:24, :], received[parent, 24:32, :])))

    def fine_ghost(face):
        code = fine_links[0, me, face]
        slot = jnp.maximum(code, 0)
        plane = unpack_face(received[slot, 0:8, :], received[slot, 8:16, :], 0, face)
        return {q: jnp.where(code >= 0, plane[q], under[face // 2][q]) for q in plane}

    new = stream(
        lambda q: f_post[q], lambda q: f_start[q], lambda q: f_weights[q], merge_ghosts(fine_ghost)
    )
    for q in range(19):
        state[q] = new[q]
    first, second = restrict(new)
    out[parent, 0:8, :] = first
    out[parent, 8:16, :] = second


def finish_kernel(state, fine_out):
    fine_out[0] = state[...].reshape(19, 4096)


def coarse_kernel(received, coarse_new, parents, coarse_out, octs, cover):
    me = lax.axis_index("dev")
    for o in range(8):
        cover[o] = 0

    def take(d, carry):
        @pl.when(parents[0, d, 0] == me)
        def _():
            octs[parents[0, d, 1]] = received[d]
            cover[parents[0, d, 1]] = 1

        return carry

    lax.fori_loop(0, 32, take, 0)
    low = iota((8, 128), 1) % 16 < 8
    tiles = [[[None, None], [None, None]] for _ in range(5)]
    for ox in range(2):
        for oy in range(2):
            o = 4 * ox + 2 * oy
            for k in range(2):
                a = octs[o, 8 * k : 8 * k + 8, :]
                b = octs[o + 1, 8 * k : 8 * k + 8, :]
                tiles[2 * k][ox][oy] = jnp.where(low, a, pltpu.roll(b, 8, 1))
                tiles[2 * k + 1][ox][oy] = jnp.where(low, pltpu.roll(a, 120, 1), b)
            tiles[4][ox][oy] = jnp.where(low, cover[o], cover[o + 1])
    density, jx, jy, jz, covered = [join(t) for t in tiles]
    covered = covered > 0
    density = jnp.where(covered, density, 1.0)
    inverse = 1.0 / density
    fine_eq = equilibrium(density, [jx * inverse, jy * inverse, jz * inverse], range(19))
    new = load(coarse_new)
    own_density, own_u = moments(new)
    own_eq = equilibrium(own_density, own_u, range(19))
    result = [new[q] + jnp.where(covered, fine_eq[q] - own_eq[q], 0.0) for q in range(19)]
    coarse_out[0] = jnp.stack(result).reshape(19, 4096)


VMEM = pl.BlockSpec(memory_space=pltpu.VMEM)
SMEM = pl.BlockSpec(memory_space=pltpu.SMEM)
PARAMS = pltpu.CompilerParams(vmem_limit_bytes=24 * 1024 * 1024)


def call(kernel, outs, ins, smem=(), scratch=(), cost=2_000_000, name=None):
    shapes = [jax.ShapeDtypeStruct(s, F32) for s in outs]
    return pl.pallas_call(
        kernel,
        out_shape=shapes,
        in_specs=[SMEM if i in smem else VMEM for i in range(len(ins))],
        out_specs=[VMEM] * len(outs),
        scratch_shapes=list(scratch),
        compiler_params=PARAMS,
        cost_estimate=pl.CostEstimate(flops=cost, bytes_accessed=2_000_000, transcendentals=0),
        name=name,
    )(*ins)


def swap(value):
    return lax.all_to_all(value, "dev", split_axis=0, concat_axis=0, tiled=True)


def body(fine_state, coarse_state, fine_depth, coarse_depth, fine_links, coarse_links, parents):
    count = lax.axis_size("group")
    octs = pltpu.VMEM((8, 16, 128), F32)
    sent, region = call(
        send_kernel,
        [(32, SLOT1, 128), (2, 16, 128)],
        [coarse_state, fine_state, coarse_links, fine_links, parents],
        smem=(2, 3, 4),
        scratch=[octs, pltpu.VMEM(FIELD, F32)],
        name="send",
    )
    up = [(i, i + 1) for i in range(count - 1)]
    down = [(b, a) for a, b in up]
    received = swap(sent)
    from_low = lax.ppermute(region[1:2], "group", up)
    from_high = lax.ppermute(region[0:1], "group", down)

    def prepare(state, depth, omega, name):
        def kernel(*refs):
            prepare_kernel(*refs, omega=omega)

        return call(kernel, [FIELD, FIELD, FIELD], [state, depth], name=name)

    c_post, c_start, c_weights = prepare(coarse_state, coarse_depth, OMEGA_COARSE, "prepare_coarse")
    f_post, f_start, f_weights = prepare(fine_state, fine_depth, OMEGA_FINE, "prepare_fine")
    sent, coarse_new, state, post = call(
        middle_kernel,
        [(32, SLOT2, 128), FIELD, FIELD, FIELD],
        [
            received, from_low, from_high, c_post, c_start, c_weights, f_post, f_start, f_weights,
            coarse_links, fine_links, parents,
        ],
        smem=(9, 10, 11),
        scratch=[octs],
        name="middle",
    )
    received = swap(sent)
    sent, state = call(
        last_kernel,
        [(32, SLOT3, 128), FIELD],
        [received, post, state, f_weights, fine_links, parents],
        smem=(4, 5),
        name="last",
    )
    received = swap(sent)
    (fine_out,) = call(finish_kernel, [(1, 19, 4096)], [state], name="finish")
    (coarse_out,) = call(
        coarse_kernel,
        [(1, 19, 4096)],
        [received, coarse_new, parents],
        smem=(2,),
        scratch=[octs, pltpu.SMEM((8,), jnp.int32)],
        name="coarse",
    )
    return fine_out, coarse_out


def solution(mesh):
    placed = (
        P(("group", "dev"), None, None),
        P(("group", "dev"), None, None),
        P(("group", "dev"), None),
        P(("group", "dev"), None),
        P("group", None, None),
        P("group", None, None),
        P("group", None, None),
    )
    return jax.shard_map(
        body,
        mesh=mesh,
        in_specs=placed,
        out_specs=(P(("group", "dev"), None, None), P(("group", "dev"), None, None)),
        check_vma=False,
    )
```

time: 1170 us -> 86.2 us (0.07); the launches traced: 1140 us -> 85.8 us
  local copies, waits for them, and re-layouts: 802 us -> 5.03 us
  blocking collectives: 156 us -> 21.5 us
  other arithmetic: 132 us -> 0 us
  between operations: 23.5 us -> 0.78 us
  waiting for transfers between devices: 10.4 us -> 25.7 us
  Pallas kernels: 0 us -> 12 us
    scatter x90 -> x0, local copies, waits for them, and re-layouts: 248 us -> none  [the longest x30 98 us: stream(): padded = padded.at[1:width + 1, position, 1:width + 1].set(plane)]
    another operation x192 -> x0, local copies, waits for them, and re-layouts: 237 us -> none
    all_gather x3 -> x0, blocking collectives: 156 us -> none  [the longest x2 101 us: fine_neighbours(): everyone = lax.all_gather(packets[None], 'dev', axis=0, tiled=True)]
    pad x54 -> x0, local copies, waits for them, and re-layouts: 60.2 us -> none  [stream(): padded = jnp.pad(post[index], 1)]
    broadcast_in_dim x187 -> x0, local copies, waits for them, and re-layouts: 55.2 us -> none  [the longest x186 55.1 us: layer_planes(): layer = jnp.repeat(jnp.repeat(layer, 2, axis=1), 2, axis=2)]
    squeeze x51 -> x0, local copies, waits for them, and re-layouts: 41.7 us -> none  [the longest x39 31.7 us: project(): total = total + VELOCITIES[index][axis] * field[index]]
    unnamed x126 -> x0, other arithmetic: 39.8 us -> none
    unnamed x519 -> x17, local copies, waits for them, and re-layouts: 43.3 us -> 5.03 us
  transfers between devices with their start and end apart: 4 -> 4, of which waited for: 1 -> 3; matrix products, arithmetic and copies ran while one was open for 24% -> 1% of each run, Pallas kernels for 0% -> 1%
where the time goes in v1:
time: 86.2 us; the launch traced here: 85.8 us
  waiting for transfers between devices  25.7 us (30%)
  blocking collectives  21.5 us (25%)
  starting transfers between devices  20.8 us (24%)
  Pallas kernels  12 us (14%)
  local copies, waits for them, and re-layouts  5.03 us (6%)
    all_to_all x2, waiting for transfers between devices, swap(): return lax.all_to_all(value, 'dev', split_axis=0, concat_axis=0, tiled=True)  24 us
    all_to_all x1, blocking collectives, swap(): return lax.all_to_all(value, 'dev', split_axis=0, concat_axis=0, tiled=True)  21.5 us
    all_to_all x2, starting transfers between devices, swap(): return lax.all_to_all(value, 'dev', split_axis=0, concat_axis=0, tiled=True)  16.5 us
    pallas_call x7, Pallas kernels, call(): pl.pallas_call(kernel, out_shape=shapes, in_specs=[SMEM if i in smem else...  12 us
    unnamed x17, local copies, waits for them, and re-layouts  5.03 us
    ppermute x1, starting transfers between devices, body(): from_low = lax.ppermute(region[1:2], 'group', up)  2.41 us
    ppermute x1, starting transfers between devices, body(): from_high = lax.ppermute(region[0:1], 'group', down)  1.92 us
  transfers between devices with their start and end apart: 4, of which 3 were waited for; matrix products, arithmetic and copies ran while one was open for 1% of the time, Pallas kernels for 1%

profile of v1, /device:TPU:16, one launch (start us, length us, event | category | flops | bytes accessed | tf_op | source)
XLA Modules:
  0.0 85.8 jit_solution(5191811864210556164)
XLA Ops:
  0.6 0.0 copy-start.3
  0.6 0.8 copy.13.parents
  1.4 0.0 copy-done.3
  1.4 0.0 copy-start.4
  1.4 0.1 copy.12.fine_links
  1.5 0.6 copy-done.4
  2.1 0.1 copy.11.coarse_links
  2.2 1.2 %copy.10.fine.refs_0_ = f32[1,19,4096]{2,1,0:T(8,128)S(1)} copy(f32[1,19,4096]{2,0,1:T(1,128)} %param.7) | data formatting | bytes 622592 | tf_op args[0]
  3.4 0.0 copy-done.2
  3.4 0.2 copy.9.coarse.refs_0_
  3.6 3.9 %send.1 = (f32[32,40,128]{2,1,0:T(8,128)}, f32[2,16,128]{2,1,0:T(8,128)S(1)}) custom-call(f32[1,19,4096]{2,1,0:T(8,128)S(1)} %copy.9.coarse.refs_0_, f32[1,19,4096]{2,1,0:T(8,128)S(1)} %copy.10.fine.refs_0_, s32[1,32,6]{2,1,0:T(8,128)S(1)} %copy.11.coarse_links, s32[1,32,6]{2,1,0:T(8,128)S(1)} %copy.12.fine_links, s32[1,32,2]{2,1,0:T(8,128)S(1)} %copy.13.parents), custom_call_target="tpu_custom_call" | custom-call | flops 2000000 | bytes 2000000 | tf_op jit(solution)/shard_map/send/pallas_call | solution.py:520
  7.5 11.3 %all-to-all-start = ((f32[32,40,128]{2,1,0:T(8,128)}), f32[32,40,128]{2,1,0:T(8,128)S(1)}, u32[]{:S(2)}, u32[]{:S(2)}) async-start(f32[32,40,128]{2,1,0:T(8,128)} %get-tuple-element.16), calls=%async_computation | async-start | bytes 1310720 | tf_op jit(solution)/shard_map/all_to_all | solution.py:533
  18.8 0.0 copy-start
  18.8 1.9 %collective-permute-start.1 = (f32[1,16,128]{2,1,0:T(8,128)S(1)}, f32[1,16,128]{2,1,0:T(8,128)S(1)}, u32[]{:S(2)}, u32[]{:S(2)}) collective-permute-start(f32[1,16,128]{2,1,0:T(8,128)S(1)} %get-tuple-element.32), channel_id=1, source_target_pairs={{32,0},{64,32},{96,64},{128,96},{160,128},{192,160},{224,192},{33,... | collective-permute-start | bytes 24584 | tf_op jit(solution)/shard_map/ppermute | solution.py:551
  20.7 0.0 copy-start.1
  20.7 2.4 %collective-permute-start = (f32[1,16,128]{2,1,0:T(8,128)S(1)}, f32[1,16,128]{2,1,0:T(8,128)S(1)}, u32[]{:S(2)}, u32[]{:S(2)}) collective-permute-start(f32[1,16,128]{2,1,0:T(8,128)S(1)} %get-tuple-element.33), channel_id=1, source_target_pairs={{0,32},{32,64},{64,96},{96,128},{128,160},{160,192},{192,224},{1,3... | collective-permute-start | bytes 24584 | tf_op jit(solution)/shard_map/ppermute | solution.py:550
  23.2 0.0 copy-done
  23.2 0.4 prepare_fine.1
  23.6 0.0 copy-done.1
  23.6 0.4 prepare_coarse.1
  24.0 0.0 collective-permute-done.1.from_high
  24.0 1.7 %collective-permute-done.from_low = f32[1,16,128]{2,1,0:T(8,128)S(1)} collective-permute-done((f32[1,16,128]{2,1,0:T(8,128)S(1)}, f32[1,16,128]{2,1,0:T(8,128)S(1)}, u32[]{:S(2)}, u32[]{:S(2)}) %collective-permute-start) | collective-permute-done | bytes 8224 | tf_op jit(solution)/shard_map/ppermute | solution.py:550
  25.7 13.5 %all-to-all-done.received = f32[32,40,128]{2,1,0:T(8,128)S(1)} async-done(((f32[32,40,128]{2,1,0:T(8,128)}), f32[32,40,128]{2,1,0:T(8,128)S(1)}, u32[]{:S(2)}, u32[]{:S(2)}) %all-to-all-start) | async-done | bytes 655392 | tf_op jit(solution)/shard_map/all_to_all | solution.py:533
  39.2 3.2 %middle.1 = (f32[32,32,128]{2,1,0:T(8,128)S(1)}, f32[19,16,256]{2,1,0:T(8,128)S(1)}, f32[19,16,256]{2,1,0:T(8,128)S(1)}, f32[19,16,256]{2,1,0:T(8,128)S(1)}) custom-call(f32[32,40,128]{2,1,0:T(8,128)S(1)} %all-to-all-done.received, f32[1,16,128]{2,1,0:T(8,128)S(1)} %collective-permute-done.from_low, f32[1,16,128]{2,1,0:T(8,128)S(1)} %collective-permute-done.1.from_high, ...), custom_call_target="tpu_custom_call" | custom-call | flops 2000000 | bytes 2000000 | tf_op jit(solution)/shard_map/middle/pallas_call | solution.py:520
  42.5 21.5 %all_to_all.15.received = f32[32,32,128]{2,1,0:T(8,128)S(1)} all-to-all(f32[32,32,128]{2,1,0:T(8,128)S(1)} %get-tuple-element.24), channel_id=1, replica_groups=mesh['group'=8,'dev'=32] {'dev'}, dimensions={0} | all-to-all | bytes 1048576 | tf_op jit(solution)/shard_map/all_to_all | solution.py:533
  64.0 2.5 %last.1 = (f32[32,16,128]{2,1,0:T(8,128)}, f32[19,16,256]{2,1,0:T(8,128)S(1)}) custom-call(f32[32,32,128]{2,1,0:T(8,128)S(1)} %all_to_all.15.received, f32[19,16,256]{2,1,0:T(8,128)S(1)} %get-tuple-element.25.f_post, f32[19,16,256]{2,1,0:T(8,128)S(1)} %get-tuple-element.26.f_start, f32[19,16,256]{2,1,0:T(8,128)S(1)} %get-tuple-element.23.f_weights, ...), custom_call_target="tpu_custom_call" | custom-call | flops 2000000 | bytes 2000000 | tf_op jit(solution)/shard_map/last/pallas_call | solution.py:520
  66.4 5.1 %all-to-all-start.2 = ((f32[32,16,128]{2,1,0:T(8,128)}), f32[32,16,128]{2,1,0:T(8,128)S(1)}, u32[]{:S(2)}, u32[]{:S(2)}) async-start(f32[32,16,128]{2,1,0:T(8,128)} %get-tuple-element.28), calls=%async_computation.2 | async-start | bytes 524288 | tf_op jit(solution)/shard_map/all_to_all | solution.py:533
  71.6 0.1 finish.1
  71.6 1.0 %copy.22 = f32[1,19,4096]{2,0,1:T(1,128)} copy(f32[1,19,4096]{2,1,0:T(8,128)S(1)} %finish.1) | data formatting | bytes 622592
  72.7 10.5 %all-to-all-done.2.received = f32[32,16,128]{2,1,0:T(8,128)S(1)} async-done(((f32[32,16,128]{2,1,0:T(8,128)}), f32[32,16,128]{2,1,0:T(8,128)S(1)}, u32[]{:S(2)}, u32[]{:S(2)}) %all-to-all-start.2) | async-done | bytes 262176 | tf_op jit(solution)/shard_map/all_to_all | solution.py:533
  83.2 1.5 %coarse.2 = f32[1,19,4096]{2,1,0:T(8,128)S(1)} custom-call(f32[32,16,128]{2,1,0:T(8,128)S(1)} %all-to-all-done.2.received, f32[19,16,256]{2,1,0:T(8,128)S(1)} %get-tuple-element.29.coarse_new, s32[1,32,2]{2,1,0:T(8,128)S(1)} %copy.13.parents), custom_call_target="tpu_custom_call" | custom-call | flops 2000000 | bytes 2000000 | tf_op jit(solution)/shard_map/coarse/pallas_call | solution.py:520
  84.8 1.0 %copy.23 = f32[1,19,4096]{2,0,1:T(1,128)} copy(f32[1,19,4096]{2,1,0:T(8,128)S(1)} %coarse.2) | data formatting | bytes 622592
  (2 shorter events, 0.0 us)
Async XLA Ops:
  0.6 0.8 copy-start.3
  1.4 0.7 copy-start.4
  2.2 1.2 %copy-start.2 = (f32[1,19,4096]{2,0,1:T(1,128)S(1)}, f32[1,19,4096]{2,0,1:T(1,128)}, u32[]{:S(2)}) copy-start(f32[1,19,4096]{2,0,1:T(1,128)} %param.8) | copy-start | bytes 933892
  7.5 31.8 %all-to-all-start = ((f32[32,40,128]{2,1,0:T(8,128)}), f32[32,40,128]{2,1,0:T(8,128)S(1)}, u32[]{:S(2)}, u32[]{:S(2)}) async-start(f32[32,40,128]{2,1,0:T(8,128)} %get-tuple-element.16), calls=%async_computation | async-start | bytes 1310720 | tf_op jit(solution)/shard_map/all_to_all | solution.py:533
  18.8 4.4 %copy-start = (s32[1,4096]{1,0:T(1,128)S(1)}, s32[1,4096]{1,0:T(1,128)}, u32[]{:S(2)}) copy-start(s32[1,4096]{1,0:T(1,128)} %refs_1_.3) | copy-start | bytes 49156
  18.8 5.2 %collective-permute-start.1 = (f32[1,16,128]{2,1,0:T(8,128)S(1)}, f32[1,16,128]{2,1,0:T(8,128)S(1)}, u32[]{:S(2)}, u32[]{:S(2)}) collective-permute-start(f32[1,16,128]{2,1,0:T(8,128)S(1)} %get-tuple-element.32), channel_id=1, source_target_pairs={{32,0},{64,32},{96,64},{128,96},{160,128},{192,160},{224,192},{33,... | collective-permute-start | bytes 24584 | tf_op jit(solution)/shard_map/ppermute | solution.py:551
  20.7 2.9 %copy-start.1 = (s32[1,4096]{1,0:T(1,128)S(1)}, s32[1,4096]{1,0:T(1,128)}, u32[]{:S(2)}) copy-start(s32[1,4096]{1,0:T(1,128)} %refs_1_.2) | copy-start | bytes 49156
  20.7 5.0 %collective-permute-start = (f32[1,16,128]{2,1,0:T(8,128)S(1)}, f32[1,16,128]{2,1,0:T(8,128)S(1)}, u32[]{:S(2)}, u32[]{:S(2)}) collective-permute-start(f32[1,16,128]{2,1,0:T(8,128)S(1)} %get-tuple-element.33), channel_id=1, source_target_pairs={{0,32},{32,64},{64,96},{96,128},{128,160},{160,192},{192,224},{1,3... | collective-permute-start | bytes 24584 | tf_op jit(solution)/shard_map/ppermute | solution.py:550
  66.4 16.8 %all-to-all-start.2 = ((f32[32,16,128]{2,1,0:T(8,128)}), f32[32,16,128]{2,1,0:T(8,128)S(1)}, u32[]{:S(2)}, u32[]{:S(2)}) async-start(f32[32,16,128]{2,1,0:T(8,128)} %get-tuple-element.28), calls=%async_computation.2 | async-start | bytes 524288 | tf_op jit(solution)/shard_map/all_to_all | solution.py:533

commit v2 on v1

--- a/solution.py
+++ b/solution.py
@@ -36,8 +36,9 @@
 INFLOW = 0.05
 F32 = jnp.float32
 FIELD = (19, 16, 256)
-SLOT1 = 40
-SLOT2 = 32
+CELL_ROWS = (19, 32, 128)
+SLOT1 = 32
+SLOT2 = 24
 SLOT3 = 16
 
 
@@ -118,41 +119,39 @@
     return [(1.0 - omega) * f[q] + omega * rest[q] for q in range(19)]
 
 
-def pack_face(post, face, offset):
+def row_parts(top, bottom, lane, sub):
+    both = jnp.where(sub < 4, jnp.broadcast_to(top, (8, 128)), jnp.broadcast_to(bottom, (8, 128)))
+    return pick(both, 32 * (sub & 3) + (lane & 31), 1)
+
+
+def pack_face(post, face):
     axis, side = face // 2, face % 2
     lane = iota((8, 128), 1)
     sub = iota((8, 128), 0)
     chosen = [post[q] for q in OUTGOING[face]]
     if axis == 0:
         at = 15 * side
-        rows = [f[at : at + 1, :] for f in chosen]
+        rows = [[f[at : at + 1, 128 * h : 128 * h + 128] for h in range(2)] for f in chosen]
         first = None
         for i in range(4):
             for half in range(2):
-                line = jnp.broadcast_to(rows[i][:, 128 * half : 128 * half + 128], (8, 128))
+                line = jnp.broadcast_to(rows[i][half], (8, 128))
                 first = line if first is None else jnp.where(sub == 2 * i + half, line, first)
-        second = None
-        for half in range(2):
-            line = jnp.broadcast_to(rows[4][:, 128 * half : 128 * half + 128], (8, 128))
-            turned = pltpu.roll(line, 64, 1)
-            low, high = (line, turned) if offset == 0 else (turned, line)
-            for k, value in ((2 * half, low), (2 * half + 1, high)):
-                second = value if second is None else jnp.where(sub == k, value, second)
-        return first, second
+        return first, row_parts(rows[4][0], rows[4][1], lane, sub)
     strips = []
     for f in chosen:
         for row in range(2):
             if axis == 1:
-                strips.append(pick(tile(f, row, side), lane % 16 + 112 * side, 1))
+                strips.append(pick(tile(f, row, side), (lane & 15) + 112 * side, 1))
             else:
-                index = (lane % 8) * 16 + 15 * side
+                index = (lane & 7) * 16 + 15 * side
                 a = pick(tile(f, row, 0), index, 1)
                 b = pick(tile(f, row, 1), index, 1)
-                strips.append(jnp.where(lane % 16 < 8, a, b))
+                strips.append(jnp.where((lane & 15) < 8, a, b))
     first = strips[0]
     for t in range(1, 8):
-        first = jnp.where(lane // 16 == t, strips[t], first)
-    second = jnp.where((lane // 16) % 2 == 0, strips[8], strips[9])
+        first = jnp.where((lane >> 4) == t, strips[t], first)
+    second = jnp.where(((lane >> 4) & 1) == 0, strips[8], strips[9])
     return first, second
 
 
@@ -165,33 +164,65 @@
             halves = []
             for half in range(2):
                 if i < 4:
-                    line = first[2 * i + half : 2 * i + half + 1, :]
+                    line = jnp.broadcast_to(first[2 * i + half : 2 * i + half + 1, :], (8, 128))
                 else:
-                    turned = pltpu.roll(second, 64, 1)
-                    low, high = (second, turned) if offset == 0 else (turned, second)
-                    line = jnp.where(
-                        lane[0:1] < 64,
-                        low[2 * half : 2 * half + 1, :],
-                        high[2 * half + 1 : 2 * half + 2, :],
-                    )
-                halves.append(jnp.broadcast_to(line, (16, 128)))
-            out[q] = jnp.concatenate(halves, axis=1)
+                    line = pick(pick(second, offset + (lane & 31), 1), 4 * half + (lane >> 5), 0)
+                halves.append(line)
+            out[q] = join([halves, halves])
             continue
         rows = []
         for row in range(2):
             source, base = (first, 16 * (2 * i + row)) if i < 4 else (second, offset + 16 * row)
             if axis == 1:
-                piece = pick(source, base + lane % 16, 1)
+                piece = pick(source, base + (lane & 15), 1)
                 rows.append([piece, piece])
             else:
                 step = 1 if side == 0 else 15
                 rows.append(
                     [
-                        pick(source, base + (8 * half + lane // 16 + step) % 16, 1)
+                        pick(source, base + ((8 * half + (lane >> 4) + step) & 15), 1)
                         for half in range(2)
                     ]
                 )
         out[q] = join(rows)
+    return out
+
+
+def pack_shell(pair):
+    lane = iota((8, 128), 1)
+    sub = iota((8, 128), 0)
+    part = lane & 31
+    along_y = part + 96 * (part >> 4)
+    which = part & 3
+    along_z = (part >> 2) * 16 + 8 * (which >> 1) + 7 * (which & 1)
+    segment = lane >> 5
+    a, b = pair
+    rows_a = row_parts(a[0:1, :], a[7:8, :], lane, sub)
+    rows_b = row_parts(b[0:1, :], b[7:8, :], lane, sub)
+    rest = pick(a, jnp.where(segment == 1, along_y, along_z), 1)
+    first = jnp.where(segment == 0, rows_a, jnp.where(segment == 3, rows_b, rest))
+    second = pick(b, jnp.where(segment == 2, along_y, along_z), 1)
+    return first, second
+
+
+def unpack_shell(first, second):
+    lane = iota((8, 128), 1)
+    sub = iota((8, 128), 0)
+    part = lane & 31
+    line = (lane >> 5) + jnp.where(sub == 7, 4, 0)
+    along_y = (lane & 15) + jnp.where(lane >= 112, 16, 0)
+    z = lane & 15
+    along_z = (lane >> 4) * 4 + 2 * (z >> 3) + jnp.where((z & 7) == 7, 1, 0)
+    on_y = (lane < 16) | (lane >= 112)
+    on_x = (sub == 0) | (sub == 7)
+    out = []
+    for rows, base_x, rest, base_y, base_z in (
+        (first, 0, first, 32, 64),
+        (first, 96, second, 64, 96),
+    ):
+        x = pick(pick(rows, base_x + part, 1), line, 0)
+        other = pick(rest, jnp.where(on_y, base_y + along_y, base_z + along_z), 1)
+        out.append(jnp.where(on_x, x, other))
     return out
 
 
@@ -207,7 +238,7 @@
 def positions():
     row = iota((16, 256), 0)
     lane = iota((16, 256), 1)
-    return row, lane // 16, lane % 16
+    return row, lane >> 4, lane & 15
 
 
 def wall_weights(depth):
@@ -255,7 +286,7 @@
 
 
 def pack_octants(fields):
-    low = iota((8, 128), 1) % 16 < 8
+    low = (iota((8, 128), 1) & 15) < 8
     out = {}
     for ox in range(2):
         for oy in range(2):
@@ -279,10 +310,10 @@
         source = pair[k // 2]
         halves = []
         for half in range(2):
-            index = (4 * half + lane // 32) * 16 + (lane % 16) // 2 + 8 * (k % 2)
+            index = (4 * half + (lane >> 5)) * 16 + ((lane & 15) >> 1) + 8 * (k % 2)
             halves.append(pick(source, index, 1))
         fields.append(
-            join([[pick(h, 4 * row + sub // 2, 0) for h in halves] for row in range(2)])
+            join([[pick(h, 4 * row + (sub >> 1), 0) for h in halves] for row in range(2)])
         )
     return fields
 
@@ -311,14 +342,14 @@
         field = field + pltpu.roll(field, 255, 1)
         field = field + pltpu.roll(field, 240, 1)
         field = 0.125 * (field + pltpu.roll(field, 15, 0))
-        index = ((lane // 16) % 4) * 32 + (lane % 8) * 2
+        index = ((lane >> 4) & 3) * 32 + (lane & 7) * 2
         halves = []
         for half in range(2):
-            upper = pick(tile(field, 0, half), (2 * sub) % 8, 0)
-            lower = pick(tile(field, 1, half), (2 * sub) % 8, 0)
+            upper = pick(tile(field, 0, half), (2 * sub) & 7, 0)
+            lower = pick(tile(field, 1, half), (2 * sub) & 7, 0)
             halves.append(pick(jnp.where(sub < 4, upper, lower), index, 1))
         packed.append(jnp.where(lane < 64, halves[0], halves[1]))
-    low = lane % 16 < 8
+    low = (lane & 15) < 8
     return jnp.where(low, packed[0], packed[1]), jnp.where(low, packed[2], packed[3])
 
 
@@ -326,53 +357,63 @@
     return [ref[q] for q in range(19)]
 
 
-def send_kernel(coarse, fine, coarse_links, fine_links, parents, out, region, octs, work):
+def load_cells(ref, q):
+    halves = [ref[q, pl.ds(half, 16, stride=2), :] for half in range(2)]
+    return jnp.concatenate(halves, axis=1)
+
+
+def store_cells(ref, q, value):
+    for half in range(2):
+        ref[q, pl.ds(half, 16, stride=2), :] = value[:, 128 * half : 128 * half + 128]
+
+
+def store_octants(fields, octs):
+    for o, pair in pack_octants(fields).items():
+        first, second = pack_shell(pair)
+        octs[o, 0:8, :] = first
+        octs[o, 8:16, :] = second
+
+
+def give_octants(octs, parents, out, at, shared):
+    for d in range(32):
+        o = parents[1, 0, d]
+        out[d, at : at + 8, :] = octs[o, 0:8, :]
+        out[d, shared : shared + 8, 64:128] = octs[o, 8:16, 64:128]
+
+
+def give_face(post, face, code, me, out, at, shared, lanes):
+    first, second = pack_face(post, face)
+    slot = jnp.where(code >= 0, code, me)
+    out[slot, at : at + 8, :] = first
+    out[slot, shared : shared + 8, lanes : lanes + 32] = second[:, lanes : lanes + 32]
+    return first, second
+
+
+def send_kernel(coarse, fine, coarse_links, fine_links, parents, out, region, octs):
     me = lax.axis_index("dev")
-    work[...] = coarse[0].reshape(FIELD)
-    f = load(work)
+    f = [load_cells(coarse, q) for q in range(19)]
     density, u = moments(f)
-    for o, pair in pack_octants([density] + u).items():
-        octs[o, 0:8, :] = pair[0]
-        octs[o, 8:16, :] = pair[1]
-
-    def give(d, carry):
-        @pl.when(parents[0, d, 0] == me)
-        def _():
-            out[d, 24:40, :] = octs[parents[0, d, 1]]
-
-        return carry
-
-    lax.fori_loop(0, 32, give, 0)
+    store_octants([density] + u, octs)
     post = collide(f, OMEGA_COARSE)
     for face in range(6):
-        first, second = pack_face(post, face, 0)
+        first, second = give_face(post, face, coarse_links[face, 0, me], me, out, 0, 16, 0)
         if face in (2, 3):
             region[face - 2, 0:8, :] = first
             region[face - 2, 8:16, :] = second
-        code = coarse_links[0, me, face]
-
-        @pl.when(code >= 0)
-        def _():
-            out[code, 0:8, :] = first
-            out[code, 16:24, 0:64] = second[:, 0:64]
-
-    work[...] = fine[0].reshape(FIELD)
-    post = collide(load(work), OMEGA_FINE)
+    post = collide([load_cells(fine, q) for q in range(19)], OMEGA_FINE)
     for face in range(6):
-        first, second = pack_face(post, face, 64)
-        code = fine_links[0, me, face]
-
-        @pl.when(code >= 0)
-        def _():
-            out[code, 8:16, :] = first
-            out[code, 16:24, 64:128] = second[:, 64:128]
+        give_face(post, face, fine_links[face, 0, me], me, out, 8, 16, 32)
+    give_octants(octs, parents, out, 24, 16)
 
 
 def prepare_kernel(state, depth, post, start, weights, *, omega):
-    start[...] = state[0].reshape(FIELD)
-    for q, value in enumerate(collide(load(start), omega)):
+    f = [load_cells(state, q) for q in range(19)]
+    for q in range(19):
+        start[q] = f[q]
+    for q, value in enumerate(collide(f, omega)):
         post[q] = value
-    for q, value in enumerate(wall_weights(depth[...].reshape(16, 256))):
+    halves = [depth[pl.ds(half, 16, stride=2), :] for half in range(2)]
+    for q, value in enumerate(wall_weights(jnp.concatenate(halves, axis=1))):
         weights[q] = value
 
 
@@ -383,6 +424,27 @@
     return ghosts
 
 
+def fine_ghosts(received, links, parents, me, plane_at, shared, moment_at):
+    parent = parents[0, 0, me]
+    shell = unpack_shell(
+        received[parent, moment_at : moment_at + 8, :], received[parent, shared : shared + 8, :]
+    )
+    under = below(upsample(shell))
+
+    def take(face):
+        code = links[face, 0, me]
+        slot = jnp.maximum(code, 0)
+        plane = unpack_face(
+            received[slot, plane_at : plane_at + 8, :],
+            received[slot, shared : shared + 8, :],
+            32,
+            face,
+        )
+        return {q: jnp.where(code >= 0, plane[q], under[face // 2][q]) for q in plane}
+
+    return merge_ghosts(take)
+
+
 def middle_kernel(
     received, from_low, from_high, c_post, c_start, c_weights, f_post, f_start, f_weights,
     coarse_links, fine_links, parents, out, coarse_new, state, post, octs,
@@ -390,7 +452,7 @@
     me = lax.axis_index("dev")
 
     def coarse_ghost(face):
-        code = coarse_links[0, me, face]
+        code = coarse_links[face, 0, me]
         slot = jnp.maximum(code, 0)
         first = received[slot, 0:8, :]
         second = received[slot, 16:24, :]
@@ -409,105 +471,84 @@
     old_density, old_u = moments([c_start[q] for q in range(19)])
     density, u = moments(new)
     mid = [0.5 * (old_density + density)] + [0.5 * (a + b) for a, b in zip(old_u, u)]
-    for o, pair in pack_octants(mid).items():
-        octs[o, 0:8, :] = pair[0]
-        octs[o, 8:16, :] = pair[1]
-
-    def give(d, carry):
-        @pl.when(parents[0, d, 0] == me)
-        def _():
-            out[d, 16:32, :] = octs[parents[0, d, 1]]
-
-        return carry
-
-    lax.fori_loop(0, 32, give, 0)
-    parent = parents[0, me, 0]
-    under = below(upsample((received[parent, 24:32, :], received[parent, 32:40, :])))
-
-    def fine_ghost(face):
-        code = fine_links[0, me, face]
-        slot = jnp.maximum(code, 0)
-        plane = unpack_face(received[slot, 8:16, :], received[slot, 16:24, :], 64, face)
-        return {q: jnp.where(code >= 0, plane[q], under[face // 2][q]) for q in plane}
-
-    new = stream(
-        lambda q: f_post[q], lambda q: f_start[q], lambda q: f_weights[q], merge_ghosts(fine_ghost)
-    )
+    store_octants(mid, octs)
+    ghosts = fine_ghosts(received, fine_links, parents, me, 8, 16, 24)
+    new = stream(lambda q: f_post[q], lambda q: f_start[q], lambda q: f_weights[q], ghosts)
     for q in range(19):
         state[q] = new[q]
     after = collide(new, OMEGA_FINE)
     for q in range(19):
         post[q] = after[q]
     for face in range(6):
-        first, second = pack_face(after, face, 0)
-        code = fine_links[0, me, face]
-
-        @pl.when(code >= 0)
-        def _():
-            out[code, 0:8, :] = first
-            out[code, 8:16, :] = second
+        give_face(after, face, fine_links[face, 0, me], me, out, 0, 8, 32)
+    give_octants(octs, parents, out, 16, 8)
 
 
 def last_kernel(received, f_post, f_start, f_weights, fine_links, parents, out, state):
     me = lax.axis_index("dev")
-    parent = parents[0, me, 0]
-    under = below(upsample((received[parent, 16:24, :], received[parent, 24:32, :])))
-
-    def fine_ghost(face):
-        code = fine_links[0, me, face]
-        slot = jnp.maximum(code, 0)
-        plane = unpack_face(received[slot, 0:8, :], received[slot, 8:16, :], 0, face)
-        return {q: jnp.where(code >= 0, plane[q], under[face // 2][q]) for q in plane}
-
-    new = stream(
-        lambda q: f_post[q], lambda q: f_start[q], lambda q: f_weights[q], merge_ghosts(fine_ghost)
-    )
+    ghosts = fine_ghosts(received, fine_links, parents, me, 0, 8, 16)
+    new = stream(lambda q: f_post[q], lambda q: f_start[q], lambda q: f_weights[q], ghosts)
     for q in range(19):
         state[q] = new[q]
     first, second = restrict(new)
+    parent = parents[0, 0, me]
     out[parent, 0:8, :] = first
     out[parent, 8:16, :] = second
 
 
-def finish_kernel(state, fine_out):
-    fine_out[0] = state[...].reshape(19, 4096)
-
-
-def coarse_kernel(received, coarse_new, parents, coarse_out, octs, cover):
+def finish_kernel(state, coarse_new, parents, fine_out, base, children):
     me = lax.axis_index("dev")
+    for q in range(19):
+        store_cells(fine_out, q, state[q])
     for o in range(8):
-        cover[o] = 0
-
-    def take(d, carry):
-        @pl.when(parents[0, d, 0] == me)
+        children[o] = -1
+
+    def note(d, carry):
+        @pl.when(parents[0, 0, d] == me)
         def _():
-            octs[parents[0, d, 1]] = received[d]
-            cover[parents[0, d, 1]] = 1
+            children[parents[1, 0, d]] = d
 
         return carry
 
-    lax.fori_loop(0, 32, take, 0)
-    low = iota((8, 128), 1) % 16 < 8
-    tiles = [[[None, None], [None, None]] for _ in range(5)]
+    lax.fori_loop(0, 32, note, 0)
+    covered = cover(children)
+    new = load(coarse_new)
+    density, u = moments(new)
+    own = equilibrium(density, u, range(19))
+    for q in range(19):
+        base[q] = jnp.where(covered, new[q] - own[q], new[q])
+
+
+def cover(children):
+    low = (iota((8, 128), 1) & 15) < 8
+    tiles = [[None, None], [None, None]]
     for ox in range(2):
         for oy in range(2):
             o = 4 * ox + 2 * oy
+            tiles[ox][oy] = jnp.where(low, children[o], children[o + 1])
+    return join(tiles) >= 0
+
+
+def coarse_kernel(received, base, children, coarse_out):
+    low = (iota((8, 128), 1) & 15) < 8
+    tiles = [[[None, None], [None, None]] for _ in range(4)]
+    for ox in range(2):
+        for oy in range(2):
+            o = 4 * ox + 2 * oy
+            near = jnp.maximum(children[o], 0)
+            far = jnp.maximum(children[o + 1], 0)
             for k in range(2):
-                a = octs[o, 8 * k : 8 * k + 8, :]
-                b = octs[o + 1, 8 * k : 8 * k + 8, :]
+                a = received[near, 8 * k : 8 * k + 8, :]
+                b = received[far, 8 * k : 8 * k + 8, :]
                 tiles[2 * k][ox][oy] = jnp.where(low, a, pltpu.roll(b, 8, 1))
                 tiles[2 * k + 1][ox][oy] = jnp.where(low, pltpu.roll(a, 120, 1), b)
-            tiles[4][ox][oy] = jnp.where(low, cover[o], cover[o + 1])
-    density, jx, jy, jz, covered = [join(t) for t in tiles]
-    covered = covered > 0
+    density, jx, jy, jz = [join(t) for t in tiles]
+    covered = cover(children)
     density = jnp.where(covered, density, 1.0)
     inverse = 1.0 / density
     fine_eq = equilibrium(density, [jx * inverse, jy * inverse, jz * inverse], range(19))
-    new = load(coarse_new)
-    own_density, own_u = moments(new)
-    own_eq = equilibrium(own_density, own_u, range(19))
-    result = [new[q] + jnp.where(covered, fine_eq[q] - own_eq[q], 0.0) for q in range(19)]
-    coarse_out[0] = jnp.stack(result).reshape(19, 4096)
+    for q in range(19):
+        store_cells(coarse_out, q, base[q] + jnp.where(covered, fine_eq[q], 0.0))
 
 
 VMEM = pl.BlockSpec(memory_space=pltpu.VMEM)
@@ -515,16 +556,21 @@
 PARAMS = pltpu.CompilerParams(vmem_limit_bytes=24 * 1024 * 1024)
 
 
-def call(kernel, outs, ins, smem=(), scratch=(), cost=2_000_000, name=None):
-    shapes = [jax.ShapeDtypeStruct(s, F32) for s in outs]
+def call(kernel, outs, ins, smem=(), scratch=(), name=None):
+    ints = [not isinstance(s, tuple) for s in outs]
     return pl.pallas_call(
         kernel,
-        out_shape=shapes,
+        out_shape=[
+            jax.ShapeDtypeStruct((s,), jnp.int32) if i else jax.ShapeDtypeStruct(s, F32)
+            for s, i in zip(outs, ints)
+        ],
         in_specs=[SMEM if i in smem else VMEM for i in range(len(ins))],
-        out_specs=[VMEM] * len(outs),
+        out_specs=[SMEM if i else VMEM for i in ints],
         scratch_shapes=list(scratch),
         compiler_params=PARAMS,
-        cost_estimate=pl.CostEstimate(flops=cost, bytes_accessed=2_000_000, transcendentals=0),
+        cost_estimate=pl.CostEstimate(
+            flops=2_000_000, bytes_accessed=2_000_000, transcendentals=0
+        ),
         name=name,
     )(*ins)
 
@@ -535,13 +581,18 @@
 
 def body(fine_state, coarse_state, fine_depth, coarse_depth, fine_links, coarse_links, parents):
     count = lax.axis_size("group")
+    fine_state, coarse_state = fine_state.reshape(CELL_ROWS), coarse_state.reshape(CELL_ROWS)
+    fine_depth, coarse_depth = fine_depth.reshape(32, 128), coarse_depth.reshape(32, 128)
+    fine_links = fine_links.transpose(2, 0, 1)
+    coarse_links = coarse_links.transpose(2, 0, 1)
+    parents = parents.transpose(2, 0, 1)
     octs = pltpu.VMEM((8, 16, 128), F32)
     sent, region = call(
         send_kernel,
         [(32, SLOT1, 128), (2, 16, 128)],
         [coarse_state, fine_state, coarse_links, fine_links, parents],
         smem=(2, 3, 4),
-        scratch=[octs, pltpu.VMEM(FIELD, F32)],
+        scratch=[octs],
         name="send",
     )
     up = [(i, i + 1) for i in range(count - 1)]
@@ -578,16 +629,21 @@
         name="last",
     )
     received = swap(sent)
-    (fine_out,) = call(finish_kernel, [(1, 19, 4096)], [state], name="finish")
+    fine_out, base, children = call(
+        finish_kernel,
+        [CELL_ROWS, FIELD, 8],
+        [state, coarse_new, parents],
+        smem=(2,),
+        name="finish",
+    )
     (coarse_out,) = call(
         coarse_kernel,
-        [(1, 19, 4096)],
-        [received, coarse_new, parents],
+        [CELL_ROWS],
+        [received, base, children],
         smem=(2,),
-        scratch=[octs, pltpu.SMEM((8,), jnp.int32)],
         name="coarse",
     )
-    return fine_out, coarse_out
+    return fine_out.reshape(1, 19, 4096), coarse_out.reshape(1, 19, 4096)
 
 
 def solution(mesh):

time: 86.2 us -> 74.8 us (0.87)
  waiting for transfers between devices: 25.7 us -> 20.6 us
  Pallas kernels: 12 us -> 9.66 us
  blocking collectives: 21.5 us -> 19.3 us
  local copies, waits for them, and re-layouts: 5.03 us -> 2.96 us
    all_to_all x2, waiting for transfers between devices: 24 us -> 19.1 us  [swap(): return lax.all_to_all(value, 'dev', split_axis=0, concat_axis=0, tiled=True)]
    pallas_call x7, Pallas kernels: 12 us -> 9.66 us  [call(): pl.pallas_call(kernel, out_shape=[jax.ShapeDtypeStruct((s,), jnp.int32) i...]
    all_to_all x1, blocking collectives: 21.5 us -> 19.3 us  [swap(): return lax.all_to_all(value, 'dev', split_axis=0, concat_axis=0, tiled=True)]
    unnamed x17 -> x18, local copies, waits for them, and re-layouts: 5.03 us -> 2.95 us
  transfers between devices with their start and end apart: 4 -> 4, of which waited for: 3 -> 3; matrix products, arithmetic and copies ran while one was open for 1% -> 0% of each run, Pallas kernels for 1% -> 3%
where the time goes in v2:
time: 74.8 us; the launch traced here: 74.3 us
  starting transfers between devices  21 us (28%)
  waiting for transfers between devices  20.6 us (28%)
  blocking collectives  19.3 us (26%)
  Pallas kernels  9.66 us (13%)
  local copies, waits for them, and re-layouts  2.96 us (4%)
  between operations  0.78 us (1%)
    all_to_all x1, blocking collectives, swap(): return lax.all_to_all(value, 'dev', split_axis=0, concat_axis=0, tiled=True)  19.3 us
    all_to_all x2, waiting for transfers between devices, swap(): return lax.all_to_all(value, 'dev', split_axis=0, concat_axis=0, tiled=True)  19.1 us
    all_to_all x2, starting transfers between devices, swap(): return lax.all_to_all(value, 'dev', split_axis=0, concat_axis=0, tiled=True)  16.6 us
    pallas_call x7, Pallas kernels, call(): pl.pallas_call(kernel, out_shape=[jax.ShapeDtypeStruct((s,), jnp.int32) i...  9.66 us
    unnamed x18, local copies, waits for them, and re-layouts  2.95 us
    ppermute x1, starting transfers between devices, body(): from_low = lax.ppermute(region[1:2], 'group', up)  2.41 us
    ppermute x1, starting transfers between devices, body(): from_high = lax.ppermute(region[0:1], 'group', down)  2.05 us
  transfers between devices with their start and end apart: 4, of which 3 were waited for; matrix products, arithmetic and copies ran while one was open for 0% of the time, Pallas kernels for 3%

profile of v2, /device:TPU:16, one launch (start us, length us, event | category | flops | bytes accessed | tf_op | source)
XLA Modules:
  0.0 74.3 jit_solution(15758521246486367813)
XLA Ops:
  0.6 0.0 copy-start.8
  0.6 0.0 copy-start.4
  0.7 0.0 copy-start.5
  0.7 0.7 copy-done.8
  1.3 0.0 copy-done.4
  1.3 0.0 copy-done.5
  1.3 0.0 copy-start
  1.3 1.0 %copy-done = f32[1,19,4096]{2,0,1:T(1,128)S(1)} copy-done((f32[1,19,4096]{2,0,1:T(1,128)S(1)}, f32[1,19,4096]{2,0,1:T(1,128)}, u32[]{:S(2)}) %copy-start) | copy-done | bytes 311320
  2.3 1.0 %copy-done.2 = f32[1,19,4096]{2,0,1:T(1,128)S(1)} copy-done((f32[1,19,4096]{2,0,1:T(1,128)S(1)}, f32[1,19,4096]{2,0,1:T(1,128)}, u32[]{:S(2)}) %copy-start.2) | copy-done | bytes 311320
  3.3 1.8 %send.1 = (f32[32,32,128]{2,1,0:T(8,128)}, f32[2,16,128]{2,1,0:T(8,128)S(1)}) custom-call(f32[19,32,128]{2,1,0:T(8,128)S(1)} %bitcast.13, f32[19,32,128]{2,1,0:T(8,128)S(1)} %bitcast.11, s32[6,1,32]{2,1,0:T(1,128)S(1)} %bitcast.24, s32[6,1,32]{2,1,0:T(1,128)S(1)} %bitcast.15, s32[2,1,32]{2,1,0:T(1,128)S(1)} %bitcast.18), custom_call_target="tpu_custom_call" | custom-call | flops 2000000 | bytes 2000000 | tf_op jit(solution)/shard_map/send/pallas_call | solution.py:561
  5.1 0.0 copy-start.1
  5.1 11.4 %all-to-all-start = ((f32[32,32,128]{2,1,0:T(8,128)}), f32[32,32,128]{2,1,0:T(8,128)S(1)}, u32[]{:S(2)}, u32[]{:S(2)}) async-start(f32[32,32,128]{2,1,0:T(8,128)} %get-tuple-element.19), calls=%async_computation | async-start | bytes 1048576 | tf_op jit(solution)/shard_map/all_to_all | solution.py:579
  16.6 0.0 copy-start.3
  16.6 2.1 %collective-permute-start.1 = (f32[1,16,128]{2,1,0:T(8,128)S(1)}, f32[1,16,128]{2,1,0:T(8,128)S(1)}, u32[]{:S(2)}, u32[]{:S(2)}) collective-permute-start(f32[1,16,128]{2,1,0:T(8,128)S(1)} %get-tuple-element.40), channel_id=1, source_target_pairs={{32,0},{64,32},{96,64},{128,96},{160,128},{192,160},{224,192},{33,... | collective-permute-start | bytes 24584 | tf_op jit(solution)/shard_map/ppermute | solution.py:602
  18.6 2.4 %collective-permute-start = (f32[1,16,128]{2,1,0:T(8,128)S(1)}, f32[1,16,128]{2,1,0:T(8,128)S(1)}, u32[]{:S(2)}, u32[]{:S(2)}) collective-permute-start(f32[1,16,128]{2,1,0:T(8,128)S(1)} %get-tuple-element.41), channel_id=1, source_target_pairs={{0,32},{32,64},{64,96},{96,128},{128,160},{160,192},{192,224},{1,3... | collective-permute-start | bytes 24584 | tf_op jit(solution)/shard_map/ppermute | solution.py:601
  21.1 0.0 copy-done.1
  21.1 0.0 copy-done.6
  21.1 0.0 copy-start.7
  21.1 0.4 prepare_fine.1
  21.5 0.0 copy-done.3
  21.5 0.3 copy-done.7
  21.8 0.4 prepare_coarse.1
  22.2 0.0 collective-permute-done.1.from_high
  22.2 1.4 %collective-permute-done.from_low = f32[1,16,128]{2,1,0:T(8,128)S(1)} collective-permute-done((f32[1,16,128]{2,1,0:T(8,128)S(1)}, f32[1,16,128]{2,1,0:T(8,128)S(1)}, u32[]{:S(2)}, u32[]{:S(2)}) %collective-permute-start) | collective-permute-done | bytes 8224 | tf_op jit(solution)/shard_map/ppermute | solution.py:601
  23.6 9.8 %all-to-all-done.received = f32[32,32,128]{2,1,0:T(8,128)S(1)} async-done(((f32[32,32,128]{2,1,0:T(8,128)}), f32[32,32,128]{2,1,0:T(8,128)S(1)}, u32[]{:S(2)}, u32[]{:S(2)}) %all-to-all-start) | async-done | bytes 524320 | tf_op jit(solution)/shard_map/all_to_all | solution.py:579
  33.4 1.8 %middle.1 = (f32[32,24,128]{2,1,0:T(8,128)S(1)}, f32[19,16,256]{2,1,0:T(8,128)S(1)}, f32[19,16,256]{2,1,0:T(8,128)S(1)}, f32[19,16,256]{2,1,0:T(8,128)S(1)}) custom-call(f32[32,32,128]{2,1,0:T(8,128)S(1)} %all-to-all-done.received, f32[1,16,128]{2,1,0:T(8,128)S(1)} %collective-permute-done.from_low, f32[1,16,128]{2,1,0:T(8,128)S(1)} %collective-permute-done.1.from_high, ...), custom_call_target="tpu_custom_call" | custom-call | flops 2000000 | bytes 2000000 | tf_op jit(solution)/shard_map/middle/pallas_call | solution.py:561
  35.2 19.3 %all_to_all.15.received = f32[32,24,128]{2,1,0:T(8,128)S(1)} all-to-all(f32[32,24,128]{2,1,0:T(8,128)S(1)} %get-tuple-element.27), channel_id=1, replica_groups=mesh['group'=8,'dev'=32] {'dev'}, dimensions={0} | all-to-all | bytes 786432 | tf_op jit(solution)/shard_map/all_to_all | solution.py:579
  54.5 2.1 %last.1 = (f32[32,16,128]{2,1,0:T(8,128)}, f32[19,16,256]{2,1,0:T(8,128)S(1)}) custom-call(f32[32,24,128]{2,1,0:T(8,128)S(1)} %all_to_all.15.received, f32[19,16,256]{2,1,0:T(8,128)S(1)} %get-tuple-element.28.f_post, f32[19,16,256]{2,1,0:T(8,128)S(1)} %get-tuple-element.29.f_start, f32[19,16,256]{2,1,0:T(8,128)S(1)} %get-tuple-element.26.f_weights, ...), custom_call_target="tpu_custom_call" | custom-call | flops 2000000 | bytes 2000000 | tf_op jit(solution)/shard_map/last/pallas_call | solution.py:561
  56.5 5.1 %all-to-all-start.2 = ((f32[32,16,128]{2,1,0:T(8,128)}), f32[32,16,128]{2,1,0:T(8,128)S(1)}, u32[]{:S(2)}, u32[]{:S(2)}) async-start(f32[32,16,128]{2,1,0:T(8,128)} %get-tuple-element.33), calls=%async_computation.2 | async-start | bytes 524288 | tf_op jit(solution)/shard_map/all_to_all | solution.py:579
  61.7 1.8 %finish.1 = (f32[19,32,128]{2,1,0:T(8,128)}, f32[19,16,256]{2,1,0:T(8,128)S(1)}, s32[8]{0:T(128)S(1)}) custom-call(f32[19,16,256]{2,1,0:T(8,128)S(1)} %get-tuple-element.30.state, f32[19,16,256]{2,1,0:T(8,128)S(1)} %get-tuple-element.31.coarse_new, s32[2,1,32]{2,1,0:T(1,128)S(1)} %bitcast.21), custom_call_target="tpu_custom_call" | custom-call | flops 2000000 | bytes 2000000 | tf_op jit(solution)/shard_map/finish/pallas_call | solution.py:561
  63.5 9.3 %all-to-all-done.2.received = f32[32,16,128]{2,1,0:T(8,128)S(1)} async-done(((f32[32,16,128]{2,1,0:T(8,128)}), f32[32,16,128]{2,1,0:T(8,128)S(1)}, u32[]{:S(2)}, u32[]{:S(2)}) %all-to-all-start.2) | async-done | bytes 262176 | tf_op jit(solution)/shard_map/all_to_all | solution.py:579
  72.8 1.4 %coarse.1 = f32[19,32,128]{2,1,0:T(8,128)} custom-call(f32[32,16,128]{2,1,0:T(8,128)S(1)} %all-to-all-done.2.received, f32[19,16,256]{2,1,0:T(8,128)S(1)} %get-tuple-element.34.base, s32[8]{0:T(128)S(1)} %get-tuple-element.35.children), custom_call_target="tpu_custom_call" | custom-call | flops 2000000 | bytes 2000000 | tf_op jit(solution)/shard_map/coarse/pallas_call | solution.py:561
  (3 shorter events, 0.0 us)
Async XLA Ops:
  0.6 0.7 copy-start.8
  0.6 0.7 copy-start.4
  0.7 0.7 copy-start.5
  1.3 1.0 %copy-start = (f32[1,19,4096]{2,0,1:T(1,128)S(1)}, f32[1,19,4096]{2,0,1:T(1,128)}, u32[]{:S(2)}) copy-start(f32[1,19,4096]{2,0,1:T(1,128)} %param.7) | copy-start | bytes 933892
  2.3 1.0 %copy-start.2 = (f32[1,19,4096]{2,0,1:T(1,128)S(1)}, f32[1,19,4096]{2,0,1:T(1,128)}, u32[]{:S(2)}) copy-start(f32[1,19,4096]{2,0,1:T(1,128)} %param.8) | copy-start | bytes 933892
  5.1 16.0 %copy-start.1 = (f32[1,19,4096]{2,0,1:T(1,128)S(1)}, f32[1,19,4096]{2,0,1:T(1,128)}, u32[]{:S(2)}) copy-start(f32[1,19,4096]{2,0,1:T(1,128)} %param.7) | copy-start | bytes 933892
  5.1 16.0 %copy-start.6 = (s32[1,4096]{1,0:T(1,128)S(1)}, s32[1,4096]{1,0:T(1,128)}, u32[]{:S(2)}) copy-start(s32[1,4096]{1,0:T(1,128)} %param.9) | copy-start | bytes 49156
  5.1 28.3 %all-to-all-start = ((f32[32,32,128]{2,1,0:T(8,128)}), f32[32,32,128]{2,1,0:T(8,128)S(1)}, u32[]{:S(2)}, u32[]{:S(2)}) async-start(f32[32,32,128]{2,1,0:T(8,128)} %get-tuple-element.19), calls=%async_computation | async-start | bytes 1048576 | tf_op jit(solution)/shard_map/all_to_all | solution.py:579
  16.6 4.9 %copy-start.3 = (f32[1,19,4096]{2,0,1:T(1,128)S(1)}, f32[1,19,4096]{2,0,1:T(1,128)}, u32[]{:S(2)}) copy-start(f32[1,19,4096]{2,0,1:T(1,128)} %param.8) | copy-start | bytes 933892
  16.6 5.6 %collective-permute-start.1 = (f32[1,16,128]{2,1,0:T(8,128)S(1)}, f32[1,16,128]{2,1,0:T(8,128)S(1)}, u32[]{:S(2)}, u32[]{:S(2)}) collective-permute-start(f32[1,16,128]{2,1,0:T(8,128)S(1)} %get-tuple-element.40), channel_id=1, source_target_pairs={{32,0},{64,32},{96,64},{128,96},{160,128},{192,160},{224,192},{33,... | collective-permute-start | bytes 24584 | tf_op jit(solution)/shard_map/ppermute | solution.py:602
  18.6 5.0 %collective-permute-start = (f32[1,16,128]{2,1,0:T(8,128)S(1)}, f32[1,16,128]{2,1,0:T(8,128)S(1)}, u32[]{:S(2)}, u32[]{:S(2)}) collective-permute-start(f32[1,16,128]{2,1,0:T(8,128)S(1)} %get-tuple-element.41), channel_id=1, source_target_pairs={{0,32},{32,64},{64,96},{96,128},{128,160},{160,192},{192,224},{1,3... | collective-permute-start | bytes 24584 | tf_op jit(solution)/shard_map/ppermute | solution.py:601
  21.1 0.7 copy-start.7
  56.5 16.3 %all-to-all-start.2 = ((f32[32,16,128]{2,1,0:T(8,128)}), f32[32,16,128]{2,1,0:T(8,128)S(1)}, u32[]{:S(2)}, u32[]{:S(2)}) async-start(f32[32,16,128]{2,1,0:T(8,128)} %get-tuple-element.33), calls=%async_computation.2 | async-start | bytes 524288 | tf_op jit(solution)/shard_map/all_to_all | solution.py:579

commit v3 on v2

--- a/solution.py
+++ b/solution.py
@@ -40,6 +40,8 @@
 SLOT1 = 32
 SLOT2 = 24
 SLOT3 = 16
+FINE_LINKS, COARSE_LINKS, PARENT, CHILDREN, OCTANTS, CODES = 0, 8, 16, 24, 32, 64
+COARSE_PARTS = ((0, 7), (7, 6), (13, 6))
 
 
 def inflow_value(q):
@@ -205,27 +207,6 @@
     return first, second
 
 
-def unpack_shell(first, second):
-    lane = iota((8, 128), 1)
-    sub = iota((8, 128), 0)
-    part = lane & 31
-    line = (lane >> 5) + jnp.where(sub == 7, 4, 0)
-    along_y = (lane & 15) + jnp.where(lane >= 112, 16, 0)
-    z = lane & 15
-    along_z = (lane >> 4) * 4 + 2 * (z >> 3) + jnp.where((z & 7) == 7, 1, 0)
-    on_y = (lane < 16) | (lane >= 112)
-    on_x = (sub == 0) | (sub == 7)
-    out = []
-    for rows, base_x, rest, base_y, base_z in (
-        (first, 0, first, 32, 64),
-        (first, 96, second, 64, 96),
-    ):
-        x = pick(pick(rows, base_x + part, 1), line, 0)
-        other = pick(rest, jnp.where(on_y, base_y + along_y, base_z + along_z), 1)
-        out.append(jnp.where(on_x, x, other))
-    return out
-
-
 def shifted(value, v):
     if v[0] != 0:
         value = pltpu.roll(value, v[0] % 16, 0)
@@ -302,34 +283,40 @@
     return out
 
 
-def upsample(pair):
+def below(first, second):
     lane = iota((8, 128), 1)
     sub = iota((8, 128), 0)
-    fields = []
+    z = lane & 15
+    fields = [[], [], []]
     for k in range(4):
-        source = pair[k // 2]
-        halves = []
+        other = k % 2
+        inner = (z >> 1) + 8 * other
+        base = 0 if k < 2 else 96
+        tiles = [[None, None], [None, None]]
         for half in range(2):
-            index = (4 * half + (lane >> 5)) * 16 + ((lane & 15) >> 1) + 8 * (k % 2)
-            halves.append(pick(source, index, 1))
-        fields.append(
-            join([[pick(h, 4 * row + (sub >> 1), 0) for h in halves] for row in range(2)])
-        )
-    return fields
-
-
-def below(fields):
-    place = positions()
+            rows = pick(first, base + ((lane >> 5) & 1) * 16 + inner, 1)
+            for row in range(2):
+                tiles[row][half] = pick(rows, 2 * half + (lane >> 6) + 4 * (1 - row), 0)
+        fields[0].append(join(tiles))
+        rest, base = (first, 32) if k < 2 else (second, 64)
+        for half in range(2):
+            line = pick(rest, base + 16 * (1 - half) + inner, 1)
+            for row in range(2):
+                tiles[row][half] = pick(line, 4 * row + (sub >> 1), 0)
+        fields[1].append(join(tiles))
+        base += 32
+        for half in range(2):
+            y = 8 * half + (lane >> 4)
+            far = 4 * (((y + 1) & 15) >> 1)
+            near = 4 * (((y + 15) & 15) >> 1) + 1
+            line = pick(rest, base + 2 * other + jnp.where(z == 15, far, near), 1)
+            for row in range(2):
+                tiles[row][half] = pick(line, 4 * row + (sub >> 1), 0)
+        fields[2].append(join(tiles))
     out = []
     for axis in range(3):
-        step = [0, 0, 0]
-        step[axis] = 1
-        back = [0, 0, 0]
-        back[axis] = -1
-        last = place[axis] == 15
-        crossed = [jnp.where(last, shifted(f, back), shifted(f, step)) for f in fields]
         chosen = [q for q in range(19) if VELOCITIES[q][axis] != 0]
-        out.append(equilibrium(crossed[0], crossed[1:], chosen))
+        out.append(equilibrium(fields[axis][0], fields[axis][1:], chosen))
     return out
 
 
@@ -337,17 +324,23 @@
     lane = iota((8, 128), 1)
     sub = iota((8, 128), 0)
     density, momentum = sums(f)
+    index = ((lane >> 4) & 3) * 32 + (lane & 7) * 2
+    even = (2 * sub) & 7
     packed = []
     for field in [density] + momentum:
-        field = field + pltpu.roll(field, 255, 1)
-        field = field + pltpu.roll(field, 240, 1)
-        field = 0.125 * (field + pltpu.roll(field, 15, 0))
-        index = ((lane >> 4) & 3) * 32 + (lane & 7) * 2
         halves = []
         for half in range(2):
-            upper = pick(tile(field, 0, half), (2 * sub) & 7, 0)
-            lower = pick(tile(field, 1, half), (2 * sub) & 7, 0)
-            halves.append(pick(jnp.where(sub < 4, upper, lower), index, 1))
+            lines = [
+                jnp.where(
+                    sub < 4,
+                    pick(tile(field, 0, half), even + odd, 0),
+                    pick(tile(field, 1, half), even + odd, 0),
+                )
+                for odd in range(2)
+            ]
+            line = lines[0] + lines[1]
+            parts = [pick(line, index + step, 1) for step in (0, 1, 16, 17)]
+            halves.append(0.125 * ((parts[0] + parts[1]) + (parts[2] + parts[3])))
         packed.append(jnp.where(lane < 64, halves[0], halves[1]))
     low = (lane & 15) < 8
     return jnp.where(low, packed[0], packed[1]), jnp.where(low, packed[2], packed[3])
@@ -374,9 +367,9 @@
         octs[o, 8:16, :] = second
 
 
-def give_octants(octs, parents, out, at, shared):
+def give_octants(octs, octant, out, at, shared):
     for d in range(32):
-        o = parents[1, 0, d]
+        o = octant(d)
         out[d, at : at + 8, :] = octs[o, 0:8, :]
         out[d, shared : shared + 8, 64:128] = octs[o, 8:16, 64:128]
 
@@ -389,21 +382,54 @@
     return first, second
 
 
-def send_kernel(coarse, fine, coarse_links, fine_links, parents, out, region, octs):
+def send_kernel(
+    coarse_in, fine_in, coarse_table, fine_table, parent_table, out, region,
+    coarse, fine, coarse_links, fine_links, parents, slots, octs, sems,
+):
+    fetch = [
+        pltpu.make_async_copy(source, target, sems.at[i])
+        for i, (source, target) in enumerate(
+            (
+                (coarse_in, coarse),
+                (coarse_table, coarse_links),
+                (fine_in, fine),
+                (fine_table, fine_links),
+                (parent_table, parents),
+            )
+        )
+    ]
+    for copy in fetch:
+        copy.start()
+
+    def put(part):
+        rows = pl.ds(8 * part, 8)
+        return pltpu.make_async_copy(slots.at[:, rows, :], out.at[:, rows, :], sems.at[5 + part])
+
     me = lax.axis_index("dev")
+    fetch[0].wait()
+    fetch[1].wait()
     f = [load_cells(coarse, q) for q in range(19)]
     density, u = moments(f)
     store_octants([density] + u, octs)
     post = collide(f, OMEGA_COARSE)
     for face in range(6):
-        first, second = give_face(post, face, coarse_links[face, 0, me], me, out, 0, 16, 0)
+        first, second = give_face(post, face, coarse_links[face, 0, me], me, slots, 0, 16, 0)
         if face in (2, 3):
             region[face - 2, 0:8, :] = first
             region[face - 2, 8:16, :] = second
+    put(0).start()
+    fetch[4].wait()
+    give_octants(octs, lambda d: parents[1, 0, d], slots, 24, 16)
+    put(3).start()
+    fetch[2].wait()
+    fetch[3].wait()
     post = collide([load_cells(fine, q) for q in range(19)], OMEGA_FINE)
     for face in range(6):
-        give_face(post, face, fine_links[face, 0, me], me, out, 8, 16, 32)
-    give_octants(octs, parents, out, 24, 16)
+        give_face(post, face, fine_links[face, 0, me], me, slots, 8, 16, 32)
+    put(1).start()
+    put(2).start()
+    for part in range(4):
+        put(part).wait()
 
 
 def prepare_kernel(state, depth, post, start, weights, *, omega):
@@ -417,6 +443,27 @@
         weights[q] = value
 
 
+def codes_kernel(coarse_links, fine_links, parents, codes):
+    me = lax.axis_index("dev")
+    for face in range(6):
+        codes[FINE_LINKS + face] = fine_links[face, 0, me]
+        codes[COARSE_LINKS + face] = coarse_links[face, 0, me]
+    codes[PARENT] = parents[0, 0, me]
+    for o in range(8):
+        codes[CHILDREN + o] = -1
+
+    def note(d, carry):
+        codes[OCTANTS + d] = parents[1, 0, d]
+
+        @pl.when(parents[0, 0, d] == me)
+        def _():
+            codes[CHILDREN + parents[1, 0, d]] = d
+
+        return carry
+
+    lax.fori_loop(0, 32, note, 0)
+
+
 def merge_ghosts(take):
     ghosts = [{}, {}, {}]
     for face in range(6):
@@ -424,15 +471,14 @@
     return ghosts
 
 
-def fine_ghosts(received, links, parents, me, plane_at, shared, moment_at):
-    parent = parents[0, 0, me]
-    shell = unpack_shell(
+def fine_ghosts(received, codes, plane_at, shared, moment_at):
+    parent = codes[PARENT]
+    under = below(
         received[parent, moment_at : moment_at + 8, :], received[parent, shared : shared + 8, :]
     )
-    under = below(upsample(shell))
 
     def take(face):
-        code = links[face, 0, me]
+        code = codes[FINE_LINKS + face]
         slot = jnp.maximum(code, 0)
         plane = unpack_face(
             received[slot, plane_at : plane_at + 8, :],
@@ -447,12 +493,12 @@
 
 def middle_kernel(
     received, from_low, from_high, c_post, c_start, c_weights, f_post, f_start, f_weights,
-    coarse_links, fine_links, parents, out, coarse_new, state, post, octs,
+    codes, out, coarse_new, state, post, octs,
 ):
     me = lax.axis_index("dev")
 
     def coarse_ghost(face):
-        code = coarse_links[face, 0, me]
+        code = codes[COARSE_LINKS + face]
         slot = jnp.maximum(code, 0)
         first = received[slot, 0:8, :]
         second = received[slot, 16:24, :]
@@ -472,7 +518,7 @@
     density, u = moments(new)
     mid = [0.5 * (old_density + density)] + [0.5 * (a + b) for a, b in zip(old_u, u)]
     store_octants(mid, octs)
-    ghosts = fine_ghosts(received, fine_links, parents, me, 8, 16, 24)
+    ghosts = fine_ghosts(received, codes, 8, 16, 24)
     new = stream(lambda q: f_post[q], lambda q: f_start[q], lambda q: f_weights[q], ghosts)
     for q in range(19):
         state[q] = new[q]
@@ -480,38 +526,27 @@
     for q in range(19):
         post[q] = after[q]
     for face in range(6):
-        give_face(after, face, fine_links[face, 0, me], me, out, 0, 8, 32)
-    give_octants(octs, parents, out, 16, 8)
-
-
-def last_kernel(received, f_post, f_start, f_weights, fine_links, parents, out, state):
-    me = lax.axis_index("dev")
-    ghosts = fine_ghosts(received, fine_links, parents, me, 0, 8, 16)
+        give_face(after, face, codes[FINE_LINKS + face], me, out, 0, 8, 32)
+    give_octants(octs, lambda d: codes[OCTANTS + d], out, 16, 8)
+
+
+def last_kernel(received, f_post, f_start, f_weights, codes, out, state, slot, sem):
+    ghosts = fine_ghosts(received, codes, 0, 8, 16)
     new = stream(lambda q: f_post[q], lambda q: f_start[q], lambda q: f_weights[q], ghosts)
+    first, second = restrict(new)
+    slot[0:8, :] = first
+    slot[8:16, :] = second
+    copy = pltpu.make_async_copy(slot, out.at[codes[PARENT]], sem)
+    copy.start()
     for q in range(19):
         state[q] = new[q]
-    first, second = restrict(new)
-    parent = parents[0, 0, me]
-    out[parent, 0:8, :] = first
-    out[parent, 8:16, :] = second
-
-
-def finish_kernel(state, coarse_new, parents, fine_out, base, children):
-    me = lax.axis_index("dev")
+    copy.wait()
+
+
+def finish_kernel(state, coarse_new, codes, fine_out, base):
     for q in range(19):
         store_cells(fine_out, q, state[q])
-    for o in range(8):
-        children[o] = -1
-
-    def note(d, carry):
-        @pl.when(parents[0, 0, d] == me)
-        def _():
-            children[parents[1, 0, d]] = d
-
-        return carry
-
-    lax.fori_loop(0, 32, note, 0)
-    covered = cover(children)
+    covered = cover(codes)
     new = load(coarse_new)
     density, u = moments(new)
     own = equilibrium(density, u, range(19))
@@ -519,44 +554,72 @@
         base[q] = jnp.where(covered, new[q] - own[q], new[q])
 
 
-def cover(children):
+def cover(codes):
     low = (iota((8, 128), 1) & 15) < 8
     tiles = [[None, None], [None, None]]
     for ox in range(2):
         for oy in range(2):
             o = 4 * ox + 2 * oy
-            tiles[ox][oy] = jnp.where(low, children[o], children[o + 1])
+            tiles[ox][oy] = jnp.where(low, codes[CHILDREN + o], codes[CHILDREN + o + 1])
     return join(tiles) >= 0
 
 
-def coarse_kernel(received, base, children, coarse_out):
+def coarse_kernel(received, base, codes, coarse_out, cells, sems):
     low = (iota((8, 128), 1) & 15) < 8
     tiles = [[[None, None], [None, None]] for _ in range(4)]
     for ox in range(2):
         for oy in range(2):
             o = 4 * ox + 2 * oy
-            near = jnp.maximum(children[o], 0)
-            far = jnp.maximum(children[o + 1], 0)
+            near = jnp.maximum(codes[CHILDREN + o], 0)
+            far = jnp.maximum(codes[CHILDREN + o + 1], 0)
             for k in range(2):
                 a = received[near, 8 * k : 8 * k + 8, :]
                 b = received[far, 8 * k : 8 * k + 8, :]
                 tiles[2 * k][ox][oy] = jnp.where(low, a, pltpu.roll(b, 8, 1))
                 tiles[2 * k + 1][ox][oy] = jnp.where(low, pltpu.roll(a, 120, 1), b)
     density, jx, jy, jz = [join(t) for t in tiles]
-    covered = cover(children)
+    covered = cover(codes)
     density = jnp.where(covered, density, 1.0)
     inverse = 1.0 / density
     fine_eq = equilibrium(density, [jx * inverse, jy * inverse, jz * inverse], range(19))
-    for q in range(19):
-        store_cells(coarse_out, q, base[q] + jnp.where(covered, fine_eq[q], 0.0))
+    copies = []
+    for i, (low_q, count) in enumerate(COARSE_PARTS):
+        for q in range(low_q, low_q + count):
+            store_cells(cells, q, base[q] + jnp.where(covered, fine_eq[q], 0.0))
+        part = pl.ds(low_q, count)
+        copies.append(pltpu.make_async_copy(cells.at[part], coarse_out.at[part], sems.at[i]))
+        copies[-1].start()
+    for copy in copies:
+        copy.wait()
 
 
 VMEM = pl.BlockSpec(memory_space=pltpu.VMEM)
 SMEM = pl.BlockSpec(memory_space=pltpu.SMEM)
-PARAMS = pltpu.CompilerParams(vmem_limit_bytes=24 * 1024 * 1024)
-
-
-def call(kernel, outs, ins, smem=(), scratch=(), name=None):
+HBM = pl.BlockSpec(memory_space=pltpu.HBM)
+SOME_VMEM = 24 * 1024 * 1024
+MOST_VMEM = 60 * 1024 * 1024
+
+
+OCTS = pltpu.VMEM((8, 16, 128), F32)
+LINKS = pltpu.SMEM((6, 1, 32), jnp.int32)
+SEND_SCRATCH = [
+    pltpu.VMEM(CELL_ROWS, F32),
+    pltpu.VMEM(CELL_ROWS, F32),
+    LINKS,
+    LINKS,
+    pltpu.SMEM((2, 1, 32), jnp.int32),
+    pltpu.VMEM((32, SLOT1, 128), F32),
+    OCTS,
+    pltpu.SemaphoreType.DMA((9,)),
+]
+LAST_SCRATCH = [pltpu.VMEM((SLOT3, 128), F32), pltpu.SemaphoreType.DMA]
+COARSE_SCRATCH = [pltpu.VMEM(CELL_ROWS, F32), pltpu.SemaphoreType.DMA((len(COARSE_PARTS),))]
+
+
+def call(kernel, outs, ins, smem=(), hbm=(), hbm_outs=(), scratch=(), vmem=SOME_VMEM, name=None):
+    def space(i, scalars, far):
+        return SMEM if scalars else HBM if i in far else VMEM
+
     ints = [not isinstance(s, tuple) for s in outs]
     return pl.pallas_call(
         kernel,
@@ -564,10 +627,10 @@
             jax.ShapeDtypeStruct((s,), jnp.int32) if i else jax.ShapeDtypeStruct(s, F32)
             for s, i in zip(outs, ints)
         ],
-        in_specs=[SMEM if i in smem else VMEM for i in range(len(ins))],
-        out_specs=[SMEM if i else VMEM for i in ints],
+        in_specs=[space(i, i in smem, hbm) for i in range(len(ins))],
+        out_specs=[space(i, scalars, hbm_outs) for i, scalars in enumerate(ints)],
         scratch_shapes=list(scratch),
-        compiler_params=PARAMS,
+        compiler_params=pltpu.CompilerParams(vmem_limit_bytes=vmem),
         cost_estimate=pl.CostEstimate(
             flops=2_000_000, bytes_accessed=2_000_000, transcendentals=0
         ),
@@ -586,13 +649,14 @@
     fine_links = fine_links.transpose(2, 0, 1)
     coarse_links = coarse_links.transpose(2, 0, 1)
     parents = parents.transpose(2, 0, 1)
-    octs = pltpu.VMEM((8, 16, 128), F32)
     sent, region = call(
         send_kernel,
         [(32, SLOT1, 128), (2, 16, 128)],
         [coarse_state, fine_state, coarse_links, fine_links, parents],
-        smem=(2, 3, 4),
-        scratch=[octs],
+        hbm=(0, 1, 2, 3, 4),
+        hbm_outs=(0,),
+        scratch=SEND_SCRATCH,
+        vmem=MOST_VMEM,
         name="send",
     )
     up = [(i, i + 1) for i in range(count - 1)]
@@ -609,38 +673,45 @@
 
     c_post, c_start, c_weights = prepare(coarse_state, coarse_depth, OMEGA_COARSE, "prepare_coarse")
     f_post, f_start, f_weights = prepare(fine_state, fine_depth, OMEGA_FINE, "prepare_fine")
+    (codes,) = call(
+        codes_kernel, [CODES], [coarse_links, fine_links, parents], smem=(0, 1, 2), name="codes"
+    )
     sent, coarse_new, state, post = call(
         middle_kernel,
         [(32, SLOT2, 128), FIELD, FIELD, FIELD],
         [
             received, from_low, from_high, c_post, c_start, c_weights, f_post, f_start, f_weights,
-            coarse_links, fine_links, parents,
+            codes,
         ],
-        smem=(9, 10, 11),
-        scratch=[octs],
+        smem=(9,),
+        scratch=[OCTS],
         name="middle",
     )
     received = swap(sent)
     sent, state = call(
         last_kernel,
         [(32, SLOT3, 128), FIELD],
-        [received, post, state, f_weights, fine_links, parents],
-        smem=(4, 5),
+        [received, post, state, f_weights, codes],
+        smem=(4,),
+        hbm_outs=(0,),
+        scratch=LAST_SCRATCH,
         name="last",
     )
     received = swap(sent)
-    fine_out, base, children = call(
+    fine_out, base = call(
         finish_kernel,
-        [CELL_ROWS, FIELD, 8],
-        [state, coarse_new, parents],
+        [CELL_ROWS, FIELD],
+        [state, coarse_new, codes],
         smem=(2,),
         name="finish",
     )
     (coarse_out,) = call(
         coarse_kernel,
         [CELL_ROWS],
-        [received, base, children],
+        [received, base, codes],
         smem=(2,),
+        hbm_outs=(0,),
+        scratch=COARSE_SCRATCH,
         name="coarse",
     )
     return fine_out.reshape(1, 19, 4096), coarse_out.reshape(1, 19, 4096)

time: 74.8 us -> 72.8 us (0.973)
  local copies, waits for them, and re-layouts: 2.96 us -> 0.36 us
  Pallas kernels: 9.66 us -> 11.5 us
  waiting for transfers between devices: 20.6 us -> 19.2 us
    unnamed x18 -> x16, local copies, waits for them, and re-layouts: 2.95 us -> 0.36 us
    pallas_call x7 -> x8, Pallas kernels: 9.66 us -> 11.5 us  [call(): pl.pallas_call(kernel, out_shape=[jax.ShapeDtypeStruct((s,), jnp.int32) i...]
    ppermute x1, waiting for transfers between devices: 1.42 us -> 0.01 us  [body(): from_low = lax.ppermute(region[1:2], 'group', up)]
  transfers between devices with their start and end apart: 4 -> 4, of which waited for: 3 -> 2; matrix products, arithmetic and copies ran while one was open for 0% -> 0% of each run, Pallas kernels for 3% -> 5%
where the time goes in v3:
time: 72.8 us; the launch traced here: 72.3 us
  starting transfers between devices  21.1 us (29%)
  blocking collectives  19.3 us (27%)
  waiting for transfers between devices  19.2 us (26%)
  Pallas kernels  11.5 us (16%)
  between operations  0.85 us (1%)
    all_to_all x1, blocking collectives, swap(): return lax.all_to_all(value, 'dev', split_axis=0, concat_axis=0, tiled=True)  19.3 us
    all_to_all x2, waiting for transfers between devices, swap(): return lax.all_to_all(value, 'dev', split_axis=0, concat_axis=0, tiled=True)  19.2 us
    all_to_all x2, starting transfers between devices, swap(): return lax.all_to_all(value, 'dev', split_axis=0, concat_axis=0, tiled=True)  16.6 us
    pallas_call x8, Pallas kernels, call(): pl.pallas_call(kernel, out_shape=[jax.ShapeDtypeStruct((s,), jnp.int32) i...  11.5 us
    ppermute x1, starting transfers between devices, body(): from_low = lax.ppermute(region[1:2], 'group', up)  2.41 us
    ppermute x1, starting transfers between devices, body(): from_high = lax.ppermute(region[0:1], 'group', down)  2.05 us
  transfers between devices with their start and end apart: 4, of which 2 were waited for; matrix products, arithmetic and copies ran while one was open for 0% of the time, Pallas kernels for 5%

profile of v3, /device:TPU:16, one launch (start us, length us, event | category | flops | bytes accessed | tf_op | source)
XLA Modules:
  0.0 72.3 jit_solution(5552215460851259726)
XLA Ops:
  0.6 2.9 %send.1 = (f32[32,32,128]{2,1,0:T(8,128)}, f32[2,16,128]{2,1,0:T(8,128)}) custom-call(f32[19,32,128]{2,1,0:T(8,128)} %bitcast.13, f32[19,32,128]{2,1,0:T(8,128)} %bitcast.11, s32[6,1,32]{2,1,0:T(1,128)} %bitcast.17, s32[6,1,32]{2,1,0:T(1,128)} %bitcast.19, s32[2,1,32]{2,1,0:T(1,128)} %bitcast.21), custom_call_target="tpu_custom_call" | custom-call | flops 2000000 | bytes 2000000 | tf_op jit(solution)/shard_map/send/pallas_call | solution.py:624
  3.6 0.0 copy-start.7
  3.6 0.0 copy-start.4
  3.6 0.0 copy-start.5
  3.6 0.0 copy-start.6
  3.6 0.0 copy-start
  3.6 0.0 copy-start.2
  3.6 11.5 %all-to-all-start = ((f32[32,32,128]{2,1,0:T(8,128)}), f32[32,32,128]{2,1,0:T(8,128)S(1)}, u32[]{:S(2)}, u32[]{:S(2)}) async-start(f32[32,32,128]{2,1,0:T(8,128)} %get-tuple-element.18), calls=%async_computation | async-start | bytes 1048576 | tf_op jit(solution)/shard_map/all_to_all | solution.py:642
  15.1 0.0 copy-start.1
  15.1 0.0 copy-done.7
  15.1 2.1 %collective-permute-start.1 = (f32[1,16,128]{2,1,0:T(8,128)S(1)}, f32[1,16,128]{2,1,0:T(8,128)S(1)}, u32[]{:S(2)}, u32[]{:S(2)}) collective-permute-start(f32[1,16,128]{2,1,0:T(8,128)S(1)} %get-tuple-element.38), channel_id=1, source_target_pairs={{32,0},{64,32},{96,64},{128,96},{160,128},{192,160},{224,192},{33,... | collective-permute-start | bytes 24584 | tf_op jit(solution)/shard_map/ppermute | solution.py:666
  17.2 2.4 %collective-permute-start = (f32[1,16,128]{2,1,0:T(8,128)S(1)}, f32[1,16,128]{2,1,0:T(8,128)S(1)}, u32[]{:S(2)}, u32[]{:S(2)}) collective-permute-start(f32[1,16,128]{2,1,0:T(8,128)S(1)} %get-tuple-element.39), channel_id=1, source_target_pairs={{0,32},{32,64},{64,96},{96,128},{128,160},{160,192},{192,224},{1,3... | collective-permute-start | bytes 24584 | tf_op jit(solution)/shard_map/ppermute | solution.py:665
  19.6 0.0 copy-done.4
  19.6 0.0 copy-done.5
  19.6 0.0 copy-done.6
  19.6 1.8 %codes.1 = s32[64]{0:T(128)S(1)} custom-call(s32[6,1,32]{2,1,0:T(1,128)S(1)} %bitcast.18, s32[6,1,32]{2,1,0:T(1,128)S(1)} %bitcast.20, s32[2,1,32]{2,1,0:T(1,128)S(1)} %bitcast.22), custom_call_target="tpu_custom_call" | custom-call | flops 2000000 | bytes 2000000 | tf_op jit(solution)/shard_map/codes/pallas_call | solution.py:624
  21.4 0.0 copy-done
  21.4 0.0 copy-start.3
  21.4 0.4 prepare_fine.1
  21.8 0.0 copy-done.1
  21.8 0.3 copy-done.3
  22.2 0.4 prepare_coarse.1
  22.6 0.0 collective-permute-done.1.from_high
  22.6 0.0 collective-permute-done.from_low
  22.6 9.4 %all-to-all-done.received = f32[32,32,128]{2,1,0:T(8,128)S(1)} async-done(((f32[32,32,128]{2,1,0:T(8,128)}), f32[32,32,128]{2,1,0:T(8,128)S(1)}, u32[]{:S(2)}, u32[]{:S(2)}) %all-to-all-start) | async-done | bytes 524320 | tf_op jit(solution)/shard_map/all_to_all | solution.py:642
  32.0 1.6 %middle.1 = (f32[32,24,128]{2,1,0:T(8,128)S(1)}, f32[19,16,256]{2,1,0:T(8,128)S(1)}, f32[19,16,256]{2,1,0:T(8,128)S(1)}, f32[19,16,256]{2,1,0:T(8,128)S(1)}) custom-call(f32[32,32,128]{2,1,0:T(8,128)S(1)} %all-to-all-done.received, f32[1,16,128]{2,1,0:T(8,128)S(1)} %collective-permute-done.from_low, f32[1,16,128]{2,1,0:T(8,128)S(1)} %collective-permute-done.1.from_high, ...), custom_call_target="tpu_custom_call" | custom-call | flops 2000000 | bytes 2000000 | tf_op jit(solution)/shard_map/middle/pallas_call | solution.py:624
  33.6 19.3 %all_to_all.15.received = f32[32,24,128]{2,1,0:T(8,128)S(1)} all-to-all(f32[32,24,128]{2,1,0:T(8,128)S(1)} %get-tuple-element.26), channel_id=1, replica_groups=mesh['group'=8,'dev'=32] {'dev'}, dimensions={0} | all-to-all | bytes 786432 | tf_op jit(solution)/shard_map/all_to_all | solution.py:642
  52.9 1.7 %last.1 = (f32[32,16,128]{2,1,0:T(8,128)}, f32[19,16,256]{2,1,0:T(8,128)S(1)}) custom-call(f32[32,24,128]{2,1,0:T(8,128)S(1)} %all_to_all.15.received, f32[19,16,256]{2,1,0:T(8,128)S(1)} %get-tuple-element.27.f_post, f32[19,16,256]{2,1,0:T(8,128)S(1)} %get-tuple-element.28.f_start, f32[19,16,256]{2,1,0:T(8,128)S(1)} %get-tuple-element.25.f_weights, s32[64]{0:T(128)S(1)} %codes.1), custom_call_target="tpu_custom_call" | custom-call | flops 2000000 | bytes 2000000 | tf_op jit(solution)/shard_map/last/pallas_call | solution.py:624
  54.6 5.1 %all-to-all-start.2 = ((f32[32,16,128]{2,1,0:T(8,128)}), f32[32,16,128]{2,1,0:T(8,128)S(1)}, u32[]{:S(2)}, u32[]{:S(2)}) async-start(f32[32,16,128]{2,1,0:T(8,128)} %get-tuple-element.32), calls=%async_computation.2 | async-start | bytes 524288 | tf_op jit(solution)/shard_map/all_to_all | solution.py:642
  59.8 1.3 %finish.1 = (f32[19,32,128]{2,1,0:T(8,128)}, f32[19,16,256]{2,1,0:T(8,128)S(1)}) custom-call(f32[19,16,256]{2,1,0:T(8,128)S(1)} %get-tuple-element.29.state, f32[19,16,256]{2,1,0:T(8,128)S(1)} %get-tuple-element.30.coarse_new, s32[64]{0:T(128)S(1)} %codes.1), custom_call_target="tpu_custom_call" | custom-call | flops 2000000 | bytes 2000000 | tf_op jit(solution)/shard_map/finish/pallas_call | solution.py:624
  61.1 9.8 %all-to-all-done.2.received = f32[32,16,128]{2,1,0:T(8,128)S(1)} async-done(((f32[32,16,128]{2,1,0:T(8,128)}), f32[32,16,128]{2,1,0:T(8,128)S(1)}, u32[]{:S(2)}, u32[]{:S(2)}) %all-to-all-start.2) | async-done | bytes 262176 | tf_op jit(solution)/shard_map/all_to_all | solution.py:642
  70.9 1.4 %coarse.1 = f32[19,32,128]{2,1,0:T(8,128)} custom-call(f32[32,16,128]{2,1,0:T(8,128)S(1)} %all-to-all-done.2.received, f32[19,16,256]{2,1,0:T(8,128)S(1)} %get-tuple-element.33.base, s32[64]{0:T(128)S(1)} %codes.1), custom_call_target="tpu_custom_call" | custom-call | flops 2000000 | bytes 2000000 | tf_op jit(solution)/shard_map/coarse/pallas_call | solution.py:624
  (2 shorter events, 0.0 us)
Async XLA Ops:
  3.6 11.6 %copy-start.7 = (f32[2,16,128]{2,1,0:T(8,128)S(1)}, f32[2,16,128]{2,1,0:T(8,128)}, u32[]{:S(2)}) copy-start(f32[2,16,128]{2,1,0:T(8,128)} %get-tuple-element.19) | copy-start | bytes 49156
  3.6 16.0 %copy-start.4 = (s32[1,32,6]{1,0,2:T(1,128)S(1)}, s32[1,32,6]{1,0,2:T(1,128)}, u32[]{:S(2)}) copy-start(s32[1,32,6]{1,0,2:T(1,128)} %param.12) | copy-start | bytes 2308
  3.6 16.0 %copy-start.5 = (s32[1,32,6]{1,0,2:T(1,128)S(1)}, s32[1,32,6]{1,0,2:T(1,128)}, u32[]{:S(2)}) copy-start(s32[1,32,6]{1,0,2:T(1,128)} %param.11) | copy-start | bytes 2308
  3.6 16.0 %copy-start.6 = (s32[1,32,2]{1,2,0:T(2,128)S(1)}, s32[1,32,2]{1,2,0:T(2,128)}, u32[]{:S(2)}) copy-start(s32[1,32,2]{1,2,0:T(2,128)} %param.13) | copy-start | bytes 772
  3.6 17.8 %copy-start = (f32[1,19,4096]{2,0,1:T(1,128)S(1)}, f32[1,19,4096]{2,0,1:T(1,128)}, u32[]{:S(2)}) copy-start(f32[1,19,4096]{2,0,1:T(1,128)} %param.7) | copy-start | bytes 933892
  3.6 17.8 %copy-start.2 = (s32[1,4096]{1,0:T(1,128)S(1)}, s32[1,4096]{1,0:T(1,128)}, u32[]{:S(2)}) copy-start(s32[1,4096]{1,0:T(1,128)} %param.9) | copy-start | bytes 49156
  3.6 28.3 %all-to-all-start = ((f32[32,32,128]{2,1,0:T(8,128)}), f32[32,32,128]{2,1,0:T(8,128)S(1)}, u32[]{:S(2)}, u32[]{:S(2)}) async-start(f32[32,32,128]{2,1,0:T(8,128)} %get-tuple-element.18), calls=%async_computation | async-start | bytes 1048576 | tf_op jit(solution)/shard_map/all_to_all | solution.py:642
  15.1 6.7 %copy-start.1 = (f32[1,19,4096]{2,0,1:T(1,128)S(1)}, f32[1,19,4096]{2,0,1:T(1,128)}, u32[]{:S(2)}) copy-start(f32[1,19,4096]{2,0,1:T(1,128)} %param.8) | copy-start | bytes 933892
  15.1 7.4 %collective-permute-start.1 = (f32[1,16,128]{2,1,0:T(8,128)S(1)}, f32[1,16,128]{2,1,0:T(8,128)S(1)}, u32[]{:S(2)}, u32[]{:S(2)}) collective-permute-start(f32[1,16,128]{2,1,0:T(8,128)S(1)} %get-tuple-element.38), channel_id=1, source_target_pairs={{32,0},{64,32},{96,64},{128,96},{160,128},{192,160},{224,192},{33,... | collective-permute-start | bytes 24584 | tf_op jit(solution)/shard_map/ppermute | solution.py:666
  17.2 5.4 %collective-permute-start = (f32[1,16,128]{2,1,0:T(8,128)S(1)}, f32[1,16,128]{2,1,0:T(8,128)S(1)}, u32[]{:S(2)}, u32[]{:S(2)}) collective-permute-start(f32[1,16,128]{2,1,0:T(8,128)S(1)} %get-tuple-element.39), channel_id=1, source_target_pairs={{0,32},{32,64},{64,96},{96,128},{128,160},{160,192},{192,224},{1,3... | collective-permute-start | bytes 24584 | tf_op jit(solution)/shard_map/ppermute | solution.py:665
  21.4 0.7 copy-start.3
  54.6 16.3 %all-to-all-start.2 = ((f32[32,16,128]{2,1,0:T(8,128)}), f32[32,16,128]{2,1,0:T(8,128)S(1)}, u32[]{:S(2)}, u32[]{:S(2)}) async-start(f32[32,16,128]{2,1,0:T(8,128)} %get-tuple-element.32), calls=%async_computation.2 | async-start | bytes 524288 | tf_op jit(solution)/shard_map/all_to_all | solution.py:642

commit v4 on v3

--- a/solution.py
+++ b/solution.py
@@ -38,7 +38,7 @@
 FIELD = (19, 16, 256)
 CELL_ROWS = (19, 32, 128)
 SLOT1 = 32
-SLOT2 = 24
+SLOT2 = (32, 5, 4, 128)
 SLOT3 = 16
 FINE_LINKS, COARSE_LINKS, PARENT, CHILDREN, OCTANTS, CODES = 0, 8, 16, 24, 32, 64
 COARSE_PARTS = ((0, 7), (7, 6), (13, 6))
@@ -190,6 +190,54 @@
     return out
 
 
+def join_rows(upper, lower):
+    return jnp.concatenate([upper, lower], axis=0)
+
+
+def shell_places(lane):
+    entry = lane - jnp.where(lane < 120, 96, 120)
+    along_z = (1 + (entry >> 2)) * 16 + 8 * ((entry >> 1) & 1) + 7 * (entry & 1)
+    part = lane & 31
+    return jnp.where(lane < 96, part + 96 * (part >> 4), along_z)
+
+
+def pack_thin_shell(pair):
+    lane = iota((8, 128), 1)
+    sub = iota((8, 128), 0)
+    a, b = pair
+    index = shell_places(lane) & 127
+    first = (lane < 64) | ((lane >= 96) & (lane < 120))
+    inside = jnp.where(first, pick(a, index, 1), pick(b, index, 1))
+    entry = 8 + (lane & 15)
+    rest = pick(b, (1 + (entry >> 2)) * 16 + 8 * ((entry >> 1) & 1) + 7 * (entry & 1), 1)
+    block = ((lane >> 4) - 2) & 3
+    rest = pick(rest, jnp.where(sub == 0, 1, 4) + block, 0)
+    shared = jnp.where((sub == 0) | (sub == 7), rest, inside)
+    rows = jnp.concatenate([a[0:1], a[7:8], b[0:1], b[7:8]], axis=0)
+    return shared, rows
+
+
+def unpack_thin_shell(shared, rows):
+    lane = iota((8, 128), 1)
+    sub = iota((8, 128), 0)
+    rows = join_rows(rows, rows)
+    edge = (lane & 15) + jnp.where(lane >= 112, 16, 0)
+    z = lane & 15
+    entry = 4 * ((lane >> 4) - 1) + 2 * (z >> 3) + jnp.where((z & 7) == 7, 1, 0)
+    on_y = (lane < 16) | (lane >= 112)
+    block = sub - jnp.where(sub > 3, 4, 1)
+    moved = pick(pick(shared, jnp.where(sub <= 3, 0, 7), 0), (24 + 16 * block + entry) & 127, 1)
+    out = []
+    for k in range(2):
+        start = 96 if k == 0 else 120
+        tile_k = pick(shared, jnp.where(on_y, 32 + 32 * k + edge, start + entry) & 127, 1)
+        if k == 1:
+            tile_k = jnp.where(on_y | (entry < 8), tile_k, moved)
+        line = pick(rows, 2 * k + jnp.where(sub == 7, 1, 0), 0)
+        out.append(jnp.where((sub == 0) | (sub == 7), line, tile_k))
+    return out
+
+
 def pack_shell(pair):
     lane = iota((8, 128), 1)
     sub = iota((8, 128), 0)
@@ -283,33 +331,68 @@
     return out
 
 
-def below(first, second):
+def packed_lines(first, second):
+    lane = iota((8, 128), 1)
+
+    def at_x(k, half, inner):
+        base = 0 if k < 2 else 96
+        return pick(first, base + ((lane >> 5) & 1) * 16 + inner, 1)
+
+    def row_of(k, half, side):
+        return 2 * half + (lane >> 6) + 4 * side
+
+    def at_y(k, side, inner):
+        rest, base = (first, 32) if k < 2 else (second, 64)
+        return pick(rest, base + 16 * side + inner, 1)
+
+    def at_z(k, y, side):
+        rest, base = (first, 64) if k < 2 else (second, 96)
+        return pick(rest, base + 4 * y + 2 * (k % 2) + side, 1)
+
+    return at_x, row_of, at_y, at_z
+
+
+def tile_lines(tiles):
+    lane = iota((8, 128), 1)
+
+    def at_x(k, half, inner):
+        return pick(tiles[k // 2], (4 * half + (lane >> 5)) * 16 + inner, 1)
+
+    def row_of(k, half, side):
+        return jnp.full((8, 128), 7 * side, jnp.int32)
+
+    def at_y(k, side, inner):
+        return pick(tiles[k // 2], 112 * side + inner, 1)
+
+    def at_z(k, y, side):
+        return pick(tiles[k // 2], 16 * y + 8 * (k % 2) + 7 * side, 1)
+
+    return at_x, row_of, at_y, at_z
+
+
+def below(lines):
+    at_x, row_of, at_y, at_z = lines
     lane = iota((8, 128), 1)
     sub = iota((8, 128), 0)
     z = lane & 15
     fields = [[], [], []]
     for k in range(4):
-        other = k % 2
-        inner = (z >> 1) + 8 * other
-        base = 0 if k < 2 else 96
+        inner = (z >> 1) + 8 * (k % 2)
         tiles = [[None, None], [None, None]]
         for half in range(2):
-            rows = pick(first, base + ((lane >> 5) & 1) * 16 + inner, 1)
+            rows = at_x(k, half, inner)
             for row in range(2):
-                tiles[row][half] = pick(rows, 2 * half + (lane >> 6) + 4 * (1 - row), 0)
+                tiles[row][half] = pick(rows, row_of(k, half, 1 - row), 0)
         fields[0].append(join(tiles))
-        rest, base = (first, 32) if k < 2 else (second, 64)
         for half in range(2):
-            line = pick(rest, base + 16 * (1 - half) + inner, 1)
+            line = at_y(k, 1 - half, inner)
             for row in range(2):
                 tiles[row][half] = pick(line, 4 * row + (sub >> 1), 0)
         fields[1].append(join(tiles))
-        base += 32
         for half in range(2):
             y = 8 * half + (lane >> 4)
-            far = 4 * (((y + 1) & 15) >> 1)
-            near = 4 * (((y + 15) & 15) >> 1) + 1
-            line = pick(rest, base + 2 * other + jnp.where(z == 15, far, near), 1)
+            far = z == 15
+            line = at_z(k, ((y + jnp.where(far, 1, 15)) & 15) >> 1, jnp.where(far, 0, 1))
             for row in range(2):
                 tiles[row][half] = pick(line, 4 * row + (sub >> 1), 0)
         fields[2].append(join(tiles))
@@ -367,11 +450,11 @@
         octs[o, 8:16, :] = second
 
 
-def give_octants(octs, octant, out, at, shared):
+def give_octants(octs, parents, out):
     for d in range(32):
-        o = octant(d)
-        out[d, at : at + 8, :] = octs[o, 0:8, :]
-        out[d, shared : shared + 8, 64:128] = octs[o, 8:16, 64:128]
+        o = parents[1, 0, d]
+        out[d, 24:32, :] = octs[o, 0:8, :]
+        out[d, 16:24, 64:128] = octs[o, 8:16, 64:128]
 
 
 def give_face(post, face, code, me, out, at, shared, lanes):
@@ -383,8 +466,8 @@
 
 
 def send_kernel(
-    coarse_in, fine_in, coarse_table, fine_table, parent_table, out, region,
-    coarse, fine, coarse_links, fine_links, parents, slots, octs, sems,
+    coarse_in, fine_in, coarse_table, fine_table, parent_table, out, region_out,
+    coarse, fine, coarse_links, fine_links, parents, slots, region, octs, sems,
 ):
     fetch = [
         pltpu.make_async_copy(source, target, sems.at[i])
@@ -418,8 +501,10 @@
             region[face - 2, 0:8, :] = first
             region[face - 2, 8:16, :] = second
     put(0).start()
+    beside = pltpu.make_async_copy(region, region_out, sems.at[9])
+    beside.start()
     fetch[4].wait()
-    give_octants(octs, lambda d: parents[1, 0, d], slots, 24, 16)
+    give_octants(octs, parents, slots)
     put(3).start()
     fetch[2].wait()
     fetch[3].wait()
@@ -430,6 +515,7 @@
     put(2).start()
     for part in range(4):
         put(part).wait()
+    beside.wait()
 
 
 def prepare_kernel(state, depth, post, start, weights, *, omega):
@@ -471,21 +557,11 @@
     return ghosts
 
 
-def fine_ghosts(received, codes, plane_at, shared, moment_at):
-    parent = codes[PARENT]
-    under = below(
-        received[parent, moment_at : moment_at + 8, :], received[parent, shared : shared + 8, :]
-    )
-
+def fine_ghosts(codes, plane_of, lanes, under):
     def take(face):
         code = codes[FINE_LINKS + face]
-        slot = jnp.maximum(code, 0)
-        plane = unpack_face(
-            received[slot, plane_at : plane_at + 8, :],
-            received[slot, shared : shared + 8, :],
-            32,
-            face,
-        )
+        first, second = plane_of(jnp.maximum(code, 0))
+        plane = unpack_face(first, second, lanes, face)
         return {q: jnp.where(code >= 0, plane[q], under[face // 2][q]) for q in plane}
 
     return merge_ghosts(take)
@@ -517,8 +593,16 @@
     old_density, old_u = moments([c_start[q] for q in range(19)])
     density, u = moments(new)
     mid = [0.5 * (old_density + density)] + [0.5 * (a + b) for a, b in zip(old_u, u)]
-    store_octants(mid, octs)
-    ghosts = fine_ghosts(received, codes, 8, 16, 24)
+    for o, pair in pack_octants(mid).items():
+        shared, rows = pack_thin_shell(pair)
+        octs[o, 0] = shared[0:4]
+        octs[o, 1] = shared[4:8]
+        octs[o, 2] = rows
+    parent = codes[PARENT]
+    under = below(packed_lines(received[parent, 24:32, :], received[parent, 16:24, :]))
+    ghosts = fine_ghosts(
+        codes, lambda d: (received[d, 8:16, :], received[d, 16:24, :]), 32, under
+    )
     new = stream(lambda q: f_post[q], lambda q: f_start[q], lambda q: f_weights[q], ghosts)
     for q in range(19):
         state[q] = new[q]
@@ -526,17 +610,31 @@
     for q in range(19):
         post[q] = after[q]
     for face in range(6):
-        give_face(after, face, codes[FINE_LINKS + face], me, out, 0, 8, 32)
-    give_octants(octs, lambda d: codes[OCTANTS + d], out, 16, 8)
+        first, second = pack_face(after, face)
+        code = codes[FINE_LINKS + face]
+        slot = jnp.where(code >= 0, code, me)
+        for part in range(2):
+            out[slot, part] = first[4 * part : 4 * part + 4]
+            out[slot, 2 + part, :, 0:32] = second[4 * part : 4 * part + 4, 0:32]
+    for d in range(32):
+        o = codes[OCTANTS + d]
+        out[d, 2, :, 32:128] = octs[o, 0, :, 32:128]
+        out[d, 3, :, 32:128] = octs[o, 1, :, 32:128]
+        out[d, 4] = octs[o, 2]
 
 
 def last_kernel(received, f_post, f_start, f_weights, codes, out, state, slot, sem):
-    ghosts = fine_ghosts(received, codes, 0, 8, 16)
+    def rows_of(d, part):
+        return join_rows(received[d, part], received[d, part + 1])
+
+    parent = codes[PARENT]
+    under = below(tile_lines(unpack_thin_shell(rows_of(parent, 2), received[parent, 4])))
+    ghosts = fine_ghosts(codes, lambda d: (rows_of(d, 0), rows_of(d, 2)), 0, under)
     new = stream(lambda q: f_post[q], lambda q: f_start[q], lambda q: f_weights[q], ghosts)
     first, second = restrict(new)
     slot[0:8, :] = first
     slot[8:16, :] = second
-    copy = pltpu.make_async_copy(slot, out.at[codes[PARENT]], sem)
+    copy = pltpu.make_async_copy(slot, out.at[parent], sem)
     copy.start()
     for q in range(19):
         state[q] = new[q]
@@ -609,8 +707,9 @@
     LINKS,
     pltpu.SMEM((2, 1, 32), jnp.int32),
     pltpu.VMEM((32, SLOT1, 128), F32),
+    pltpu.VMEM((2, 16, 128), F32),
     OCTS,
-    pltpu.SemaphoreType.DMA((9,)),
+    pltpu.SemaphoreType.DMA((10,)),
 ]
 LAST_SCRATCH = [pltpu.VMEM((SLOT3, 128), F32), pltpu.SemaphoreType.DMA]
 COARSE_SCRATCH = [pltpu.VMEM(CELL_ROWS, F32), pltpu.SemaphoreType.DMA((len(COARSE_PARTS),))]
@@ -654,7 +753,7 @@
         [(32, SLOT1, 128), (2, 16, 128)],
         [coarse_state, fine_state, coarse_links, fine_links, parents],
         hbm=(0, 1, 2, 3, 4),
-        hbm_outs=(0,),
+        hbm_outs=(0, 1),
         scratch=SEND_SCRATCH,
         vmem=MOST_VMEM,
         name="send",
@@ -678,13 +777,13 @@
     )
     sent, coarse_new, state, post = call(
         middle_kernel,
-        [(32, SLOT2, 128), FIELD, FIELD, FIELD],
+        [SLOT2, FIELD, FIELD, FIELD],
         [
             received, from_low, from_high, c_post, c_start, c_weights, f_post, f_start, f_weights,
             codes,
         ],
         smem=(9,),
-        scratch=[OCTS],
+        scratch=[pltpu.VMEM((8, 3, 4, 128), F32)],
         name="middle",
     )
     received = swap(sent)

time: 72.8 us -> 71.3 us (0.979)
  blocking collectives: 19.3 us -> 18.1 us
    all_to_all x1, blocking collectives: 19.3 us -> 18.1 us  [swap(): return lax.all_to_all(value, 'dev', split_axis=0, concat_axis=0, tiled=True)]
where the time goes in v4:
time: 71.3 us; the launch traced here: 70.8 us
  starting transfers between devices  20.8 us (29%)
  waiting for transfers between devices  19.7 us (28%)
  blocking collectives  18.1 us (25%)
  Pallas kernels  10.9 us (15%)
  between operations  0.85 us (1%)
    all_to_all x2, waiting for transfers between devices, swap(): return lax.all_to_all(value, 'dev', split_axis=0, concat_axis=0, tiled=True)  19.7 us
    all_to_all x1, blocking collectives, swap(): return lax.all_to_all(value, 'dev', split_axis=0, concat_axis=0, tiled=True)  18.1 us
    all_to_all x2, starting transfers between devices, swap(): return lax.all_to_all(value, 'dev', split_axis=0, concat_axis=0, tiled=True)  16.4 us
    pallas_call x8, Pallas kernels, call(): pl.pallas_call(kernel, out_shape=[jax.ShapeDtypeStruct((s,), jnp.int32) i...  10.9 us
    ppermute x1, starting transfers between devices, body(): from_low = lax.ppermute(region[1:2], 'group', up)  2.41 us
    ppermute x1, starting transfers between devices, body(): from_high = lax.ppermute(region[0:1], 'group', down)  2.05 us
  transfers between devices with their start and end apart: 4, of which 2 were waited for; matrix products, arithmetic and copies ran while one was open for 0% of the time, Pallas kernels for 5%

profile of v4, /device:TPU:16, one launch (start us, length us, event | category | flops | bytes accessed | tf_op | source)
XLA Modules:
  0.0 70.8 jit_solution(11704707785863777562)
XLA Ops:
  0.6 2.3 %send.1 = (f32[32,32,128]{2,1,0:T(8,128)}, f32[2,16,128]{2,1,0:T(8,128)}) custom-call(f32[19,32,128]{2,1,0:T(8,128)} %bitcast.13, f32[19,32,128]{2,1,0:T(8,128)} %bitcast.11, s32[6,1,32]{2,1,0:T(1,128)} %bitcast.17, s32[6,1,32]{2,1,0:T(1,128)} %bitcast.19, s32[2,1,32]{2,1,0:T(1,128)} %bitcast.21), custom_call_target="tpu_custom_call" | custom-call | flops 2000000 | bytes 2000000 | tf_op jit(solution)/shard_map/send/pallas_call | solution.py:723
  2.9 0.0 copy-start.7
  3.0 0.0 copy-start.4
  3.0 0.0 copy-start.5
  3.0 0.0 copy-start.6
  3.0 0.0 copy-start
  3.0 0.0 copy-start.2
  3.0 11.5 %all-to-all-start = ((f32[32,32,128]{2,1,0:T(8,128)}), f32[32,32,128]{2,1,0:T(8,128)S(1)}, u32[]{:S(2)}, u32[]{:S(2)}) async-start(f32[32,32,128]{2,1,0:T(8,128)} %get-tuple-element.18), calls=%async_computation | async-start | bytes 1048576 | tf_op jit(solution)/shard_map/all_to_all | solution.py:741
  14.5 0.0 copy-start.1
  14.5 0.0 copy-done.7
  14.5 2.1 %collective-permute-start.1 = (f32[1,16,128]{2,1,0:T(8,128)S(1)}, f32[1,16,128]{2,1,0:T(8,128)S(1)}, u32[]{:S(2)}, u32[]{:S(2)}) collective-permute-start(f32[1,16,128]{2,1,0:T(8,128)S(1)} %get-tuple-element.38), channel_id=1, source_target_pairs={{32,0},{64,32},{96,64},{128,96},{160,128},{192,160},{224,192},{33,... | collective-permute-start | bytes 24584 | tf_op jit(solution)/shard_map/ppermute | solution.py:765
  16.6 2.4 %collective-permute-start = (f32[1,16,128]{2,1,0:T(8,128)S(1)}, f32[1,16,128]{2,1,0:T(8,128)S(1)}, u32[]{:S(2)}, u32[]{:S(2)}) collective-permute-start(f32[1,16,128]{2,1,0:T(8,128)S(1)} %get-tuple-element.39), channel_id=1, source_target_pairs={{0,32},{32,64},{64,96},{96,128},{128,160},{160,192},{192,224},{1,3... | collective-permute-start | bytes 24584 | tf_op jit(solution)/shard_map/ppermute | solution.py:764
  19.0 0.0 copy-done.4
  19.0 0.0 copy-done.5
  19.0 0.0 copy-done.6
  19.0 1.8 %codes.1 = s32[64]{0:T(128)S(1)} custom-call(s32[6,1,32]{2,1,0:T(1,128)S(1)} %bitcast.18, s32[6,1,32]{2,1,0:T(1,128)S(1)} %bitcast.20, s32[2,1,32]{2,1,0:T(1,128)S(1)} %bitcast.22), custom_call_target="tpu_custom_call" | custom-call | flops 2000000 | bytes 2000000 | tf_op jit(solution)/shard_map/codes/pallas_call | solution.py:723
  20.8 0.0 copy-done
  20.8 0.0 copy-done.2
  20.8 0.0 copy-start.3
  20.8 0.4 prepare_fine.1
  21.2 0.3 copy-done.3
  21.5 0.4 prepare_coarse.1
  21.9 0.0 collective-permute-done.1.from_high
  21.9 0.0 collective-permute-done.from_low
  22.0 9.4 %all-to-all-done.received = f32[32,32,128]{2,1,0:T(8,128)S(1)} async-done(((f32[32,32,128]{2,1,0:T(8,128)}), f32[32,32,128]{2,1,0:T(8,128)S(1)}, u32[]{:S(2)}, u32[]{:S(2)}) %all-to-all-start) | async-done | bytes 524320 | tf_op jit(solution)/shard_map/all_to_all | solution.py:741
  31.4 1.6 %middle.1 = (f32[32,5,4,128]{3,2,1,0:T(4,128)S(1)}, f32[19,16,256]{2,1,0:T(8,128)S(1)}, f32[19,16,256]{2,1,0:T(8,128)S(1)}, f32[19,16,256]{2,1,0:T(8,128)S(1)}) custom-call(f32[32,32,128]{2,1,0:T(8,128)S(1)} %all-to-all-done.received, f32[1,16,128]{2,1,0:T(8,128)S(1)} %collective-permute-done.from_low, f32[1,16,128]{2,1,0:T(8,128)S(1)} %collective-permute-done.1.from_high, ...), custom_call_target="tpu_custom_call" | custom-call | flops 2000000 | bytes 2000000 | tf_op jit(solution)/shard_map/middle/pallas_call | solution.py:723
  33.0 18.1 %all_to_all.15.received = f32[32,5,4,128]{3,2,1,0:T(4,128)S(1)} all-to-all(f32[32,5,4,128]{3,2,1,0:T(4,128)S(1)} %get-tuple-element.26), channel_id=1, replica_groups=mesh['group'=8,'dev'=32] {'dev'}, dimensions={0} | all-to-all | bytes 655360 | tf_op jit(solution)/shard_map/all_to_all | solution.py:741
  51.1 1.7 %last.1 = (f32[32,16,128]{2,1,0:T(8,128)}, f32[19,16,256]{2,1,0:T(8,128)S(1)}) custom-call(f32[32,5,4,128]{3,2,1,0:T(4,128)S(1)} %all_to_all.15.received, f32[19,16,256]{2,1,0:T(8,128)S(1)} %get-tuple-element.27.f_post, f32[19,16,256]{2,1,0:T(8,128)S(1)} %get-tuple-element.28.f_start, f32[19,16,256]{2,1,0:T(8,128)S(1)} %get-tuple-element.25.f_weights, ...), custom_call_target="tpu_custom_call" | custom-call | flops 2000000 | bytes 2000000 | tf_op jit(solution)/shard_map/last/pallas_call | solution.py:723
  52.8 4.9 %all-to-all-start.2 = ((f32[32,16,128]{2,1,0:T(8,128)}), f32[32,16,128]{2,1,0:T(8,128)S(1)}, u32[]{:S(2)}, u32[]{:S(2)}) async-start(f32[32,16,128]{2,1,0:T(8,128)} %get-tuple-element.32), calls=%async_computation.2 | async-start | bytes 524288 | tf_op jit(solution)/shard_map/all_to_all | solution.py:741
  57.7 1.3 %finish.1 = (f32[19,32,128]{2,1,0:T(8,128)}, f32[19,16,256]{2,1,0:T(8,128)S(1)}) custom-call(f32[19,16,256]{2,1,0:T(8,128)S(1)} %get-tuple-element.29.state, f32[19,16,256]{2,1,0:T(8,128)S(1)} %get-tuple-element.30.coarse_new, s32[64]{0:T(128)S(1)} %codes.1), custom_call_target="tpu_custom_call" | custom-call | flops 2000000 | bytes 2000000 | tf_op jit(solution)/shard_map/finish/pallas_call | solution.py:723
  59.0 10.3 %all-to-all-done.2.received = f32[32,16,128]{2,1,0:T(8,128)S(1)} async-done(((f32[32,16,128]{2,1,0:T(8,128)}), f32[32,16,128]{2,1,0:T(8,128)S(1)}, u32[]{:S(2)}, u32[]{:S(2)}) %all-to-all-start.2) | async-done | bytes 262176 | tf_op jit(solution)/shard_map/all_to_all | solution.py:741
  69.4 1.4 %coarse.1 = f32[19,32,128]{2,1,0:T(8,128)} custom-call(f32[32,16,128]{2,1,0:T(8,128)S(1)} %all-to-all-done.2.received, f32[19,16,256]{2,1,0:T(8,128)S(1)} %get-tuple-element.33.base, s32[64]{0:T(128)S(1)} %codes.1), custom_call_target="tpu_custom_call" | custom-call | flops 2000000 | bytes 2000000 | tf_op jit(solution)/shard_map/coarse/pallas_call | solution.py:723
  (2 shorter events, 0.0 us)
Async XLA Ops:
  2.9 11.6 %copy-start.7 = (f32[2,16,128]{2,1,0:T(8,128)S(1)}, f32[2,16,128]{2,1,0:T(8,128)}, u32[]{:S(2)}) copy-start(f32[2,16,128]{2,1,0:T(8,128)} %get-tuple-element.19) | copy-start | bytes 49156
  3.0 16.0 %copy-start.4 = (s32[1,32,6]{1,0,2:T(1,128)S(1)}, s32[1,32,6]{1,0,2:T(1,128)}, u32[]{:S(2)}) copy-start(s32[1,32,6]{1,0,2:T(1,128)} %param.12) | copy-start | bytes 2308
  3.0 16.0 %copy-start.5 = (s32[1,32,6]{1,0,2:T(1,128)S(1)}, s32[1,32,6]{1,0,2:T(1,128)}, u32[]{:S(2)}) copy-start(s32[1,32,6]{1,0,2:T(1,128)} %param.11) | copy-start | bytes 2308
  3.0 16.0 %copy-start.6 = (s32[1,32,2]{1,2,0:T(2,128)S(1)}, s32[1,32,2]{1,2,0:T(2,128)}, u32[]{:S(2)}) copy-start(s32[1,32,2]{1,2,0:T(2,128)} %param.13) | copy-start | bytes 772
  3.0 17.8 %copy-start = (f32[1,19,4096]{2,0,1:T(1,128)S(1)}, f32[1,19,4096]{2,0,1:T(1,128)}, u32[]{:S(2)}) copy-start(f32[1,19,4096]{2,0,1:T(1,128)} %param.7) | copy-start | bytes 933892
  3.0 17.8 %copy-start.2 = (s32[1,4096]{1,0:T(1,128)S(1)}, s32[1,4096]{1,0:T(1,128)}, u32[]{:S(2)}) copy-start(s32[1,4096]{1,0:T(1,128)} %param.9) | copy-start | bytes 49156
  3.0 28.3 %all-to-all-start = ((f32[32,32,128]{2,1,0:T(8,128)}), f32[32,32,128]{2,1,0:T(8,128)S(1)}, u32[]{:S(2)}, u32[]{:S(2)}) async-start(f32[32,32,128]{2,1,0:T(8,128)} %get-tuple-element.18), calls=%async_computation | async-start | bytes 1048576 | tf_op jit(solution)/shard_map/all_to_all | solution.py:741
  14.5 6.7 %copy-start.1 = (f32[1,19,4096]{2,0,1:T(1,128)S(1)}, f32[1,19,4096]{2,0,1:T(1,128)}, u32[]{:S(2)}) copy-start(f32[1,19,4096]{2,0,1:T(1,128)} %param.8) | copy-start | bytes 933892
  14.5 7.4 %collective-permute-start.1 = (f32[1,16,128]{2,1,0:T(8,128)S(1)}, f32[1,16,128]{2,1,0:T(8,128)S(1)}, u32[]{:S(2)}, u32[]{:S(2)}) collective-permute-start(f32[1,16,128]{2,1,0:T(8,128)S(1)} %get-tuple-element.38), channel_id=1, source_target_pairs={{32,0},{64,32},{96,64},{128,96},{160,128},{192,160},{224,192},{33,... | collective-permute-start | bytes 24584 | tf_op jit(solution)/shard_map/ppermute | solution.py:765
  16.6 5.4 %collective-permute-start = (f32[1,16,128]{2,1,0:T(8,128)S(1)}, f32[1,16,128]{2,1,0:T(8,128)S(1)}, u32[]{:S(2)}, u32[]{:S(2)}) collective-permute-start(f32[1,16,128]{2,1,0:T(8,128)S(1)} %get-tuple-element.39), channel_id=1, source_target_pairs={{0,32},{32,64},{64,96},{96,128},{128,160},{160,192},{192,224},{1,3... | collective-permute-start | bytes 24584 | tf_op jit(solution)/shard_map/ppermute | solution.py:764
  20.8 0.7 %copy-start.3 = (s32[1,4096]{1,0:T(1,128)S(1)}, s32[1,4096]{1,0:T(1,128)}, u32[]{:S(2)}) copy-start(s32[1,4096]{1,0:T(1,128)} %param.10) | copy-start | bytes 49156
  52.8 16.5 %all-to-all-start.2 = ((f32[32,16,128]{2,1,0:T(8,128)}), f32[32,16,128]{2,1,0:T(8,128)S(1)}, u32[]{:S(2)}, u32[]{:S(2)}) async-start(f32[32,16,128]{2,1,0:T(8,128)} %get-tuple-element.32), calls=%async_computation.2 | async-start | bytes 524288 | tf_op jit(solution)/shard_map/all_to_all | solution.py:741

commit v5 on v4

--- a/solution.py
+++ b/solution.py
@@ -41,7 +41,6 @@
 SLOT2 = (32, 5, 4, 128)
 SLOT3 = 16
 FINE_LINKS, COARSE_LINKS, PARENT, CHILDREN, OCTANTS, CODES = 0, 8, 16, 24, 32, 64
-COARSE_PARTS = ((0, 7), (7, 6), (13, 6))
 
 
 def inflow_value(q):
@@ -623,7 +622,7 @@
         out[d, 4] = octs[o, 2]
 
 
-def last_kernel(received, f_post, f_start, f_weights, codes, out, state, slot, sem):
+def last_kernel(received, f_post, f_start, f_weights, codes, out, state):
     def rows_of(d, part):
         return join_rows(received[d, part], received[d, part + 1])
 
@@ -631,25 +630,11 @@
     under = below(tile_lines(unpack_thin_shell(rows_of(parent, 2), received[parent, 4])))
     ghosts = fine_ghosts(codes, lambda d: (rows_of(d, 0), rows_of(d, 2)), 0, under)
     new = stream(lambda q: f_post[q], lambda q: f_start[q], lambda q: f_weights[q], ghosts)
-    first, second = restrict(new)
-    slot[0:8, :] = first
-    slot[8:16, :] = second
-    copy = pltpu.make_async_copy(slot, out.at[parent], sem)
-    copy.start()
     for q in range(19):
         state[q] = new[q]
-    copy.wait()
-
-
-def finish_kernel(state, coarse_new, codes, fine_out, base):
-    for q in range(19):
-        store_cells(fine_out, q, state[q])
-    covered = cover(codes)
-    new = load(coarse_new)
-    density, u = moments(new)
-    own = equilibrium(density, u, range(19))
-    for q in range(19):
-        base[q] = jnp.where(covered, new[q] - own[q], new[q])
+    first, second = restrict(new)
+    out[parent, 0:8, :] = first
+    out[parent, 8:16, :] = second
 
 
 def cover(codes):
@@ -662,7 +647,11 @@
     return join(tiles) >= 0
 
 
-def coarse_kernel(received, base, codes, coarse_out, cells, sems):
+def final_kernel(received, state, coarse_new, codes, fine_out, coarse_out, f_cells, c_cells, sems):
+    for q in range(19):
+        store_cells(f_cells, q, state[q])
+    fine_copy = pltpu.make_async_copy(f_cells, fine_out, sems.at[0])
+    fine_copy.start()
     low = (iota((8, 128), 1) & 15) < 8
     tiles = [[[None, None], [None, None]] for _ in range(4)]
     for ox in range(2):
@@ -680,15 +669,15 @@
     density = jnp.where(covered, density, 1.0)
     inverse = 1.0 / density
     fine_eq = equilibrium(density, [jx * inverse, jy * inverse, jz * inverse], range(19))
-    copies = []
-    for i, (low_q, count) in enumerate(COARSE_PARTS):
-        for q in range(low_q, low_q + count):
-            store_cells(cells, q, base[q] + jnp.where(covered, fine_eq[q], 0.0))
-        part = pl.ds(low_q, count)
-        copies.append(pltpu.make_async_copy(cells.at[part], coarse_out.at[part], sems.at[i]))
-        copies[-1].start()
-    for copy in copies:
-        copy.wait()
+    new = load(coarse_new)
+    own_density, own_u = moments(new)
+    own_eq = equilibrium(own_density, own_u, range(19))
+    for q in range(19):
+        store_cells(c_cells, q, new[q] + jnp.where(covered, fine_eq[q] - own_eq[q], 0.0))
+    coarse_copy = pltpu.make_async_copy(c_cells, coarse_out, sems.at[1])
+    coarse_copy.start()
+    fine_copy.wait()
+    coarse_copy.wait()
 
 
 VMEM = pl.BlockSpec(memory_space=pltpu.VMEM)
@@ -711,8 +700,11 @@
     OCTS,
     pltpu.SemaphoreType.DMA((10,)),
 ]
-LAST_SCRATCH = [pltpu.VMEM((SLOT3, 128), F32), pltpu.SemaphoreType.DMA]
-COARSE_SCRATCH = [pltpu.VMEM(CELL_ROWS, F32), pltpu.SemaphoreType.DMA((len(COARSE_PARTS),))]
+FINAL_SCRATCH = [
+    pltpu.VMEM(CELL_ROWS, F32),
+    pltpu.VMEM(CELL_ROWS, F32),
+    pltpu.SemaphoreType.DMA((2,)),
+]
 
 
 def call(kernel, outs, ins, smem=(), hbm=(), hbm_outs=(), scratch=(), vmem=SOME_VMEM, name=None):
@@ -792,26 +784,17 @@
         [(32, SLOT3, 128), FIELD],
         [received, post, state, f_weights, codes],
         smem=(4,),
-        hbm_outs=(0,),
-        scratch=LAST_SCRATCH,
         name="last",
     )
     received = swap(sent)
-    fine_out, base = call(
-        finish_kernel,
-        [CELL_ROWS, FIELD],
-        [state, coarse_new, codes],
-        smem=(2,),
-        name="finish",
-    )
-    (coarse_out,) = call(
-        coarse_kernel,
-        [CELL_ROWS],
-        [received, base, codes],
-        smem=(2,),
-        hbm_outs=(0,),
-        scratch=COARSE_SCRATCH,
-        name="coarse",
+    fine_out, coarse_out = call(
+        final_kernel,
+        [CELL_ROWS, CELL_ROWS],
+        [received, state, coarse_new, codes],
+        smem=(3,),
+        hbm_outs=(0, 1),
+        scratch=FINAL_SCRATCH,
+        name="final",
     )
     return fine_out.reshape(1, 19, 4096), coarse_out.reshape(1, 19, 4096)
 

time: 71.3 us -> 70.5 us (0.989)
  blocking collectives: 18.1 us -> 34.4 us
  waiting for transfers between devices: 19.7 us -> 9.41 us
  starting transfers between devices: 20.8 us -> 15.9 us
  Pallas kernels: 10.9 us -> 9.1 us
    all_to_all x1 -> x2, blocking collectives: 18.1 us -> 34.4 us  [swap(): return lax.all_to_all(value, 'dev', split_axis=0, concat_axis=0, tiled=True)]
    all_to_all x2 -> x1, waiting for transfers between devices: 19.7 us -> 9.4 us  [swap(): return lax.all_to_all(value, 'dev', split_axis=0, concat_axis=0, tiled=True)]
    all_to_all x2 -> x1, starting transfers between devices: 16.4 us -> 11.5 us  [swap(): return lax.all_to_all(value, 'dev', split_axis=0, concat_axis=0, tiled=True)]
    pallas_call x8 -> x7, Pallas kernels: 10.9 us -> 9.1 us  [call(): pl.pallas_call(kernel, out_shape=[jax.ShapeDtypeStruct((s,), jnp.int32) i...]
  transfers between devices with their start and end apart: 4 -> 3, of which waited for: 2 -> 1; matrix products, arithmetic and copies ran while one was open for 0% -> 0% of each run, Pallas kernels for 5% -> 4%
where the time goes in v5:
time: 70.5 us; the launch traced here: 70.1 us
  blocking collectives  34.4 us (49%)
  starting transfers between devices  15.9 us (23%)
  waiting for transfers between devices  9.41 us (13%)
  Pallas kernels  9.1 us (13%)
  between operations  0.84 us (1%)
    all_to_all x2, blocking collectives, swap(): return lax.all_to_all(value, 'dev', split_axis=0, concat_axis=0, tiled=True)  34.4 us
    all_to_all x1, starting transfers between devices, swap(): return lax.all_to_all(value, 'dev', split_axis=0, concat_axis=0, tiled=True)  11.5 us
    all_to_all x1, waiting for transfers between devices, swap(): return lax.all_to_all(value, 'dev', split_axis=0, concat_axis=0, tiled=True)  9.4 us
    pallas_call x7, Pallas kernels, call(): pl.pallas_call(kernel, out_shape=[jax.ShapeDtypeStruct((s,), jnp.int32) i...  9.1 us
    ppermute x1, starting transfers between devices, body(): from_low = lax.ppermute(region[1:2], 'group', up)  2.41 us
    ppermute x1, starting transfers between devices, body(): from_high = lax.ppermute(region[0:1], 'group', down)  2.05 us
  transfers between devices with their start and end apart: 3, of which 1 were waited for; matrix products, arithmetic and copies ran while one was open for 0% of the time, Pallas kernels for 4%

profile of v5, /device:TPU:16, one launch (start us, length us, event | category | flops | bytes accessed | tf_op | source)
XLA Modules:
  0.0 70.1 jit_solution(1986126693338053580)
XLA Ops:
  0.6 2.3 %send.1 = (f32[32,32,128]{2,1,0:T(8,128)}, f32[2,16,128]{2,1,0:T(8,128)}) custom-call(f32[19,32,128]{2,1,0:T(8,128)} %bitcast.13, f32[19,32,128]{2,1,0:T(8,128)} %bitcast.11, s32[6,1,32]{2,1,0:T(1,128)} %bitcast.17, s32[6,1,32]{2,1,0:T(1,128)} %bitcast.19, s32[2,1,32]{2,1,0:T(1,128)} %bitcast.21), custom_call_target="tpu_custom_call" | custom-call | flops 2000000 | bytes 2000000 | tf_op jit(solution)/shard_map/send/pallas_call | solution.py:715
  3.0 0.0 copy-start.7
  3.0 0.0 copy-start.4
  3.0 0.0 copy-start.5
  3.0 0.0 copy-start.6
  3.0 0.0 copy-start
  3.0 0.0 copy-start.2
  3.0 11.5 %all-to-all-start = ((f32[32,32,128]{2,1,0:T(8,128)}), f32[32,32,128]{2,1,0:T(8,128)S(1)}, u32[]{:S(2)}, u32[]{:S(2)}) async-start(f32[32,32,128]{2,1,0:T(8,128)} %get-tuple-element.18), calls=%async_computation | async-start | bytes 1048576 | tf_op jit(solution)/shard_map/all_to_all | solution.py:733
  14.5 0.0 copy-start.1
  14.5 0.0 copy-done.7
  14.5 2.1 %collective-permute-start.1 = (f32[1,16,128]{2,1,0:T(8,128)S(1)}, f32[1,16,128]{2,1,0:T(8,128)S(1)}, u32[]{:S(2)}, u32[]{:S(2)}) collective-permute-start(f32[1,16,128]{2,1,0:T(8,128)S(1)} %get-tuple-element.38), channel_id=1, source_target_pairs={{32,0},{64,32},{96,64},{128,96},{160,128},{192,160},{224,192},{33,... | collective-permute-start | bytes 24584 | tf_op jit(solution)/shard_map/ppermute | solution.py:757
  16.6 2.4 %collective-permute-start = (f32[1,16,128]{2,1,0:T(8,128)S(1)}, f32[1,16,128]{2,1,0:T(8,128)S(1)}, u32[]{:S(2)}, u32[]{:S(2)}) collective-permute-start(f32[1,16,128]{2,1,0:T(8,128)S(1)} %get-tuple-element.39), channel_id=1, source_target_pairs={{0,32},{32,64},{64,96},{96,128},{128,160},{160,192},{192,224},{1,3... | collective-permute-start | bytes 24584 | tf_op jit(solution)/shard_map/ppermute | solution.py:756
  19.0 0.0 copy-done.4
  19.0 0.0 copy-done.5
  19.0 0.0 copy-done.6
  19.0 1.8 %codes.1 = s32[64]{0:T(128)S(1)} custom-call(s32[6,1,32]{2,1,0:T(1,128)S(1)} %bitcast.18, s32[6,1,32]{2,1,0:T(1,128)S(1)} %bitcast.20, s32[2,1,32]{2,1,0:T(1,128)S(1)} %bitcast.22), custom_call_target="tpu_custom_call" | custom-call | flops 2000000 | bytes 2000000 | tf_op jit(solution)/shard_map/codes/pallas_call | solution.py:715
  20.8 0.0 copy-done
  20.8 0.0 copy-done.2
  20.8 0.0 copy-start.3
  20.8 0.4 prepare_fine.1
  21.2 0.0 copy-done.1
  21.2 0.3 copy-done.3
  21.5 0.4 prepare_coarse.1
  21.9 0.0 collective-permute-done.1.from_high
  21.9 0.0 collective-permute-done.from_low
  22.0 9.4 %all-to-all-done.received = f32[32,32,128]{2,1,0:T(8,128)S(1)} async-done(((f32[32,32,128]{2,1,0:T(8,128)}), f32[32,32,128]{2,1,0:T(8,128)S(1)}, u32[]{:S(2)}, u32[]{:S(2)}) %all-to-all-start) | async-done | bytes 524320 | tf_op jit(solution)/shard_map/all_to_all | solution.py:733
  31.4 1.6 %middle.1 = (f32[32,5,4,128]{3,2,1,0:T(4,128)S(1)}, f32[19,16,256]{2,1,0:T(8,128)S(1)}, f32[19,16,256]{2,1,0:T(8,128)S(1)}, f32[19,16,256]{2,1,0:T(8,128)S(1)}) custom-call(f32[32,32,128]{2,1,0:T(8,128)S(1)} %all-to-all-done.received, f32[1,16,128]{2,1,0:T(8,128)S(1)} %collective-permute-done.from_low, f32[1,16,128]{2,1,0:T(8,128)S(1)} %collective-permute-done.1.from_high, ...), custom_call_target="tpu_custom_call" | custom-call | flops 2000000 | bytes 2000000 | tf_op jit(solution)/shard_map/middle/pallas_call | solution.py:715
  33.0 18.1 %all_to_all.15.received = f32[32,5,4,128]{3,2,1,0:T(4,128)S(1)} all-to-all(f32[32,5,4,128]{3,2,1,0:T(4,128)S(1)} %get-tuple-element.26), channel_id=1, replica_groups=mesh['group'=8,'dev'=32] {'dev'}, dimensions={0} | all-to-all | bytes 655360 | tf_op jit(solution)/shard_map/all_to_all | solution.py:733
  51.1 1.1 %last.1 = (f32[32,16,128]{2,1,0:T(8,128)S(1)}, f32[19,16,256]{2,1,0:T(8,128)S(1)}) custom-call(f32[32,5,4,128]{3,2,1,0:T(4,128)S(1)} %all_to_all.15.received, f32[19,16,256]{2,1,0:T(8,128)S(1)} %get-tuple-element.27.f_post, f32[19,16,256]{2,1,0:T(8,128)S(1)} %get-tuple-element.28.f_start, f32[19,16,256]{2,1,0:T(8,128)S(1)} %get-tuple-element.25.f_weights, ...), custom_call_target="tpu_custom_call" | custom-call | flops 2000000 | bytes 2000000 | tf_op jit(solution)/shard_map/last/pallas_call | solution.py:715
  52.2 16.3 %all_to_all.16.received = f32[32,16,128]{2,1,0:T(8,128)S(1)} all-to-all(f32[32,16,128]{2,1,0:T(8,128)S(1)} %get-tuple-element.29), channel_id=1, replica_groups=mesh['group'=8,'dev'=32] {'dev'}, dimensions={0} | all-to-all | bytes 524288 | tf_op jit(solution)/shard_map/all_to_all | solution.py:733
  68.5 1.5 %final.1 = (f32[19,32,128]{2,1,0:T(8,128)}, f32[19,32,128]{2,1,0:T(8,128)}) custom-call(f32[32,16,128]{2,1,0:T(8,128)S(1)} %all_to_all.16.received, f32[19,16,256]{2,1,0:T(8,128)S(1)} %get-tuple-element.30.state, f32[19,16,256]{2,1,0:T(8,128)S(1)} %get-tuple-element.31.coarse_new, s32[64]{0:T(128)S(1)} %codes.1), custom_call_target="tpu_custom_call" | custom-call | flops 2000000 | bytes 2000000 | tf_op jit(solution)/shard_map/final/pallas_call | solution.py:715
  (1 shorter events, 0.0 us)
Async XLA Ops:
  3.0 11.6 %copy-start.7 = (f32[2,16,128]{2,1,0:T(8,128)S(1)}, f32[2,16,128]{2,1,0:T(8,128)}, u32[]{:S(2)}) copy-start(f32[2,16,128]{2,1,0:T(8,128)} %get-tuple-element.19) | copy-start | bytes 49156
  3.0 16.0 %copy-start.4 = (s32[1,32,6]{1,0,2:T(1,128)S(1)}, s32[1,32,6]{1,0,2:T(1,128)}, u32[]{:S(2)}) copy-start(s32[1,32,6]{1,0,2:T(1,128)} %param.12) | copy-start | bytes 2308
  3.0 16.0 %copy-start.5 = (s32[1,32,6]{1,0,2:T(1,128)S(1)}, s32[1,32,6]{1,0,2:T(1,128)}, u32[]{:S(2)}) copy-start(s32[1,32,6]{1,0,2:T(1,128)} %param.11) | copy-start | bytes 2308
  3.0 16.0 %copy-start.6 = (s32[1,32,2]{1,2,0:T(2,128)S(1)}, s32[1,32,2]{1,2,0:T(2,128)}, u32[]{:S(2)}) copy-start(s32[1,32,2]{1,2,0:T(2,128)} %param.13) | copy-start | bytes 772
  3.0 17.8 %copy-start = (f32[1,19,4096]{2,0,1:T(1,128)S(1)}, f32[1,19,4096]{2,0,1:T(1,128)}, u32[]{:S(2)}) copy-start(f32[1,19,4096]{2,0,1:T(1,128)} %param.7) | copy-start | bytes 933892
  3.0 17.8 %copy-start.2 = (s32[1,4096]{1,0:T(1,128)S(1)}, s32[1,4096]{1,0:T(1,128)}, u32[]{:S(2)}) copy-start(s32[1,4096]{1,0:T(1,128)} %param.9) | copy-start | bytes 49156
  3.0 28.3 %all-to-all-start = ((f32[32,32,128]{2,1,0:T(8,128)}), f32[32,32,128]{2,1,0:T(8,128)S(1)}, u32[]{:S(2)}, u32[]{:S(2)}) async-start(f32[32,32,128]{2,1,0:T(8,128)} %get-tuple-element.18), calls=%async_computation | async-start | bytes 1048576 | tf_op jit(solution)/shard_map/all_to_all | solution.py:733
  14.5 6.7 %copy-start.1 = (f32[1,19,4096]{2,0,1:T(1,128)S(1)}, f32[1,19,4096]{2,0,1:T(1,128)}, u32[]{:S(2)}) copy-start(f32[1,19,4096]{2,0,1:T(1,128)} %param.8) | copy-start | bytes 933892
  14.5 7.4 %collective-permute-start.1 = (f32[1,16,128]{2,1,0:T(8,128)S(1)}, f32[1,16,128]{2,1,0:T(8,128)S(1)}, u32[]{:S(2)}, u32[]{:S(2)}) collective-permute-start(f32[1,16,128]{2,1,0:T(8,128)S(1)} %get-tuple-element.38), channel_id=1, source_target_pairs={{32,0},{64,32},{96,64},{128,96},{160,128},{192,160},{224,192},{33,... | collective-permute-start | bytes 24584 | tf_op jit(solution)/shard_map/ppermute | solution.py:757
  16.6 5.4 %collective-permute-start = (f32[1,16,128]{2,1,0:T(8,128)S(1)}, f32[1,16,128]{2,1,0:T(8,128)S(1)}, u32[]{:S(2)}, u32[]{:S(2)}) collective-permute-start(f32[1,16,128]{2,1,0:T(8,128)S(1)} %get-tuple-element.39), channel_id=1, source_target_pairs={{0,32},{32,64},{64,96},{96,128},{128,160},{160,192},{192,224},{1,3... | collective-permute-start | bytes 24584 | tf_op jit(solution)/shard_map/ppermute | solution.py:756
  20.8 0.7 %copy-start.3 = (s32[1,4096]{1,0:T(1,128)S(1)}, s32[1,4096]{1,0:T(1,128)}, u32[]{:S(2)}) copy-start(s32[1,4096]{1,0:T(1,128)} %param.10) | copy-start | bytes 49156

commit v6 on v5

--- a/solution.py
+++ b/solution.py
@@ -40,7 +40,7 @@
 SLOT1 = 32
 SLOT2 = (32, 5, 4, 128)
 SLOT3 = 16
-FINE_LINKS, COARSE_LINKS, PARENT, CHILDREN, OCTANTS, CODES = 0, 8, 16, 24, 32, 64
+FINE_LINKS, COARSE_LINKS, PARENT, CHILDREN, OCTANTS = (0, 0), (0, 1), (6, 0), (0, 2), (7, 32)
 
 
 def inflow_value(q):
@@ -530,23 +530,39 @@
 
 def codes_kernel(coarse_links, fine_links, parents, codes):
     me = lax.axis_index("dev")
+    lane = iota((1, 32), 1)
+    place = [iota((8, 128), 0), iota((8, 128), 1)]
+    owner, octant = parents[0], parents[1]
+
+    def own(line):
+        return jnp.sum(jnp.where(lane == me, line, 0), axis=1, keepdims=True)
+
+    values = {}
     for face in range(6):
-        codes[FINE_LINKS + face] = fine_links[face, 0, me]
-        codes[COARSE_LINKS + face] = coarse_links[face, 0, me]
-    codes[PARENT] = parents[0, 0, me]
+        values[FINE_LINKS[0] + face, FINE_LINKS[1]] = own(fine_links[face])
+        values[COARSE_LINKS[0] + face, COARSE_LINKS[1]] = own(coarse_links[face])
+    values[PARENT] = own(owner)
     for o in range(8):
-        codes[CHILDREN + o] = -1
-
-    def note(d, carry):
-        codes[OCTANTS + d] = parents[1, 0, d]
-
-        @pl.when(parents[0, 0, d] == me)
-        def _():
-            codes[CHILDREN + parents[1, 0, d]] = d
-
-        return carry
-
-    lax.fori_loop(0, 32, note, 0)
+        child = jnp.where((owner == me) & (octant == o), lane, -1)
+        values[CHILDREN[0] + o, CHILDREN[1]] = jnp.max(child, axis=1, keepdims=True)
+    tile_of = jnp.zeros((8, 128), jnp.int32)
+    for (row, at), value in values.items():
+        tile_of = jnp.where((place[0] == row) & (place[1] == at), value, tile_of)
+    codes[...] = tile_of
+    row, at = OCTANTS
+    codes[row : row + 1, at : at + 32] = octant
+
+
+class Codes:
+    def __init__(self, ref):
+        self.tile = ref[...]
+        self.seen = {}
+
+    def __call__(self, start, step=0):
+        row, at = (start[0], start[1] + step) if start == OCTANTS else (start[0] + step, start[1])
+        if (row, at) not in self.seen:
+            self.seen[row, at] = self.tile[row, at]
+        return self.seen[row, at]
 
 
 def merge_ghosts(take):
@@ -558,7 +574,7 @@
 
 def fine_ghosts(codes, plane_of, lanes, under):
     def take(face):
-        code = codes[FINE_LINKS + face]
+        code = codes(FINE_LINKS, face)
         first, second = plane_of(jnp.maximum(code, 0))
         plane = unpack_face(first, second, lanes, face)
         return {q: jnp.where(code >= 0, plane[q], under[face // 2][q]) for q in plane}
@@ -568,12 +584,13 @@
 
 def middle_kernel(
     received, from_low, from_high, c_post, c_start, c_weights, f_post, f_start, f_weights,
-    codes, out, coarse_new, state, post, octs,
+    table, out, coarse_new, state, post, octs,
 ):
     me = lax.axis_index("dev")
+    codes = Codes(table)
 
     def coarse_ghost(face):
-        code = codes[COARSE_LINKS + face]
+        code = codes(COARSE_LINKS, face)
         slot = jnp.maximum(code, 0)
         first = received[slot, 0:8, :]
         second = received[slot, 16:24, :]
@@ -597,7 +614,7 @@
         octs[o, 0] = shared[0:4]
         octs[o, 1] = shared[4:8]
         octs[o, 2] = rows
-    parent = codes[PARENT]
+    parent = codes(PARENT)
     under = below(packed_lines(received[parent, 24:32, :], received[parent, 16:24, :]))
     ghosts = fine_ghosts(
         codes, lambda d: (received[d, 8:16, :], received[d, 16:24, :]), 32, under
@@ -610,23 +627,24 @@
         post[q] = after[q]
     for face in range(6):
         first, second = pack_face(after, face)
-        code = codes[FINE_LINKS + face]
+        code = codes(FINE_LINKS, face)
         slot = jnp.where(code >= 0, code, me)
         for part in range(2):
             out[slot, part] = first[4 * part : 4 * part + 4]
             out[slot, 2 + part, :, 0:32] = second[4 * part : 4 * part + 4, 0:32]
     for d in range(32):
-        o = codes[OCTANTS + d]
+        o = codes(OCTANTS, d)
         out[d, 2, :, 32:128] = octs[o, 0, :, 32:128]
         out[d, 3, :, 32:128] = octs[o, 1, :, 32:128]
         out[d, 4] = octs[o, 2]
 
 
-def last_kernel(received, f_post, f_start, f_weights, codes, out, state):
+def last_kernel(received, f_post, f_start, f_weights, table, out, state):
+    codes = Codes(table)
     def rows_of(d, part):
         return join_rows(received[d, part], received[d, part + 1])
 
-    parent = codes[PARENT]
+    parent = codes(PARENT)
     under = below(tile_lines(unpack_thin_shell(rows_of(parent, 2), received[parent, 4])))
     ghosts = fine_ghosts(codes, lambda d: (rows_of(d, 0), rows_of(d, 2)), 0, under)
     new = stream(lambda q: f_post[q], lambda q: f_start[q], lambda q: f_weights[q], ghosts)
@@ -643,11 +661,12 @@
     for ox in range(2):
         for oy in range(2):
             o = 4 * ox + 2 * oy
-            tiles[ox][oy] = jnp.where(low, codes[CHILDREN + o], codes[CHILDREN + o + 1])
+            tiles[ox][oy] = jnp.where(low, codes(CHILDREN, o), codes(CHILDREN, o + 1))
     return join(tiles) >= 0
 
 
-def final_kernel(received, state, coarse_new, codes, fine_out, coarse_out, f_cells, c_cells, sems):
+def final_kernel(received, state, coarse_new, table, fine_out, coarse_out, f_cells, c_cells, sems):
+    codes = Codes(table)
     for q in range(19):
         store_cells(f_cells, q, state[q])
     fine_copy = pltpu.make_async_copy(f_cells, fine_out, sems.at[0])
@@ -657,8 +676,8 @@
     for ox in range(2):
         for oy in range(2):
             o = 4 * ox + 2 * oy
-            near = jnp.maximum(codes[CHILDREN + o], 0)
-            far = jnp.maximum(codes[CHILDREN + o + 1], 0)
+            near = jnp.maximum(codes(CHILDREN, o), 0)
+            far = jnp.maximum(codes(CHILDREN, o + 1), 0)
             for k in range(2):
                 a = received[near, 8 * k : 8 * k + 8, :]
                 b = received[far, 8 * k : 8 * k + 8, :]
@@ -681,7 +700,6 @@
 
 
 VMEM = pl.BlockSpec(memory_space=pltpu.VMEM)
-SMEM = pl.BlockSpec(memory_space=pltpu.SMEM)
 HBM = pl.BlockSpec(memory_space=pltpu.HBM)
 SOME_VMEM = 24 * 1024 * 1024
 MOST_VMEM = 60 * 1024 * 1024
@@ -707,19 +725,12 @@
 ]
 
 
-def call(kernel, outs, ins, smem=(), hbm=(), hbm_outs=(), scratch=(), vmem=SOME_VMEM, name=None):
-    def space(i, scalars, far):
-        return SMEM if scalars else HBM if i in far else VMEM
-
-    ints = [not isinstance(s, tuple) for s in outs]
+def call(kernel, outs, ins, hbm=(), hbm_outs=(), scratch=(), vmem=SOME_VMEM, name=None):
     return pl.pallas_call(
         kernel,
-        out_shape=[
-            jax.ShapeDtypeStruct((s,), jnp.int32) if i else jax.ShapeDtypeStruct(s, F32)
-            for s, i in zip(outs, ints)
-        ],
-        in_specs=[space(i, i in smem, hbm) for i in range(len(ins))],
-        out_specs=[space(i, scalars, hbm_outs) for i, scalars in enumerate(ints)],
+        out_shape=[jax.ShapeDtypeStruct(s, F32) for s in outs],
+        in_specs=[HBM if i in hbm else VMEM for i in range(len(ins))],
+        out_specs=[HBM if i in hbm_outs else VMEM for i in range(len(outs))],
         scratch_shapes=list(scratch),
         compiler_params=pltpu.CompilerParams(vmem_limit_bytes=vmem),
         cost_estimate=pl.CostEstimate(
@@ -764,9 +775,14 @@
 
     c_post, c_start, c_weights = prepare(coarse_state, coarse_depth, OMEGA_COARSE, "prepare_coarse")
     f_post, f_start, f_weights = prepare(fine_state, fine_depth, OMEGA_FINE, "prepare_fine")
-    (codes,) = call(
-        codes_kernel, [CODES], [coarse_links, fine_links, parents], smem=(0, 1, 2), name="codes"
-    )
+    codes = pl.pallas_call(
+        codes_kernel,
+        out_shape=jax.ShapeDtypeStruct((8, 128), jnp.int32),
+        in_specs=[VMEM] * 3,
+        out_specs=VMEM,
+        compiler_params=pltpu.CompilerParams(vmem_limit_bytes=SOME_VMEM),
+        name="codes",
+    )(coarse_links, fine_links, parents)
     sent, coarse_new, state, post = call(
         middle_kernel,
         [SLOT2, FIELD, FIELD, FIELD],
@@ -774,7 +790,6 @@
             received, from_low, from_high, c_post, c_start, c_weights, f_post, f_start, f_weights,
             codes,
         ],
-        smem=(9,),
         scratch=[pltpu.VMEM((8, 3, 4, 128), F32)],
         name="middle",
     )
@@ -783,7 +798,6 @@
         last_kernel,
         [(32, SLOT3, 128), FIELD],
         [received, post, state, f_weights, codes],
-        smem=(4,),
         name="last",
     )
     received = swap(sent)
@@ -791,7 +805,6 @@
         final_kernel,
         [CELL_ROWS, CELL_ROWS],
         [received, state, coarse_new, codes],
-        smem=(3,),
         hbm_outs=(0, 1),
         scratch=FINAL_SCRATCH,
         name="final",

time: 70.5 us -> 69.1 us (0.980)
  Pallas kernels: 9.1 us -> 6.14 us
  waiting for transfers between devices: 9.41 us -> 11 us
    pallas_call x7, Pallas kernels: 9.1 us -> 6.14 us  [the longest x6 5.97 us: call(): pl.pallas_call(kernel, out_shape=[jax.ShapeDtypeStruct(s, F32) for s in o...]
    ppermute x1, waiting for transfers between devices: 0.01 us -> 1.2 us  [body(): from_low = lax.ppermute(region[1:2], 'group', up)]
  transfers between devices with their start and end apart: 3 -> 3, of which waited for: 1 -> 2; matrix products, arithmetic and copies ran while one was open for 0% -> 0% of each run, Pallas kernels for 4% -> 1%
where the time goes in v6:
time: 69.1 us; the launch traced here: 68.7 us
  blocking collectives  34.4 us (50%)
  starting transfers between devices  15.9 us (23%)
  waiting for transfers between devices  11 us (16%)
  Pallas kernels  6.14 us (9%)
  between operations  0.84 us (1%)
    all_to_all x2, blocking collectives, swap(): return lax.all_to_all(value, 'dev', split_axis=0, concat_axis=0, tiled=True)  34.4 us
    all_to_all x1, starting transfers between devices, swap(): return lax.all_to_all(value, 'dev', split_axis=0, concat_axis=0, tiled=True)  11.5 us
    all_to_all x1, waiting for transfers between devices, swap(): return lax.all_to_all(value, 'dev', split_axis=0, concat_axis=0, tiled=True)  9.8 us
    pallas_call x6, Pallas kernels, call(): pl.pallas_call(kernel, out_shape=[jax.ShapeDtypeStruct(s, F32) for s in o...  5.97 us
    ppermute x1, starting transfers between devices, body(): from_low = lax.ppermute(region[1:2], 'group', up)  2.41 us
    ppermute x1, starting transfers between devices, body(): from_high = lax.ppermute(region[0:1], 'group', down)  2.05 us
  transfers between devices with their start and end apart: 3, of which 2 were waited for; matrix products, arithmetic and copies ran while one was open for 0% of the time, Pallas kernels for 1%

profile of v6, /device:TPU:16, one launch (start us, length us, event | category | flops | bytes accessed | tf_op | source)
XLA Modules:
  0.0 68.7 jit_solution(8704817360799345693)
XLA Ops:
  0.6 2.3 %send.1 = (f32[32,32,128]{2,1,0:T(8,128)}, f32[2,16,128]{2,1,0:T(8,128)}) custom-call(f32[19,32,128]{2,1,0:T(8,128)} %bitcast.13, f32[19,32,128]{2,1,0:T(8,128)} %bitcast.11, s32[6,1,32]{2,1,0:T(1,128)} %bitcast.17, s32[6,1,32]{2,1,0:T(1,128)} %bitcast.19, s32[2,1,32]{2,1,0:T(1,128)} %bitcast.21), custom_call_target="tpu_custom_call" | custom-call | flops 2000000 | bytes 2000000 | tf_op jit(solution)/shard_map/send/pallas_call | solution.py:729
  3.0 0.0 copy-start.7
  3.0 0.0 copy-start.4
  3.0 0.0 copy-start.5
  3.0 0.0 copy-start.6
  3.0 0.0 copy-start
  3.0 0.0 copy-start.2
  3.0 11.5 %all-to-all-start = ((f32[32,32,128]{2,1,0:T(8,128)}), f32[32,32,128]{2,1,0:T(8,128)S(1)}, u32[]{:S(2)}, u32[]{:S(2)}) async-start(f32[32,32,128]{2,1,0:T(8,128)} %get-tuple-element.18), calls=%async_computation | async-start | bytes 1048576 | tf_op jit(solution)/shard_map/all_to_all | solution.py:744
  14.5 0.0 copy-start.1
  14.5 0.0 copy-done.7
  14.5 2.1 %collective-permute-start.1 = (f32[1,16,128]{2,1,0:T(8,128)S(1)}, f32[1,16,128]{2,1,0:T(8,128)S(1)}, u32[]{:S(2)}, u32[]{:S(2)}) collective-permute-start(f32[1,16,128]{2,1,0:T(8,128)S(1)} %get-tuple-element.38), channel_id=1, source_target_pairs={{32,0},{64,32},{96,64},{128,96},{160,128},{192,160},{224,192},{33,... | collective-permute-start | bytes 24584 | tf_op jit(solution)/shard_map/ppermute | solution.py:768
  16.6 2.4 %collective-permute-start = (f32[1,16,128]{2,1,0:T(8,128)S(1)}, f32[1,16,128]{2,1,0:T(8,128)S(1)}, u32[]{:S(2)}, u32[]{:S(2)}) collective-permute-start(f32[1,16,128]{2,1,0:T(8,128)S(1)} %get-tuple-element.39), channel_id=1, source_target_pairs={{0,32},{32,64},{64,96},{96,128},{128,160},{160,192},{192,224},{1,3... | collective-permute-start | bytes 24584 | tf_op jit(solution)/shard_map/ppermute | solution.py:767
  19.0 0.0 copy-done.4
  19.0 0.0 copy-done.5
  19.0 0.0 copy-done.6
  19.0 0.2 codes.1.table
  19.2 0.0 copy-done
  19.2 0.0 copy-done.2
  19.2 0.0 copy-start.3
  19.2 0.4 prepare_fine.1
  19.6 0.0 copy-done.1
  19.6 0.3 copy-done.3
  20.0 0.4 prepare_coarse.1
  20.3 0.0 collective-permute-done.1.from_high
  20.4 1.2 %collective-permute-done.from_low = f32[1,16,128]{2,1,0:T(8,128)S(1)} collective-permute-done((f32[1,16,128]{2,1,0:T(8,128)S(1)}, f32[1,16,128]{2,1,0:T(8,128)S(1)}, u32[]{:S(2)}, u32[]{:S(2)}) %collective-permute-start) | collective-permute-done | bytes 8224 | tf_op jit(solution)/shard_map/ppermute | solution.py:767
  21.6 9.8 %all-to-all-done.received = f32[32,32,128]{2,1,0:T(8,128)S(1)} async-done(((f32[32,32,128]{2,1,0:T(8,128)}), f32[32,32,128]{2,1,0:T(8,128)S(1)}, u32[]{:S(2)}, u32[]{:S(2)}) %all-to-all-start) | async-done | bytes 524320 | tf_op jit(solution)/shard_map/all_to_all | solution.py:744
  31.4 1.2 %middle.1 = (f32[32,5,4,128]{3,2,1,0:T(4,128)S(1)}, f32[19,16,256]{2,1,0:T(8,128)S(1)}, f32[19,16,256]{2,1,0:T(8,128)S(1)}, f32[19,16,256]{2,1,0:T(8,128)S(1)}) custom-call(f32[32,32,128]{2,1,0:T(8,128)S(1)} %all-to-all-done.received, f32[1,16,128]{2,1,0:T(8,128)S(1)} %collective-permute-done.from_low, f32[1,16,128]{2,1,0:T(8,128)S(1)} %collective-permute-done.1.from_high, ...), custom_call_target="tpu_custom_call" | custom-call | flops 2000000 | bytes 2000000 | tf_op jit(solution)/shard_map/middle/pallas_call | solution.py:729
  32.5 18.1 %all_to_all.15.received = f32[32,5,4,128]{3,2,1,0:T(4,128)S(1)} all-to-all(f32[32,5,4,128]{3,2,1,0:T(4,128)S(1)} %get-tuple-element.26), channel_id=1, replica_groups=mesh['group'=8,'dev'=32] {'dev'}, dimensions={0} | all-to-all | bytes 655360 | tf_op jit(solution)/shard_map/all_to_all | solution.py:744
  50.6 0.6 last.1
  51.3 16.3 %all_to_all.16.received = f32[32,16,128]{2,1,0:T(8,128)S(1)} all-to-all(f32[32,16,128]{2,1,0:T(8,128)S(1)} %get-tuple-element.29), channel_id=1, replica_groups=mesh['group'=8,'dev'=32] {'dev'}, dimensions={0} | all-to-all | bytes 524288 | tf_op jit(solution)/shard_map/all_to_all | solution.py:744
  67.6 1.1 %final.1 = (f32[19,32,128]{2,1,0:T(8,128)}, f32[19,32,128]{2,1,0:T(8,128)}) custom-call(f32[32,16,128]{2,1,0:T(8,128)S(1)} %all_to_all.16.received, f32[19,16,256]{2,1,0:T(8,128)S(1)} %get-tuple-element.30.state, f32[19,16,256]{2,1,0:T(8,128)S(1)} %get-tuple-element.31.coarse_new, s32[8,128]{1,0:T(8,128)S(1)} %codes.1.table), custom_call_target="tpu_custom_call" | custom-call | flops 2000000 | bytes 2000000 | tf_op jit(solution)/shard_map/final/pallas_call | solution.py:729
  (1 shorter events, 0.0 us)
Async XLA Ops:
  3.0 11.6 %copy-start.7 = (f32[2,16,128]{2,1,0:T(8,128)S(1)}, f32[2,16,128]{2,1,0:T(8,128)}, u32[]{:S(2)}) copy-start(f32[2,16,128]{2,1,0:T(8,128)} %get-tuple-element.19) | copy-start | bytes 49156
  3.0 16.0 %copy-start.4 = (s32[1,32,6]{1,0,2:T(1,128)S(1)}, s32[1,32,6]{1,0,2:T(1,128)}, u32[]{:S(2)}) copy-start(s32[1,32,6]{1,0,2:T(1,128)} %param.12) | copy-start | bytes 2308
  3.0 16.0 %copy-start.5 = (s32[1,32,6]{1,0,2:T(1,128)S(1)}, s32[1,32,6]{1,0,2:T(1,128)}, u32[]{:S(2)}) copy-start(s32[1,32,6]{1,0,2:T(1,128)} %param.11) | copy-start | bytes 2308
  3.0 16.0 %copy-start.6 = (s32[1,32,2]{1,2,0:T(2,128)S(1)}, s32[1,32,2]{1,2,0:T(2,128)}, u32[]{:S(2)}) copy-start(s32[1,32,2]{1,2,0:T(2,128)} %param.13) | copy-start | bytes 772
  3.0 16.2 %copy-start = (f32[1,19,4096]{2,0,1:T(1,128)S(1)}, f32[1,19,4096]{2,0,1:T(1,128)}, u32[]{:S(2)}) copy-start(f32[1,19,4096]{2,0,1:T(1,128)} %param.7) | copy-start | bytes 933892
  3.0 16.2 %copy-start.2 = (s32[1,4096]{1,0:T(1,128)S(1)}, s32[1,4096]{1,0:T(1,128)}, u32[]{:S(2)}) copy-start(s32[1,4096]{1,0:T(1,128)} %param.9) | copy-start | bytes 49156
  3.0 28.3 %all-to-all-start = ((f32[32,32,128]{2,1,0:T(8,128)}), f32[32,32,128]{2,1,0:T(8,128)S(1)}, u32[]{:S(2)}, u32[]{:S(2)}) async-start(f32[32,32,128]{2,1,0:T(8,128)} %get-tuple-element.18), calls=%async_computation | async-start | bytes 1048576 | tf_op jit(solution)/shard_map/all_to_all | solution.py:744
  14.5 5.1 %copy-start.1 = (f32[1,19,4096]{2,0,1:T(1,128)S(1)}, f32[1,19,4096]{2,0,1:T(1,128)}, u32[]{:S(2)}) copy-start(f32[1,19,4096]{2,0,1:T(1,128)} %param.8) | copy-start | bytes 933892
  14.5 5.8 %collective-permute-start.1 = (f32[1,16,128]{2,1,0:T(8,128)S(1)}, f32[1,16,128]{2,1,0:T(8,128)S(1)}, u32[]{:S(2)}, u32[]{:S(2)}) collective-permute-start(f32[1,16,128]{2,1,0:T(8,128)S(1)} %get-tuple-element.38), channel_id=1, source_target_pairs={{32,0},{64,32},{96,64},{128,96},{160,128},{192,160},{224,192},{33,... | collective-permute-start | bytes 24584 | tf_op jit(solution)/shard_map/ppermute | solution.py:768
  16.6 5.0 %collective-permute-start = (f32[1,16,128]{2,1,0:T(8,128)S(1)}, f32[1,16,128]{2,1,0:T(8,128)S(1)}, u32[]{:S(2)}, u32[]{:S(2)}) collective-permute-start(f32[1,16,128]{2,1,0:T(8,128)S(1)} %get-tuple-element.39), channel_id=1, source_target_pairs={{0,32},{32,64},{64,96},{96,128},{128,160},{160,192},{192,224},{1,3... | collective-permute-start | bytes 24584 | tf_op jit(solution)/shard_map/ppermute | solution.py:767
  19.2 0.7 %copy-start.3 = (s32[1,4096]{1,0:T(1,128)S(1)}, s32[1,4096]{1,0:T(1,128)}, u32[]{:S(2)}) copy-start(s32[1,4096]{1,0:T(1,128)} %param.10) | copy-start | bytes 49156

commit v7 on v6

--- a/solution.py
+++ b/solution.py
@@ -37,7 +37,7 @@
 F32 = jnp.float32
 FIELD = (19, 16, 256)
 CELL_ROWS = (19, 32, 128)
-SLOT1 = 32
+SLOT1 = (32, 15, 2, 128)
 SLOT2 = (32, 5, 4, 128)
 SLOT3 = 16
 FINE_LINKS, COARSE_LINKS, PARENT, CHILDREN, OCTANTS = (0, 0), (0, 1), (6, 0), (0, 2), (7, 32)
@@ -237,21 +237,46 @@
     return out
 
 
+def z_place(entry):
+    return ((1 + (entry >> 2)) * 16 + 8 * ((entry >> 1) & 1) + 7 * (entry & 1)) & 127
+
+
 def pack_shell(pair):
     lane = iota((8, 128), 1)
     sub = iota((8, 128), 0)
+    a, b = pair
     part = lane & 31
     along_y = part + 96 * (part >> 4)
-    which = part & 3
-    along_z = (part >> 2) * 16 + 8 * (which >> 1) + 7 * (which & 1)
-    segment = lane >> 5
-    a, b = pair
-    rows_a = row_parts(a[0:1, :], a[7:8, :], lane, sub)
-    rows_b = row_parts(b[0:1, :], b[7:8, :], lane, sub)
-    rest = pick(a, jnp.where(segment == 1, along_y, along_z), 1)
-    first = jnp.where(segment == 0, rows_a, jnp.where(segment == 3, rows_b, rest))
-    second = pick(b, jnp.where(segment == 2, along_y, along_z), 1)
-    return first, second
+    inside = jnp.where(lane < 96, pick(a, along_y, 1), pick(b, along_y, 1))
+    sixth = jnp.full((8, 128), 6, jnp.int32)
+    last = [pick(pick(t, z_place(part), 1), sixth, 0) for t in pair]
+    shared = jnp.where(sub == 0, last[0], jnp.where(sub == 7, last[1], inside))
+    rows = jnp.concatenate([a[0:1], a[7:8], b[0:1], b[7:8]], axis=0)
+    block = (lane * 171) >> 12
+    lines = [pick(pick(t, z_place(lane - 24 * block), 1), 1 + block, 0) for t in pair]
+    return shared, rows, jnp.concatenate([lines[0][0:1], lines[1][0:1]], axis=0)
+
+
+def unpack_shell(shared, rows, extra):
+    lane = iota((8, 128), 1)
+    sub = iota((8, 128), 0)
+    rows = join_rows(rows, rows)
+    extra = jnp.concatenate([extra] * 4, axis=0)
+    edge = (lane & 15) + jnp.where(lane >= 112, 16, 0)
+    z = lane & 15
+    entry = 4 * ((lane >> 4) - 1) + 2 * (z >> 3) + jnp.where((z & 7) == 7, 1, 0)
+    on_y = (lane < 16) | (lane >= 112)
+    place = (jnp.where(sub == 6, 64, 24 * (sub - 1)) + entry) & 127
+    out = []
+    for k in range(2):
+        whole = jnp.full((8, 128), k, jnp.int32)
+        source = jnp.where(sub == 6, pick(shared, 7 * whole, 0), pick(extra, whole, 0))
+        along_z = pick(source, place, 1)
+        along_y = pick(shared, 64 + 32 * k + edge, 1)
+        line = pick(rows, 2 * k + jnp.where(sub == 7, 1, 0), 0)
+        tile_k = jnp.where(on_y, along_y, along_z)
+        out.append(jnp.where((sub == 0) | (sub == 7), line, tile_k))
+    return out
 
 
 def shifted(value, v):
@@ -328,27 +353,6 @@
                 jnp.where(low, pltpu.roll(c, 120, 1), d),
             )
     return out
-
-
-def packed_lines(first, second):
-    lane = iota((8, 128), 1)
-
-    def at_x(k, half, inner):
-        base = 0 if k < 2 else 96
-        return pick(first, base + ((lane >> 5) & 1) * 16 + inner, 1)
-
-    def row_of(k, half, side):
-        return 2 * half + (lane >> 6) + 4 * side
-
-    def at_y(k, side, inner):
-        rest, base = (first, 32) if k < 2 else (second, 64)
-        return pick(rest, base + 16 * side + inner, 1)
-
-    def at_z(k, y, side):
-        rest, base = (first, 64) if k < 2 else (second, 96)
-        return pick(rest, base + 4 * y + 2 * (k % 2) + side, 1)
-
-    return at_x, row_of, at_y, at_z
 
 
 def tile_lines(tiles):
@@ -444,24 +448,33 @@
 
 def store_octants(fields, octs):
     for o, pair in pack_octants(fields).items():
-        first, second = pack_shell(pair)
-        octs[o, 0:8, :] = first
-        octs[o, 8:16, :] = second
+        shared, rows, extra = pack_shell(pair)
+        for part in range(4):
+            octs[o, part] = shared[2 * part : 2 * part + 2]
+        for part in range(2):
+            octs[o, 4 + part] = rows[2 * part : 2 * part + 2]
+        octs[o, 6] = extra
 
 
 def give_octants(octs, parents, out):
     for d in range(32):
         o = parents[1, 0, d]
-        out[d, 24:32, :] = octs[o, 0:8, :]
-        out[d, 16:24, 64:128] = octs[o, 8:16, 64:128]
-
-
-def give_face(post, face, code, me, out, at, shared, lanes):
+        out[d, 8:12, :, 64:128] = octs[o, 0:4, :, 64:128]
+        out[d, 12:15] = octs[o, 4:7]
+
+
+def give_face(post, face, code, me, out, at, lanes):
     first, second = pack_face(post, face)
     slot = jnp.where(code >= 0, code, me)
-    out[slot, at : at + 8, :] = first
-    out[slot, shared : shared + 8, lanes : lanes + 32] = second[:, lanes : lanes + 32]
+    for part in range(4):
+        rows = slice(2 * part, 2 * part + 2)
+        out[slot, at + part] = first[rows]
+        out[slot, 8 + part, :, lanes : lanes + 32] = second[rows, lanes : lanes + 32]
     return first, second
+
+
+def rows_of_pairs(ref, slot, at):
+    return jnp.concatenate([ref[slot, at + part] for part in range(4)], axis=0)
 
 
 def send_kernel(
@@ -484,8 +497,8 @@
         copy.start()
 
     def put(part):
-        rows = pl.ds(8 * part, 8)
-        return pltpu.make_async_copy(slots.at[:, rows, :], out.at[:, rows, :], sems.at[5 + part])
+        rows = pl.ds(4 * part, 4 if part < 3 else 3)
+        return pltpu.make_async_copy(slots.at[:, rows], out.at[:, rows], sems.at[5 + part])
 
     me = lax.axis_index("dev")
     fetch[0].wait()
@@ -495,7 +508,7 @@
     store_octants([density] + u, octs)
     post = collide(f, OMEGA_COARSE)
     for face in range(6):
-        first, second = give_face(post, face, coarse_links[face, 0, me], me, slots, 0, 16, 0)
+        first, second = give_face(post, face, coarse_links[face, 0, me], me, slots, 0, 0)
         if face in (2, 3):
             region[face - 2, 0:8, :] = first
             region[face - 2, 8:16, :] = second
@@ -509,7 +522,7 @@
     fetch[3].wait()
     post = collide([load_cells(fine, q) for q in range(19)], OMEGA_FINE)
     for face in range(6):
-        give_face(post, face, fine_links[face, 0, me], me, slots, 8, 16, 32)
+        give_face(post, face, fine_links[face, 0, me], me, slots, 4, 32)
     put(1).start()
     put(2).start()
     for part in range(4):
@@ -592,8 +605,8 @@
     def coarse_ghost(face):
         code = codes(COARSE_LINKS, face)
         slot = jnp.maximum(code, 0)
-        first = received[slot, 0:8, :]
-        second = received[slot, 16:24, :]
+        first = rows_of_pairs(received, slot, 0)
+        second = rows_of_pairs(received, slot, 8)
         if face in (2, 3):
             beside = from_low if face == 2 else from_high
             first = jnp.where(code == -2, beside[0, 0:8, :], first)
@@ -615,9 +628,14 @@
         octs[o, 1] = shared[4:8]
         octs[o, 2] = rows
     parent = codes(PARENT)
-    under = below(packed_lines(received[parent, 24:32, :], received[parent, 16:24, :]))
+    rows = join_rows(received[parent, 12], received[parent, 13])
+    shell = unpack_shell(rows_of_pairs(received, parent, 8), rows, received[parent, 14])
+    under = below(tile_lines(shell))
     ghosts = fine_ghosts(
-        codes, lambda d: (received[d, 8:16, :], received[d, 16:24, :]), 32, under
+        codes,
+        lambda d: (rows_of_pairs(received, d, 4), rows_of_pairs(received, d, 8)),
+        32,
+        under,
     )
     new = stream(lambda q: f_post[q], lambda q: f_start[q], lambda q: f_weights[q], ghosts)
     for q in range(19):
@@ -705,7 +723,7 @@
 MOST_VMEM = 60 * 1024 * 1024
 
 
-OCTS = pltpu.VMEM((8, 16, 128), F32)
+OCTS = pltpu.VMEM((8, 7, 2, 128), F32)
 LINKS = pltpu.SMEM((6, 1, 32), jnp.int32)
 SEND_SCRATCH = [
     pltpu.VMEM(CELL_ROWS, F32),
@@ -713,7 +731,7 @@
     LINKS,
     LINKS,
     pltpu.SMEM((2, 1, 32), jnp.int32),
-    pltpu.VMEM((32, SLOT1, 128), F32),
+    pltpu.VMEM(SLOT1, F32),
     pltpu.VMEM((2, 16, 128), F32),
     OCTS,
     pltpu.SemaphoreType.DMA((10,)),
@@ -753,7 +771,7 @@
     parents = parents.transpose(2, 0, 1)
     sent, region = call(
         send_kernel,
-        [(32, SLOT1, 128), (2, 16, 128)],
+        [SLOT1, (2, 16, 128)],
         [coarse_state, fine_state, coarse_links, fine_links, parents],
         hbm=(0, 1, 2, 3, 4),
         hbm_outs=(0, 1),

time: 69.1 us -> 68.5 us (level)
  waiting for transfers between devices: 11 us -> 10.1 us
    all_to_all x1, waiting for transfers between devices: 9.8 us -> 8.85 us  [swap(): return lax.all_to_all(value, 'dev', split_axis=0, concat_axis=0, tiled=True)]
where the time goes in v7:
time: 68.5 us; the launch traced here: 68.1 us
  blocking collectives  34.6 us (51%)
  starting transfers between devices  15.9 us (23%)
  waiting for transfers between devices  10.1 us (15%)
  Pallas kernels  6.28 us (9%)
  between operations  0.84 us (1%)
    all_to_all x2, blocking collectives, swap(): return lax.all_to_all(value, 'dev', split_axis=0, concat_axis=0, tiled=True)  34.6 us
    all_to_all x1, starting transfers between devices, swap(): return lax.all_to_all(value, 'dev', split_axis=0, concat_axis=0, tiled=True)  11.5 us
    all_to_all x1, waiting for transfers between devices, swap(): return lax.all_to_all(value, 'dev', split_axis=0, concat_axis=0, tiled=True)  8.85 us
    pallas_call x6, Pallas kernels, call(): pl.pallas_call(kernel, out_shape=[jax.ShapeDtypeStruct(s, F32) for s in o...  6.11 us
    ppermute x1, starting transfers between devices, body(): from_low = lax.ppermute(region[1:2], 'group', up)  2.41 us
    ppermute x1, starting transfers between devices, body(): from_high = lax.ppermute(region[0:1], 'group', down)  2.05 us
  transfers between devices with their start and end apart: 3, of which 2 were waited for; matrix products, arithmetic and copies ran while one was open for 0% of the time, Pallas kernels for 1%

profile of v7, /device:TPU:16, one launch (start us, length us, event | category | flops | bytes accessed | tf_op | source)
XLA Modules:
  0.0 68.1 jit_solution(6849411342857888616)
XLA Ops:
  0.6 2.4 %send.1 = (f32[32,15,2,128]{3,2,1,0:T(2,128)}, f32[2,16,128]{2,1,0:T(8,128)}) custom-call(f32[19,32,128]{2,1,0:T(8,128)} %bitcast.13, f32[19,32,128]{2,1,0:T(8,128)} %bitcast.11, s32[6,1,32]{2,1,0:T(1,128)} %bitcast.17, s32[6,1,32]{2,1,0:T(1,128)} %bitcast.19, s32[2,1,32]{2,1,0:T(1,128)} %bitcast.21), custom_call_target="tpu_custom_call" | custom-call | flops 2000000 | bytes 2000000 | tf_op jit(solution)/shard_map/send/pallas_call | solution.py:747
  3.1 0.0 copy-start.7
  3.1 0.0 copy-start.4
  3.1 0.0 copy-start.5
  3.1 0.0 copy-start.6
  3.1 0.0 copy-start
  3.1 0.0 copy-start.2
  3.2 11.5 %all-to-all-start = ((f32[32,15,2,128]{3,2,1,0:T(2,128)}), f32[32,15,2,128]{3,2,1,0:T(2,128)S(1)}, u32[]{:S(2)}, u32[]{:S(2)}) async-start(f32[32,15,2,128]{3,2,1,0:T(2,128)} %get-tuple-element.18), calls=%async_computation | async-start | bytes 983040 | tf_op jit(solution)/shard_map/all_to_all | solution.py:762
  14.6 0.0 copy-start.1
  14.6 0.0 copy-done.7
  14.7 2.1 %collective-permute-start.1 = (f32[1,16,128]{2,1,0:T(8,128)S(1)}, f32[1,16,128]{2,1,0:T(8,128)S(1)}, u32[]{:S(2)}, u32[]{:S(2)}) collective-permute-start(f32[1,16,128]{2,1,0:T(8,128)S(1)} %get-tuple-element.38), channel_id=1, source_target_pairs={{32,0},{64,32},{96,64},{128,96},{160,128},{192,160},{224,192},{33,... | collective-permute-start | bytes 24584 | tf_op jit(solution)/shard_map/ppermute | solution.py:786
  16.7 2.4 %collective-permute-start = (f32[1,16,128]{2,1,0:T(8,128)S(1)}, f32[1,16,128]{2,1,0:T(8,128)S(1)}, u32[]{:S(2)}, u32[]{:S(2)}) collective-permute-start(f32[1,16,128]{2,1,0:T(8,128)S(1)} %get-tuple-element.39), channel_id=1, source_target_pairs={{0,32},{32,64},{64,96},{96,128},{128,160},{160,192},{192,224},{1,3... | collective-permute-start | bytes 24584 | tf_op jit(solution)/shard_map/ppermute | solution.py:785
  19.1 0.0 copy-done.4
  19.1 0.0 copy-done.5
  19.2 0.0 copy-done.6
  19.2 0.2 codes.1.table
  19.3 0.0 copy-done
  19.4 0.0 copy-done.2
  19.4 0.0 copy-start.3
  19.4 0.4 prepare_fine.1
  19.8 0.0 copy-done.1
  19.8 0.3 copy-done.3
  20.1 0.4 prepare_coarse.1
  20.5 0.0 collective-permute-done.1.from_high
  20.5 1.2 %collective-permute-done.from_low = f32[1,16,128]{2,1,0:T(8,128)S(1)} collective-permute-done((f32[1,16,128]{2,1,0:T(8,128)S(1)}, f32[1,16,128]{2,1,0:T(8,128)S(1)}, u32[]{:S(2)}, u32[]{:S(2)}) %collective-permute-start) | collective-permute-done | bytes 8224 | tf_op jit(solution)/shard_map/ppermute | solution.py:785
  21.7 8.8 %all-to-all-done.received = f32[32,15,2,128]{3,2,1,0:T(2,128)S(1)} async-done(((f32[32,15,2,128]{3,2,1,0:T(2,128)}), f32[32,15,2,128]{3,2,1,0:T(2,128)S(1)}, u32[]{:S(2)}, u32[]{:S(2)}) %all-to-all-start) | async-done | bytes 491552 | tf_op jit(solution)/shard_map/all_to_all | solution.py:762
  30.5 1.2 %middle.1 = (f32[32,5,4,128]{3,2,1,0:T(4,128)S(1)}, f32[19,16,256]{2,1,0:T(8,128)S(1)}, f32[19,16,256]{2,1,0:T(8,128)S(1)}, f32[19,16,256]{2,1,0:T(8,128)S(1)}) custom-call(f32[32,15,2,128]{3,2,1,0:T(2,128)S(1)} %all-to-all-done.received, f32[1,16,128]{2,1,0:T(8,128)S(1)} %collective-permute-done.from_low, ...), custom_call_target="tpu_custom_call" | custom-call | flops 2000000 | bytes 2000000 | tf_op jit(solution)/shard_map/middle/pallas_call | solution.py:747
  31.7 18.7 %all_to_all.15.received = f32[32,5,4,128]{3,2,1,0:T(4,128)S(1)} all-to-all(f32[32,5,4,128]{3,2,1,0:T(4,128)S(1)} %get-tuple-element.26), channel_id=1, replica_groups=mesh['group'=8,'dev'=32] {'dev'}, dimensions={0} | all-to-all | bytes 655360 | tf_op jit(solution)/shard_map/all_to_all | solution.py:762
  50.5 0.6 last.1
  51.1 15.9 %all_to_all.16.received = f32[32,16,128]{2,1,0:T(8,128)S(1)} all-to-all(f32[32,16,128]{2,1,0:T(8,128)S(1)} %get-tuple-element.29), channel_id=1, replica_groups=mesh['group'=8,'dev'=32] {'dev'}, dimensions={0} | all-to-all | bytes 524288 | tf_op jit(solution)/shard_map/all_to_all | solution.py:762
  67.0 1.1 %final.1 = (f32[19,32,128]{2,1,0:T(8,128)}, f32[19,32,128]{2,1,0:T(8,128)}) custom-call(f32[32,16,128]{2,1,0:T(8,128)S(1)} %all_to_all.16.received, f32[19,16,256]{2,1,0:T(8,128)S(1)} %get-tuple-element.30.state, f32[19,16,256]{2,1,0:T(8,128)S(1)} %get-tuple-element.31.coarse_new, s32[8,128]{1,0:T(8,128)S(1)} %codes.1.table), custom_call_target="tpu_custom_call" | custom-call | flops 2000000 | bytes 2000000 | tf_op jit(solution)/shard_map/final/pallas_call | solution.py:747
  (1 shorter events, 0.0 us)
Async XLA Ops:
  3.1 11.6 %copy-start.7 = (f32[2,16,128]{2,1,0:T(8,128)S(1)}, f32[2,16,128]{2,1,0:T(8,128)}, u32[]{:S(2)}) copy-start(f32[2,16,128]{2,1,0:T(8,128)} %get-tuple-element.19) | copy-start | bytes 49156
  3.1 16.0 %copy-start.4 = (s32[1,32,6]{1,0,2:T(1,128)S(1)}, s32[1,32,6]{1,0,2:T(1,128)}, u32[]{:S(2)}) copy-start(s32[1,32,6]{1,0,2:T(1,128)} %param.12) | copy-start | bytes 2308
  3.1 16.0 %copy-start.5 = (s32[1,32,6]{1,0,2:T(1,128)S(1)}, s32[1,32,6]{1,0,2:T(1,128)}, u32[]{:S(2)}) copy-start(s32[1,32,6]{1,0,2:T(1,128)} %param.11) | copy-start | bytes 2308
  3.1 16.0 %copy-start.6 = (s32[1,32,2]{1,2,0:T(2,128)S(1)}, s32[1,32,2]{1,2,0:T(2,128)}, u32[]{:S(2)}) copy-start(s32[1,32,2]{1,2,0:T(2,128)} %param.13) | copy-start | bytes 772
  3.1 16.2 %copy-start = (f32[1,19,4096]{2,0,1:T(1,128)S(1)}, f32[1,19,4096]{2,0,1:T(1,128)}, u32[]{:S(2)}) copy-start(f32[1,19,4096]{2,0,1:T(1,128)} %param.7) | copy-start | bytes 933892
  3.1 16.2 %copy-start.2 = (s32[1,4096]{1,0:T(1,128)S(1)}, s32[1,4096]{1,0:T(1,128)}, u32[]{:S(2)}) copy-start(s32[1,4096]{1,0:T(1,128)} %param.9) | copy-start | bytes 49156
  3.2 27.4 %all-to-all-start = ((f32[32,15,2,128]{3,2,1,0:T(2,128)}), f32[32,15,2,128]{3,2,1,0:T(2,128)S(1)}, u32[]{:S(2)}, u32[]{:S(2)}) async-start(f32[32,15,2,128]{3,2,1,0:T(2,128)} %get-tuple-element.18), calls=%async_computation | async-start | bytes 983040 | tf_op jit(solution)/shard_map/all_to_all | solution.py:762
  14.6 5.1 %copy-start.1 = (f32[1,19,4096]{2,0,1:T(1,128)S(1)}, f32[1,19,4096]{2,0,1:T(1,128)}, u32[]{:S(2)}) copy-start(f32[1,19,4096]{2,0,1:T(1,128)} %param.8) | copy-start | bytes 933892
  14.7 5.8 %collective-permute-start.1 = (f32[1,16,128]{2,1,0:T(8,128)S(1)}, f32[1,16,128]{2,1,0:T(8,128)S(1)}, u32[]{:S(2)}, u32[]{:S(2)}) collective-permute-start(f32[1,16,128]{2,1,0:T(8,128)S(1)} %get-tuple-element.38), channel_id=1, source_target_pairs={{32,0},{64,32},{96,64},{128,96},{160,128},{192,160},{224,192},{33,... | collective-permute-start | bytes 24584 | tf_op jit(solution)/shard_map/ppermute | solution.py:786
  16.7 5.0 %collective-permute-start = (f32[1,16,128]{2,1,0:T(8,128)S(1)}, f32[1,16,128]{2,1,0:T(8,128)S(1)}, u32[]{:S(2)}, u32[]{:S(2)}) collective-permute-start(f32[1,16,128]{2,1,0:T(8,128)S(1)} %get-tuple-element.39), channel_id=1, source_target_pairs={{0,32},{32,64},{64,96},{96,128},{128,160},{160,192},{192,224},{1,3... | collective-permute-start | bytes 24584 | tf_op jit(solution)/shard_map/ppermute | solution.py:785
  19.4 0.7 %copy-start.3 = (s32[1,4096]{1,0:T(1,128)S(1)}, s32[1,4096]{1,0:T(1,128)}, u32[]{:S(2)}) copy-start(s32[1,4096]{1,0:T(1,128)} %param.10) | copy-start | bytes 49156

commit v8 on v7

--- a/solution.py
+++ b/solution.py
@@ -530,12 +530,16 @@
     beside.wait()
 
 
-def prepare_kernel(state, depth, post, start, weights, *, omega):
+def prepare_kernel(state, depth, post, start, weights, *old, omega):
     f = [load_cells(state, q) for q in range(19)]
     for q in range(19):
         start[q] = f[q]
     for q, value in enumerate(collide(f, omega)):
         post[q] = value
+    if old:
+        density, u = moments(f)
+        for i, value in enumerate([density] + u):
+            old[0][i] = value
     halves = [depth[pl.ds(half, 16, stride=2), :] for half in range(2)]
     for q, value in enumerate(wall_weights(jnp.concatenate(halves, axis=1))):
         weights[q] = value
@@ -597,7 +601,7 @@
 
 def middle_kernel(
     received, from_low, from_high, c_post, c_start, c_weights, f_post, f_start, f_weights,
-    table, out, coarse_new, state, post, octs,
+    old, table, out, coarse_new, state, post, octs,
 ):
     me = lax.axis_index("dev")
     codes = Codes(table)
@@ -619,9 +623,8 @@
     )
     for q in range(19):
         coarse_new[q] = new[q]
-    old_density, old_u = moments([c_start[q] for q in range(19)])
     density, u = moments(new)
-    mid = [0.5 * (old_density + density)] + [0.5 * (a + b) for a, b in zip(old_u, u)]
+    mid = [0.5 * (old[i] + value) for i, value in enumerate([density] + u)]
     for o, pair in pack_octants(mid).items():
         shared, rows = pack_thin_shell(pair)
         octs[o, 0] = shared[0:4]
@@ -667,7 +670,7 @@
     ghosts = fine_ghosts(codes, lambda d: (rows_of(d, 0), rows_of(d, 2)), 0, under)
     new = stream(lambda q: f_post[q], lambda q: f_start[q], lambda q: f_weights[q], ghosts)
     for q in range(19):
-        state[q] = new[q]
+        store_cells(state, q, new[q])
     first, second = restrict(new)
     out[parent, 0:8, :] = first
     out[parent, 8:16, :] = second
@@ -683,12 +686,10 @@
     return join(tiles) >= 0
 
 
-def final_kernel(received, state, coarse_new, table, fine_out, coarse_out, f_cells, c_cells, sems):
+def final_kernel(received, state, coarse_new, table, fine_out, coarse_out, cells, sems):
+    fine_copy = pltpu.make_async_copy(state, fine_out, sems.at[0])
+    fine_copy.start()
     codes = Codes(table)
-    for q in range(19):
-        store_cells(f_cells, q, state[q])
-    fine_copy = pltpu.make_async_copy(f_cells, fine_out, sems.at[0])
-    fine_copy.start()
     low = (iota((8, 128), 1) & 15) < 8
     tiles = [[[None, None], [None, None]] for _ in range(4)]
     for ox in range(2):
@@ -710,8 +711,8 @@
     own_density, own_u = moments(new)
     own_eq = equilibrium(own_density, own_u, range(19))
     for q in range(19):
-        store_cells(c_cells, q, new[q] + jnp.where(covered, fine_eq[q] - own_eq[q], 0.0))
-    coarse_copy = pltpu.make_async_copy(c_cells, coarse_out, sems.at[1])
+        store_cells(cells, q, new[q] + jnp.where(covered, fine_eq[q] - own_eq[q], 0.0))
+    coarse_copy = pltpu.make_async_copy(cells, coarse_out, sems.at[1])
     coarse_copy.start()
     fine_copy.wait()
     coarse_copy.wait()
@@ -736,11 +737,7 @@
     OCTS,
     pltpu.SemaphoreType.DMA((10,)),
 ]
-FINAL_SCRATCH = [
-    pltpu.VMEM(CELL_ROWS, F32),
-    pltpu.VMEM(CELL_ROWS, F32),
-    pltpu.SemaphoreType.DMA((2,)),
-]
+FINAL_SCRATCH = [pltpu.VMEM(CELL_ROWS, F32), pltpu.SemaphoreType.DMA((2,))]
 
 
 def call(kernel, outs, ins, hbm=(), hbm_outs=(), scratch=(), vmem=SOME_VMEM, name=None):
@@ -785,13 +782,15 @@
     from_low = lax.ppermute(region[1:2], "group", up)
     from_high = lax.ppermute(region[0:1], "group", down)
 
-    def prepare(state, depth, omega, name):
+    def prepare(state, depth, omega, name, more=()):
         def kernel(*refs):
             prepare_kernel(*refs, omega=omega)
 
-        return call(kernel, [FIELD, FIELD, FIELD], [state, depth], name=name)
-
-    c_post, c_start, c_weights = prepare(coarse_state, coarse_depth, OMEGA_COARSE, "prepare_coarse")
+        return call(kernel, [FIELD, FIELD, FIELD, *more], [state, depth], name=name)
+
+    c_post, c_start, c_weights, old = prepare(
+        coarse_state, coarse_depth, OMEGA_COARSE, "prepare_coarse", [(4, 16, 256)]
+    )
     f_post, f_start, f_weights = prepare(fine_state, fine_depth, OMEGA_FINE, "prepare_fine")
     codes = pl.pallas_call(
         codes_kernel,
@@ -806,7 +805,7 @@
         [SLOT2, FIELD, FIELD, FIELD],
         [
             received, from_low, from_high, c_post, c_start, c_weights, f_post, f_start, f_weights,
-            codes,
+            old, codes,
         ],
         scratch=[pltpu.VMEM((8, 3, 4, 128), F32)],
         name="middle",
@@ -814,7 +813,7 @@
     received = swap(sent)
     sent, state = call(
         last_kernel,
-        [(32, SLOT3, 128), FIELD],
+        [(32, SLOT3, 128), CELL_ROWS],
         [received, post, state, f_weights, codes],
         name="last",
     )

time: 68.5 us -> 68.4 us (level)
  no operation moved by 1% of the time
where the time goes in v8:
time: 68.4 us; the launch traced here: 68 us
  blocking collectives  34.6 us (51%)
  starting transfers between devices  15.9 us (23%)
  waiting for transfers between devices  10.1 us (15%)
  Pallas kernels  6.23 us (9%)
  between operations  0.84 us (1%)
    all_to_all x2, blocking collectives, swap(): return lax.all_to_all(value, 'dev', split_axis=0, concat_axis=0, tiled=True)  34.6 us
    all_to_all x1, starting transfers between devices, swap(): return lax.all_to_all(value, 'dev', split_axis=0, concat_axis=0, tiled=True)  11.5 us
    all_to_all x1, waiting for transfers between devices, swap(): return lax.all_to_all(value, 'dev', split_axis=0, concat_axis=0, tiled=True)  8.85 us
    pallas_call x6, Pallas kernels, call(): pl.pallas_call(kernel, out_shape=[jax.ShapeDtypeStruct(s, F32) for s in o...  6.06 us
    ppermute x1, starting transfers between devices, body(): from_low = lax.ppermute(region[1:2], 'group', up)  2.41 us
    ppermute x1, starting transfers between devices, body(): from_high = lax.ppermute(region[0:1], 'group', down)  2.05 us
  transfers between devices with their start and end apart: 3, of which 2 were waited for; matrix products, arithmetic and copies ran while one was open for 0% of the time, Pallas kernels for 1%

profile of v8, /device:TPU:16, one launch (start us, length us, event | category | flops | bytes accessed | tf_op | source)
XLA Modules:
  0.0 68.0 jit_solution(1009456826384793736)
XLA Ops:
  0.6 2.4 %send.1 = (f32[32,15,2,128]{3,2,1,0:T(2,128)}, f32[2,16,128]{2,1,0:T(8,128)}) custom-call(f32[19,32,128]{2,1,0:T(8,128)} %bitcast.13, f32[19,32,128]{2,1,0:T(8,128)} %bitcast.11, s32[6,1,32]{2,1,0:T(1,128)} %bitcast.17, s32[6,1,32]{2,1,0:T(1,128)} %bitcast.19, s32[2,1,32]{2,1,0:T(1,128)} %bitcast.21), custom_call_target="tpu_custom_call" | custom-call | flops 2000000 | bytes 2000000 | tf_op jit(solution)/shard_map/send/pallas_call | solution.py:744
  3.1 0.0 copy-start.7
  3.1 0.0 copy-start.4
  3.1 0.0 copy-start.5
  3.1 0.0 copy-start.6
  3.1 0.0 copy-start
  3.1 0.0 copy-start.2
  3.2 11.5 %all-to-all-start = ((f32[32,15,2,128]{3,2,1,0:T(2,128)}), f32[32,15,2,128]{3,2,1,0:T(2,128)S(1)}, u32[]{:S(2)}, u32[]{:S(2)}) async-start(f32[32,15,2,128]{3,2,1,0:T(2,128)} %get-tuple-element.19), calls=%async_computation | async-start | bytes 983040 | tf_op jit(solution)/shard_map/all_to_all | solution.py:759
  14.6 0.0 copy-start.1
  14.6 0.0 copy-done.7
  14.7 2.1 %collective-permute-start.1 = (f32[1,16,128]{2,1,0:T(8,128)S(1)}, f32[1,16,128]{2,1,0:T(8,128)S(1)}, u32[]{:S(2)}, u32[]{:S(2)}) collective-permute-start(f32[1,16,128]{2,1,0:T(8,128)S(1)} %get-tuple-element.40), channel_id=1, source_target_pairs={{32,0},{64,32},{96,64},{128,96},{160,128},{192,160},{224,192},{33,... | collective-permute-start | bytes 24584 | tf_op jit(solution)/shard_map/ppermute | solution.py:783
  16.7 2.4 %collective-permute-start = (f32[1,16,128]{2,1,0:T(8,128)S(1)}, f32[1,16,128]{2,1,0:T(8,128)S(1)}, u32[]{:S(2)}, u32[]{:S(2)}) collective-permute-start(f32[1,16,128]{2,1,0:T(8,128)S(1)} %get-tuple-element.41), channel_id=1, source_target_pairs={{0,32},{32,64},{64,96},{96,128},{128,160},{160,192},{192,224},{1,3... | collective-permute-start | bytes 24584 | tf_op jit(solution)/shard_map/ppermute | solution.py:782
  19.1 0.0 copy-done.4
  19.1 0.0 copy-done.5
  19.2 0.0 copy-done.6
  19.2 0.2 codes.1.table
  19.3 0.0 copy-done
  19.4 0.0 copy-done.2
  19.4 0.0 copy-start.3
  19.4 0.4 prepare_fine.1
  19.8 0.0 copy-done.1
  19.8 0.3 copy-done.3
  20.1 0.4 prepare_coarse.1
  20.5 0.0 collective-permute-done.1.from_high
  20.5 1.2 %collective-permute-done.from_low = f32[1,16,128]{2,1,0:T(8,128)S(1)} collective-permute-done((f32[1,16,128]{2,1,0:T(8,128)S(1)}, f32[1,16,128]{2,1,0:T(8,128)S(1)}, u32[]{:S(2)}, u32[]{:S(2)}) %collective-permute-start) | collective-permute-done | bytes 8224 | tf_op jit(solution)/shard_map/ppermute | solution.py:782
  21.7 8.8 %all-to-all-done.received = f32[32,15,2,128]{3,2,1,0:T(2,128)S(1)} async-done(((f32[32,15,2,128]{3,2,1,0:T(2,128)}), f32[32,15,2,128]{3,2,1,0:T(2,128)S(1)}, u32[]{:S(2)}, u32[]{:S(2)}) %all-to-all-start) | async-done | bytes 491552 | tf_op jit(solution)/shard_map/all_to_all | solution.py:759
  30.5 1.2 %middle.1 = (f32[32,5,4,128]{3,2,1,0:T(4,128)S(1)}, f32[19,16,256]{2,1,0:T(8,128)S(1)}, f32[19,16,256]{2,1,0:T(8,128)S(1)}, f32[19,16,256]{2,1,0:T(8,128)S(1)}) custom-call(f32[32,15,2,128]{3,2,1,0:T(2,128)S(1)} %all-to-all-done.received, f32[1,16,128]{2,1,0:T(8,128)S(1)} %collective-permute-done.from_low, ...), custom_call_target="tpu_custom_call" | custom-call | flops 2000000 | bytes 2000000 | tf_op jit(solution)/shard_map/middle/pallas_call | solution.py:744
  31.7 18.7 %all_to_all.15.received = f32[32,5,4,128]{3,2,1,0:T(4,128)S(1)} all-to-all(f32[32,5,4,128]{3,2,1,0:T(4,128)S(1)} %get-tuple-element.28), channel_id=1, replica_groups=mesh['group'=8,'dev'=32] {'dev'}, dimensions={0} | all-to-all | bytes 655360 | tf_op jit(solution)/shard_map/all_to_all | solution.py:759
  50.4 0.6 last.1
  51.1 15.9 %all_to_all.16.received = f32[32,16,128]{2,1,0:T(8,128)S(1)} all-to-all(f32[32,16,128]{2,1,0:T(8,128)S(1)} %get-tuple-element.31), channel_id=1, replica_groups=mesh['group'=8,'dev'=32] {'dev'}, dimensions={0} | all-to-all | bytes 524288 | tf_op jit(solution)/shard_map/all_to_all | solution.py:759
  67.0 1.1 %final.1 = (f32[19,32,128]{2,1,0:T(8,128)}, f32[19,32,128]{2,1,0:T(8,128)}) custom-call(f32[32,16,128]{2,1,0:T(8,128)S(1)} %all_to_all.16.received, f32[19,32,128]{2,1,0:T(8,128)S(1)} %get-tuple-element.32.state, f32[19,16,256]{2,1,0:T(8,128)S(1)} %get-tuple-element.33.coarse_new, s32[8,128]{1,0:T(8,128)S(1)} %codes.1.table), custom_call_target="tpu_custom_call" | custom-call | flops 2000000 | bytes 2000000 | tf_op jit(solution)/shard_map/final/pallas_call | solution.py:744
  (1 shorter events, 0.0 us)
Async XLA Ops:
  3.1 11.6 %copy-start.7 = (f32[2,16,128]{2,1,0:T(8,128)S(1)}, f32[2,16,128]{2,1,0:T(8,128)}, u32[]{:S(2)}) copy-start(f32[2,16,128]{2,1,0:T(8,128)} %get-tuple-element.20) | copy-start | bytes 49156
  3.1 16.0 %copy-start.4 = (s32[1,32,6]{1,0,2:T(1,128)S(1)}, s32[1,32,6]{1,0,2:T(1,128)}, u32[]{:S(2)}) copy-start(s32[1,32,6]{1,0,2:T(1,128)} %param.12) | copy-start | bytes 2308
  3.1 16.0 %copy-start.5 = (s32[1,32,6]{1,0,2:T(1,128)S(1)}, s32[1,32,6]{1,0,2:T(1,128)}, u32[]{:S(2)}) copy-start(s32[1,32,6]{1,0,2:T(1,128)} %param.11) | copy-start | bytes 2308
  3.1 16.0 %copy-start.6 = (s32[1,32,2]{1,2,0:T(2,128)S(1)}, s32[1,32,2]{1,2,0:T(2,128)}, u32[]{:S(2)}) copy-start(s32[1,32,2]{1,2,0:T(2,128)} %param.13) | copy-start | bytes 772
  3.1 16.2 %copy-start = (f32[1,19,4096]{2,0,1:T(1,128)S(1)}, f32[1,19,4096]{2,0,1:T(1,128)}, u32[]{:S(2)}) copy-start(f32[1,19,4096]{2,0,1:T(1,128)} %param.7) | copy-start | bytes 933892
  3.1 16.2 %copy-start.2 = (s32[1,4096]{1,0:T(1,128)S(1)}, s32[1,4096]{1,0:T(1,128)}, u32[]{:S(2)}) copy-start(s32[1,4096]{1,0:T(1,128)} %param.9) | copy-start | bytes 49156
  3.2 27.4 %all-to-all-start = ((f32[32,15,2,128]{3,2,1,0:T(2,128)}), f32[32,15,2,128]{3,2,1,0:T(2,128)S(1)}, u32[]{:S(2)}, u32[]{:S(2)}) async-start(f32[32,15,2,128]{3,2,1,0:T(2,128)} %get-tuple-element.19), calls=%async_computation | async-start | bytes 983040 | tf_op jit(solution)/shard_map/all_to_all | solution.py:759
  14.6 5.1 %copy-start.1 = (f32[1,19,4096]{2,0,1:T(1,128)S(1)}, f32[1,19,4096]{2,0,1:T(1,128)}, u32[]{:S(2)}) copy-start(f32[1,19,4096]{2,0,1:T(1,128)} %param.8) | copy-start | bytes 933892
  14.7 5.8 %collective-permute-start.1 = (f32[1,16,128]{2,1,0:T(8,128)S(1)}, f32[1,16,128]{2,1,0:T(8,128)S(1)}, u32[]{:S(2)}, u32[]{:S(2)}) collective-permute-start(f32[1,16,128]{2,1,0:T(8,128)S(1)} %get-tuple-element.40), channel_id=1, source_target_pairs={{32,0},{64,32},{96,64},{128,96},{160,128},{192,160},{224,192},{33,... | collective-permute-start | bytes 24584 | tf_op jit(solution)/shard_map/ppermute | solution.py:783
  16.7 5.0 %collective-permute-start = (f32[1,16,128]{2,1,0:T(8,128)S(1)}, f32[1,16,128]{2,1,0:T(8,128)S(1)}, u32[]{:S(2)}, u32[]{:S(2)}) collective-permute-start(f32[1,16,128]{2,1,0:T(8,128)S(1)} %get-tuple-element.41), channel_id=1, source_target_pairs={{0,32},{32,64},{64,96},{96,128},{128,160},{160,192},{192,224},{1,3... | collective-permute-start | bytes 24584 | tf_op jit(solution)/shard_map/ppermute | solution.py:782
  19.4 0.7 %copy-start.3 = (s32[1,4096]{1,0:T(1,128)S(1)}, s32[1,4096]{1,0:T(1,128)}, u32[]{:S(2)}) copy-start(s32[1,4096]{1,0:T(1,128)} %param.10) | copy-start | bytes 49156

commit v9 on v8

--- a/solution.py
+++ b/solution.py
@@ -497,7 +497,7 @@
         copy.start()
 
     def put(part):
-        rows = pl.ds(4 * part, 4 if part < 3 else 3)
+        rows = (pl.ds(0, 4), pl.ds(4, 8), pl.ds(12, 3))[part]
         return pltpu.make_async_copy(slots.at[:, rows], out.at[:, rows], sems.at[5 + part])
 
     me = lax.axis_index("dev")
@@ -513,19 +513,18 @@
             region[face - 2, 0:8, :] = first
             region[face - 2, 8:16, :] = second
     put(0).start()
-    beside = pltpu.make_async_copy(region, region_out, sems.at[9])
+    beside = pltpu.make_async_copy(region, region_out, sems.at[8])
     beside.start()
     fetch[4].wait()
     give_octants(octs, parents, slots)
-    put(3).start()
+    put(2).start()
     fetch[2].wait()
     fetch[3].wait()
     post = collide([load_cells(fine, q) for q in range(19)], OMEGA_FINE)
     for face in range(6):
         give_face(post, face, fine_links[face, 0, me], me, slots, 4, 32)
     put(1).start()
-    put(2).start()
-    for part in range(4):
+    for part in range(3):
         put(part).wait()
     beside.wait()
 
@@ -735,7 +734,7 @@
     pltpu.VMEM(SLOT1, F32),
     pltpu.VMEM((2, 16, 128), F32),
     OCTS,
-    pltpu.SemaphoreType.DMA((10,)),
+    pltpu.SemaphoreType.DMA((9,)),
 ]
 FINAL_SCRATCH = [pltpu.VMEM(CELL_ROWS, F32), pltpu.SemaphoreType.DMA((2,))]
 

time: 68.4 us -> 68.5 us (level)
  no operation moved by 1% of the time
where the time goes in v9:
time: 68.5 us; the launch traced here: 68.1 us
  blocking collectives  34.6 us (51%)
  starting transfers between devices  15.9 us (23%)
  waiting for transfers between devices  10.1 us (15%)
  Pallas kernels  6.27 us (9%)
  between operations  0.84 us (1%)
    all_to_all x2, blocking collectives, swap(): return lax.all_to_all(value, 'dev', split_axis=0, concat_axis=0, tiled=True)  34.6 us
    all_to_all x1, starting transfers between devices, swap(): return lax.all_to_all(value, 'dev', split_axis=0, concat_axis=0, tiled=True)  11.5 us
    all_to_all x1, waiting for transfers between devices, swap(): return lax.all_to_all(value, 'dev', split_axis=0, concat_axis=0, tiled=True)  8.85 us
    pallas_call x6, Pallas kernels, call(): pl.pallas_call(kernel, out_shape=[jax.ShapeDtypeStruct(s, F32) for s in o...  6.1 us
    ppermute x1, starting transfers between devices, body(): from_low = lax.ppermute(region[1:2], 'group', up)  2.41 us
    ppermute x1, starting transfers between devices, body(): from_high = lax.ppermute(region[0:1], 'group', down)  2.05 us
  transfers between devices with their start and end apart: 3, of which 2 were waited for; matrix products, arithmetic and copies ran while one was open for 0% of the time, Pallas kernels for 1%

profile of v9, /device:TPU:16, one launch (start us, length us, event | category | flops | bytes accessed | tf_op | source)
XLA Modules:
  0.0 68.1 jit_solution(9706933193134414837)
XLA Ops:
  0.6 2.5 %send.1 = (f32[32,15,2,128]{3,2,1,0:T(2,128)}, f32[2,16,128]{2,1,0:T(8,128)}) custom-call(f32[19,32,128]{2,1,0:T(8,128)} %bitcast.13, f32[19,32,128]{2,1,0:T(8,128)} %bitcast.11, s32[6,1,32]{2,1,0:T(1,128)} %bitcast.17, s32[6,1,32]{2,1,0:T(1,128)} %bitcast.19, s32[2,1,32]{2,1,0:T(1,128)} %bitcast.21), custom_call_target="tpu_custom_call" | custom-call | flops 2000000 | bytes 2000000 | tf_op jit(solution)/shard_map/send/pallas_call | solution.py:743
  3.1 0.0 copy-start.7
  3.1 0.0 copy-start.4
  3.1 0.0 copy-start.5
  3.2 0.0 copy-start.6
  3.2 0.0 copy-start
  3.2 0.0 copy-start.2
  3.2 11.5 %all-to-all-start = ((f32[32,15,2,128]{3,2,1,0:T(2,128)}), f32[32,15,2,128]{3,2,1,0:T(2,128)S(1)}, u32[]{:S(2)}, u32[]{:S(2)}) async-start(f32[32,15,2,128]{3,2,1,0:T(2,128)} %get-tuple-element.19), calls=%async_computation | async-start | bytes 983040 | tf_op jit(solution)/shard_map/all_to_all | solution.py:758
  14.7 0.0 copy-start.1
  14.7 0.0 copy-done.7
  14.7 2.1 %collective-permute-start.1 = (f32[1,16,128]{2,1,0:T(8,128)S(1)}, f32[1,16,128]{2,1,0:T(8,128)S(1)}, u32[]{:S(2)}, u32[]{:S(2)}) collective-permute-start(f32[1,16,128]{2,1,0:T(8,128)S(1)} %get-tuple-element.40), channel_id=1, source_target_pairs={{32,0},{64,32},{96,64},{128,96},{160,128},{192,160},{224,192},{33,... | collective-permute-start | bytes 24584 | tf_op jit(solution)/shard_map/ppermute | solution.py:782
  16.8 2.4 %collective-permute-start = (f32[1,16,128]{2,1,0:T(8,128)S(1)}, f32[1,16,128]{2,1,0:T(8,128)S(1)}, u32[]{:S(2)}, u32[]{:S(2)}) collective-permute-start(f32[1,16,128]{2,1,0:T(8,128)S(1)} %get-tuple-element.41), channel_id=1, source_target_pairs={{0,32},{32,64},{64,96},{96,128},{128,160},{160,192},{192,224},{1,3... | collective-permute-start | bytes 24584 | tf_op jit(solution)/shard_map/ppermute | solution.py:781
  19.2 0.0 copy-done.4
  19.2 0.0 copy-done.5
  19.2 0.0 copy-done.6
  19.2 0.2 codes.1.table
  19.4 0.0 copy-done
  19.4 0.0 copy-done.2
  19.4 0.0 copy-start.3
  19.4 0.4 prepare_fine.1
  19.8 0.0 copy-done.1
  19.8 0.3 copy-done.3
  20.1 0.4 prepare_coarse.1
  20.5 0.0 collective-permute-done.1.from_high
  20.5 1.2 %collective-permute-done.from_low = f32[1,16,128]{2,1,0:T(8,128)S(1)} collective-permute-done((f32[1,16,128]{2,1,0:T(8,128)S(1)}, f32[1,16,128]{2,1,0:T(8,128)S(1)}, u32[]{:S(2)}, u32[]{:S(2)}) %collective-permute-start) | collective-permute-done | bytes 8224 | tf_op jit(solution)/shard_map/ppermute | solution.py:781
  21.7 8.8 %all-to-all-done.received = f32[32,15,2,128]{3,2,1,0:T(2,128)S(1)} async-done(((f32[32,15,2,128]{3,2,1,0:T(2,128)}), f32[32,15,2,128]{3,2,1,0:T(2,128)S(1)}, u32[]{:S(2)}, u32[]{:S(2)}) %all-to-all-start) | async-done | bytes 491552 | tf_op jit(solution)/shard_map/all_to_all | solution.py:758
  30.6 1.2 %middle.1 = (f32[32,5,4,128]{3,2,1,0:T(4,128)S(1)}, f32[19,16,256]{2,1,0:T(8,128)S(1)}, f32[19,16,256]{2,1,0:T(8,128)S(1)}, f32[19,16,256]{2,1,0:T(8,128)S(1)}) custom-call(f32[32,15,2,128]{3,2,1,0:T(2,128)S(1)} %all-to-all-done.received, f32[1,16,128]{2,1,0:T(8,128)S(1)} %collective-permute-done.from_low, ...), custom_call_target="tpu_custom_call" | custom-call | flops 2000000 | bytes 2000000 | tf_op jit(solution)/shard_map/middle/pallas_call | solution.py:743
  31.7 18.7 %all_to_all.15.received = f32[32,5,4,128]{3,2,1,0:T(4,128)S(1)} all-to-all(f32[32,5,4,128]{3,2,1,0:T(4,128)S(1)} %get-tuple-element.28), channel_id=1, replica_groups=mesh['group'=8,'dev'=32] {'dev'}, dimensions={0} | all-to-all | bytes 655360 | tf_op jit(solution)/shard_map/all_to_all | solution.py:758
  50.5 0.6 last.1
  51.1 15.9 %all_to_all.16.received = f32[32,16,128]{2,1,0:T(8,128)S(1)} all-to-all(f32[32,16,128]{2,1,0:T(8,128)S(1)} %get-tuple-element.31), channel_id=1, replica_groups=mesh['group'=8,'dev'=32] {'dev'}, dimensions={0} | all-to-all | bytes 524288 | tf_op jit(solution)/shard_map/all_to_all | solution.py:758
  67.0 1.1 %final.1 = (f32[19,32,128]{2,1,0:T(8,128)}, f32[19,32,128]{2,1,0:T(8,128)}) custom-call(f32[32,16,128]{2,1,0:T(8,128)S(1)} %all_to_all.16.received, f32[19,32,128]{2,1,0:T(8,128)S(1)} %get-tuple-element.32.state, f32[19,16,256]{2,1,0:T(8,128)S(1)} %get-tuple-element.33.coarse_new, s32[8,128]{1,0:T(8,128)S(1)} %codes.1.table), custom_call_target="tpu_custom_call" | custom-call | flops 2000000 | bytes 2000000 | tf_op jit(solution)/shard_map/final/pallas_call | solution.py:743
  (1 shorter events, 0.0 us)
Async XLA Ops:
  3.1 11.6 %copy-start.7 = (f32[2,16,128]{2,1,0:T(8,128)S(1)}, f32[2,16,128]{2,1,0:T(8,128)}, u32[]{:S(2)}) copy-start(f32[2,16,128]{2,1,0:T(8,128)} %get-tuple-element.20) | copy-start | bytes 49156
  3.1 16.0 %copy-start.4 = (s32[1,32,6]{1,0,2:T(1,128)S(1)}, s32[1,32,6]{1,0,2:T(1,128)}, u32[]{:S(2)}) copy-start(s32[1,32,6]{1,0,2:T(1,128)} %param.12) | copy-start | bytes 2308
  3.1 16.0 %copy-start.5 = (s32[1,32,6]{1,0,2:T(1,128)S(1)}, s32[1,32,6]{1,0,2:T(1,128)}, u32[]{:S(2)}) copy-start(s32[1,32,6]{1,0,2:T(1,128)} %param.11) | copy-start | bytes 2308
  3.2 16.0 %copy-start.6 = (s32[1,32,2]{1,2,0:T(2,128)S(1)}, s32[1,32,2]{1,2,0:T(2,128)}, u32[]{:S(2)}) copy-start(s32[1,32,2]{1,2,0:T(2,128)} %param.13) | copy-start | bytes 772
  3.2 16.2 %copy-start = (f32[1,19,4096]{2,0,1:T(1,128)S(1)}, f32[1,19,4096]{2,0,1:T(1,128)}, u32[]{:S(2)}) copy-start(f32[1,19,4096]{2,0,1:T(1,128)} %param.7) | copy-start | bytes 933892
  3.2 16.2 %copy-start.2 = (s32[1,4096]{1,0:T(1,128)S(1)}, s32[1,4096]{1,0:T(1,128)}, u32[]{:S(2)}) copy-start(s32[1,4096]{1,0:T(1,128)} %param.9) | copy-start | bytes 49156
  3.2 27.4 %all-to-all-start = ((f32[32,15,2,128]{3,2,1,0:T(2,128)}), f32[32,15,2,128]{3,2,1,0:T(2,128)S(1)}, u32[]{:S(2)}, u32[]{:S(2)}) async-start(f32[32,15,2,128]{3,2,1,0:T(2,128)} %get-tuple-element.19), calls=%async_computation | async-start | bytes 983040 | tf_op jit(solution)/shard_map/all_to_all | solution.py:758
  14.7 5.1 %copy-start.1 = (f32[1,19,4096]{2,0,1:T(1,128)S(1)}, f32[1,19,4096]{2,0,1:T(1,128)}, u32[]{:S(2)}) copy-start(f32[1,19,4096]{2,0,1:T(1,128)} %param.8) | copy-start | bytes 933892
  14.7 5.8 %collective-permute-start.1 = (f32[1,16,128]{2,1,0:T(8,128)S(1)}, f32[1,16,128]{2,1,0:T(8,128)S(1)}, u32[]{:S(2)}, u32[]{:S(2)}) collective-permute-start(f32[1,16,128]{2,1,0:T(8,128)S(1)} %get-tuple-element.40), channel_id=1, source_target_pairs={{32,0},{64,32},{96,64},{128,96},{160,128},{192,160},{224,192},{33,... | collective-permute-start | bytes 24584 | tf_op jit(solution)/shard_map/ppermute | solution.py:782
  16.8 5.0 %collective-permute-start = (f32[1,16,128]{2,1,0:T(8,128)S(1)}, f32[1,16,128]{2,1,0:T(8,128)S(1)}, u32[]{:S(2)}, u32[]{:S(2)}) collective-permute-start(f32[1,16,128]{2,1,0:T(8,128)S(1)} %get-tuple-element.41), channel_id=1, source_target_pairs={{0,32},{32,64},{64,96},{96,128},{128,160},{160,192},{192,224},{1,3... | collective-permute-start | bytes 24584 | tf_op jit(solution)/shard_map/ppermute | solution.py:781
  19.4 0.7 %copy-start.3 = (s32[1,4096]{1,0:T(1,128)S(1)}, s32[1,4096]{1,0:T(1,128)}, u32[]{:S(2)}) copy-start(s32[1,4096]{1,0:T(1,128)} %param.10) | copy-start | bytes 49156

commit v10 on v8

--- a/solution.py
+++ b/solution.py
@@ -401,8 +401,17 @@
         fields[2].append(join(tiles))
     out = []
     for axis in range(3):
-        chosen = [q for q in range(19) if VELOCITIES[q][axis] != 0]
-        out.append(equilibrium(fields[axis][0], fields[axis][1:], chosen))
+        ghosts = {}
+        for sign in (1, -1):
+            chosen = [q for q in range(19) if VELOCITIES[q][axis] == sign]
+            part = fields[axis]
+            if axis < 2:
+                size, at = (8, 128)[axis], (8, 128)[axis] if sign > 0 else 0
+                part = [lax.slice_in_dim(f, at, at + size, axis=axis) for f in part]
+            rest = equilibrium(part[0], part[1:], chosen)
+            for q in chosen:
+                ghosts[q] = jnp.concatenate([rest[q]] * 2, axis=axis) if axis < 2 else rest[q]
+        out.append(ghosts)
     return out
 
 

time: 68.4 us -> 68.4 us (level)
  no operation moved by 1% of the time
where the time goes in v10:
time: 68.4 us; the launch traced here: 68 us
  blocking collectives  34.6 us (51%)
  starting transfers between devices  15.9 us (23%)
  waiting for transfers between devices  10.1 us (15%)
  Pallas kernels  6.23 us (9%)
  between operations  0.84 us (1%)
    all_to_all x2, blocking collectives, swap(): return lax.all_to_all(value, 'dev', split_axis=0, concat_axis=0, tiled=True)  34.6 us
    all_to_all x1, starting transfers between devices, swap(): return lax.all_to_all(value, 'dev', split_axis=0, concat_axis=0, tiled=True)  11.5 us
    all_to_all x1, waiting for transfers between devices, swap(): return lax.all_to_all(value, 'dev', split_axis=0, concat_axis=0, tiled=True)  8.85 us
    pallas_call x6, Pallas kernels, call(): pl.pallas_call(kernel, out_shape=[jax.ShapeDtypeStruct(s, F32) for s in o...  6.05 us
    ppermute x1, starting transfers between devices, body(): from_low = lax.ppermute(region[1:2], 'group', up)  2.41 us
    ppermute x1, starting transfers between devices, body(): from_high = lax.ppermute(region[0:1], 'group', down)  2.05 us
  transfers between devices with their start and end apart: 3, of which 2 were waited for; matrix products, arithmetic and copies ran while one was open for 0% of the time, Pallas kernels for 1%

profile of v10, /device:TPU:16, one launch (start us, length us, event | category | flops | bytes accessed | tf_op | source)
XLA Modules:
  0.0 68.0 jit_solution(17980356295034280874)
XLA Ops:
  0.6 2.4 %send.1 = (f32[32,15,2,128]{3,2,1,0:T(2,128)}, f32[2,16,128]{2,1,0:T(8,128)}) custom-call(f32[19,32,128]{2,1,0:T(8,128)} %bitcast.13, f32[19,32,128]{2,1,0:T(8,128)} %bitcast.11, s32[6,1,32]{2,1,0:T(1,128)} %bitcast.17, s32[6,1,32]{2,1,0:T(1,128)} %bitcast.19, s32[2,1,32]{2,1,0:T(1,128)} %bitcast.21), custom_call_target="tpu_custom_call" | custom-call | flops 2000000 | bytes 2000000 | tf_op jit(solution)/shard_map/send/pallas_call | solution.py:753
  3.1 0.0 copy-start.7
  3.1 0.0 copy-start.4
  3.1 0.0 copy-start.5
  3.1 0.0 copy-start.6
  3.1 0.0 copy-start
  3.1 0.0 copy-start.2
  3.2 11.5 %all-to-all-start = ((f32[32,15,2,128]{3,2,1,0:T(2,128)}), f32[32,15,2,128]{3,2,1,0:T(2,128)S(1)}, u32[]{:S(2)}, u32[]{:S(2)}) async-start(f32[32,15,2,128]{3,2,1,0:T(2,128)} %get-tuple-element.19), calls=%async_computation | async-start | bytes 983040 | tf_op jit(solution)/shard_map/all_to_all | solution.py:768
  14.6 0.0 copy-start.1
  14.6 0.0 copy-done.7
  14.7 2.1 %collective-permute-start.1 = (f32[1,16,128]{2,1,0:T(8,128)S(1)}, f32[1,16,128]{2,1,0:T(8,128)S(1)}, u32[]{:S(2)}, u32[]{:S(2)}) collective-permute-start(f32[1,16,128]{2,1,0:T(8,128)S(1)} %get-tuple-element.40), channel_id=1, source_target_pairs={{32,0},{64,32},{96,64},{128,96},{160,128},{192,160},{224,192},{33,... | collective-permute-start | bytes 24584 | tf_op jit(solution)/shard_map/ppermute | solution.py:792
  16.7 2.4 %collective-permute-start = (f32[1,16,128]{2,1,0:T(8,128)S(1)}, f32[1,16,128]{2,1,0:T(8,128)S(1)}, u32[]{:S(2)}, u32[]{:S(2)}) collective-permute-start(f32[1,16,128]{2,1,0:T(8,128)S(1)} %get-tuple-element.41), channel_id=1, source_target_pairs={{0,32},{32,64},{64,96},{96,128},{128,160},{160,192},{192,224},{1,3... | collective-permute-start | bytes 24584 | tf_op jit(solution)/shard_map/ppermute | solution.py:791
  19.1 0.0 copy-done.4
  19.1 0.0 copy-done.5
  19.2 0.0 copy-done.6
  19.2 0.2 codes.1.table
  19.3 0.0 copy-done
  19.4 0.0 copy-done.2
  19.4 0.0 copy-start.3
  19.4 0.4 prepare_fine.1
  19.8 0.0 copy-done.1
  19.8 0.3 copy-done.3
  20.1 0.4 prepare_coarse.1
  20.5 0.0 collective-permute-done.1.from_high
  20.5 1.2 %collective-permute-done.from_low = f32[1,16,128]{2,1,0:T(8,128)S(1)} collective-permute-done((f32[1,16,128]{2,1,0:T(8,128)S(1)}, f32[1,16,128]{2,1,0:T(8,128)S(1)}, u32[]{:S(2)}, u32[]{:S(2)}) %collective-permute-start) | collective-permute-done | bytes 8224 | tf_op jit(solution)/shard_map/ppermute | solution.py:791
  21.7 8.8 %all-to-all-done.received = f32[32,15,2,128]{3,2,1,0:T(2,128)S(1)} async-done(((f32[32,15,2,128]{3,2,1,0:T(2,128)}), f32[32,15,2,128]{3,2,1,0:T(2,128)S(1)}, u32[]{:S(2)}, u32[]{:S(2)}) %all-to-all-start) | async-done | bytes 491552 | tf_op jit(solution)/shard_map/all_to_all | solution.py:768
  30.5 1.2 %middle.1 = (f32[32,5,4,128]{3,2,1,0:T(4,128)S(1)}, f32[19,16,256]{2,1,0:T(8,128)S(1)}, f32[19,16,256]{2,1,0:T(8,128)S(1)}, f32[19,16,256]{2,1,0:T(8,128)S(1)}) custom-call(f32[32,15,2,128]{3,2,1,0:T(2,128)S(1)} %all-to-all-done.received, f32[1,16,128]{2,1,0:T(8,128)S(1)} %collective-permute-done.from_low, ...), custom_call_target="tpu_custom_call" | custom-call | flops 2000000 | bytes 2000000 | tf_op jit(solution)/shard_map/middle/pallas_call | solution.py:753
  31.7 18.7 %all_to_all.15.received = f32[32,5,4,128]{3,2,1,0:T(4,128)S(1)} all-to-all(f32[32,5,4,128]{3,2,1,0:T(4,128)S(1)} %get-tuple-element.28), channel_id=1, replica_groups=mesh['group'=8,'dev'=32] {'dev'}, dimensions={0} | all-to-all | bytes 655360 | tf_op jit(solution)/shard_map/all_to_all | solution.py:768
  50.4 0.6 last.1
  51.1 15.9 %all_to_all.16.received = f32[32,16,128]{2,1,0:T(8,128)S(1)} all-to-all(f32[32,16,128]{2,1,0:T(8,128)S(1)} %get-tuple-element.31), channel_id=1, replica_groups=mesh['group'=8,'dev'=32] {'dev'}, dimensions={0} | all-to-all | bytes 524288 | tf_op jit(solution)/shard_map/all_to_all | solution.py:768
  67.0 1.1 %final.1 = (f32[19,32,128]{2,1,0:T(8,128)}, f32[19,32,128]{2,1,0:T(8,128)}) custom-call(f32[32,16,128]{2,1,0:T(8,128)S(1)} %all_to_all.16.received, f32[19,32,128]{2,1,0:T(8,128)S(1)} %get-tuple-element.32.state, f32[19,16,256]{2,1,0:T(8,128)S(1)} %get-tuple-element.33.coarse_new, s32[8,128]{1,0:T(8,128)S(1)} %codes.1.table), custom_call_target="tpu_custom_call" | custom-call | flops 2000000 | bytes 2000000 | tf_op jit(solution)/shard_map/final/pallas_call | solution.py:753
  (1 shorter events, 0.0 us)
Async XLA Ops:
  3.1 11.6 %copy-start.7 = (f32[2,16,128]{2,1,0:T(8,128)S(1)}, f32[2,16,128]{2,1,0:T(8,128)}, u32[]{:S(2)}) copy-start(f32[2,16,128]{2,1,0:T(8,128)} %get-tuple-element.20) | copy-start | bytes 49156
  3.1 16.0 %copy-start.4 = (s32[1,32,6]{1,0,2:T(1,128)S(1)}, s32[1,32,6]{1,0,2:T(1,128)}, u32[]{:S(2)}) copy-start(s32[1,32,6]{1,0,2:T(1,128)} %param.12) | copy-start | bytes 2308
  3.1 16.0 %copy-start.5 = (s32[1,32,6]{1,0,2:T(1,128)S(1)}, s32[1,32,6]{1,0,2:T(1,128)}, u32[]{:S(2)}) copy-start(s32[1,32,6]{1,0,2:T(1,128)} %param.11) | copy-start | bytes 2308
  3.1 16.0 %copy-start.6 = (s32[1,32,2]{1,2,0:T(2,128)S(1)}, s32[1,32,2]{1,2,0:T(2,128)}, u32[]{:S(2)}) copy-start(s32[1,32,2]{1,2,0:T(2,128)} %param.13) | copy-start | bytes 772
  3.1 16.2 %copy-start = (f32[1,19,4096]{2,0,1:T(1,128)S(1)}, f32[1,19,4096]{2,0,1:T(1,128)}, u32[]{:S(2)}) copy-start(f32[1,19,4096]{2,0,1:T(1,128)} %param.7) | copy-start | bytes 933892
  3.1 16.2 %copy-start.2 = (s32[1,4096]{1,0:T(1,128)S(1)}, s32[1,4096]{1,0:T(1,128)}, u32[]{:S(2)}) copy-start(s32[1,4096]{1,0:T(1,128)} %param.9) | copy-start | bytes 49156
  3.2 27.4 %all-to-all-start = ((f32[32,15,2,128]{3,2,1,0:T(2,128)}), f32[32,15,2,128]{3,2,1,0:T(2,128)S(1)}, u32[]{:S(2)}, u32[]{:S(2)}) async-start(f32[32,15,2,128]{3,2,1,0:T(2,128)} %get-tuple-element.19), calls=%async_computation | async-start | bytes 983040 | tf_op jit(solution)/shard_map/all_to_all | solution.py:768
  14.6 5.1 %copy-start.1 = (f32[1,19,4096]{2,0,1:T(1,128)S(1)}, f32[1,19,4096]{2,0,1:T(1,128)}, u32[]{:S(2)}) copy-start(f32[1,19,4096]{2,0,1:T(1,128)} %param.8) | copy-start | bytes 933892
  14.7 5.8 %collective-permute-start.1 = (f32[1,16,128]{2,1,0:T(8,128)S(1)}, f32[1,16,128]{2,1,0:T(8,128)S(1)}, u32[]{:S(2)}, u32[]{:S(2)}) collective-permute-start(f32[1,16,128]{2,1,0:T(8,128)S(1)} %get-tuple-element.40), channel_id=1, source_target_pairs={{32,0},{64,32},{96,64},{128,96},{160,128},{192,160},{224,192},{33,... | collective-permute-start | bytes 24584 | tf_op jit(solution)/shard_map/ppermute | solution.py:792
  16.7 5.0 %collective-permute-start = (f32[1,16,128]{2,1,0:T(8,128)S(1)}, f32[1,16,128]{2,1,0:T(8,128)S(1)}, u32[]{:S(2)}, u32[]{:S(2)}) collective-permute-start(f32[1,16,128]{2,1,0:T(8,128)S(1)} %get-tuple-element.41), channel_id=1, source_target_pairs={{0,32},{32,64},{64,96},{96,128},{128,160},{160,192},{192,224},{1,3... | collective-permute-start | bytes 24584 | tf_op jit(solution)/shard_map/ppermute | solution.py:791
  19.4 0.7 %copy-start.3 = (s32[1,4096]{1,0:T(1,128)S(1)}, s32[1,4096]{1,0:T(1,128)}, u32[]{:S(2)}) copy-start(s32[1,4096]{1,0:T(1,128)} %param.10) | copy-start | bytes 49156
